TPU v7x, 512 devices: a whole 4x4x16 slice. The times are simulated.
512 devices in a mesh: rep: 8 (over x, core), section: 8 (over z_lo), tp: 8 (over y, z_hi).
Axes of the slice: x: 4, y: 4, z: 16 (z_hi: 2, z_lo: 8; z = z_hi * 8 + z_lo), core: 2. Of those that a mesh axis runs over, the one named last changes fastest.
Arguments:
- cotangent: bfloat16 [1024, 6144], P('rep', ('section', 'tp')), may hold values from -6 to 6
- saved_inputs: bfloat16 [1024, 6144], P('rep', ('section', 'tp')), may hold values from -6 to 6
- up_weight: bfloat16 [6144, 24576], P('rep', ('section', 'tp')), may hold values from -0.078125 to 0.078125
- down_weight: bfloat16 [24576, 6144], P(('section', 'tp'), 'rep'), may hold values from -0.0390625 to 0.0390625
- block_owner: int32 [2, 8], replicated, may hold values from 0 to 7, each once within a row
Outputs:
- input_grads: bfloat16 [1024, 6144], P('rep', ('section', 'tp'))
- weight_grads: float32 [2, 8, 768, 24576], P(None, 'rep', None, ('section', 'tp'))
Inputs may be any that keep to these rules, and one draw needn't show every extreme that they name: `block_owner`: each row is a permutation.
All inputs are finite; a program needn't handle non-finite values.
Results may differ from a plain program's by a relative error of at most 0.0034.
Values may be sent and summed in bfloat16 or wider, within the bound.
No kernel may reach another device: no remote copies, remote signals or barrier semaphores. Data moves between devices by JAX's collectives and lax.ppermute only.
A program may use at most 64 MiB of HBM per device.

v0:
```python
import math

import jax
import jax.numpy as jnp
from jax import lax
from jax.sharding import PartitionSpec as P

GELU_SCALE = math.sqrt(2.0 / math.pi)
GELU_CUBIC = 0.044715


def gelu_value(values):
    inner = GELU_SCALE * (values + GELU_CUBIC * values * values * values)
    return 0.5 * values * (1.0 + jnp.tanh(inner))


def gelu_deriv(values):
    tanh_part = jnp.tanh(GELU_SCALE * (values + GELU_CUBIC * values * values * values))
    return 0.5 * (1.0 + tanh_part) + 0.5 * values * (1.0 - tanh_part * tanh_part) * GELU_SCALE * (
        1.0 + 3.0 * GELU_CUBIC * values * values
    )


def contract_rows(left, right):
    return lax.dot_general(
        left, right, (((0,), (0,)), ((), ())), preferred_element_type=jnp.float32
    )


def contract_cols(left, right):
    return lax.dot_general(
        left, right, (((1,), (1,)), ((), ())), preferred_element_type=jnp.float32
    )


def body(cotangent, saved_inputs, up_weight, down_weight, block_owner):
    rep_count = lax.axis_size("rep")
    grad_full, input_full = (
        lax.all_gather(cotangent, ("section", "tp"), axis=1, tiled=True),
        lax.all_gather(saved_inputs, ("section", "tp"), axis=1, tiled=True),
    )
    tokens_here = grad_full.shape[0]
    model_width = grad_full.shape[1]
    columns = grad_full
    back_grad = contract_cols(columns, lax.all_gather(down_weight, "rep", axis=1, tiled=True))
    columns = input_full
    pre_act = jnp.dot(
        columns,
        lax.all_gather(up_weight, "rep", axis=0, tiled=True),
        preferred_element_type=jnp.float32,
    )
    hidden = gelu_value(pre_act).astype(jnp.bfloat16)
    dpre = (back_grad * gelu_deriv(pre_act)).astype(jnp.bfloat16)
    partial_grad = contract_cols(dpre, lax.all_gather(up_weight, "rep", axis=0, tiled=True))
    summed = lax.psum_scatter(partial_grad, ("section", "tp"), scatter_dimension=1, tiled=True)
    input_grads = (cotangent.astype(jnp.float32) + summed).astype(jnp.bfloat16)
    owners = jnp.arange(rep_count, dtype=jnp.int32)
    inverse = jnp.sum(
        jnp.where(block_owner[:, None, :] == owners[None, :, None], owners[None, None, :], 0),
        axis=2,
    )
    block_rows = model_width // rep_count
    send_inputs = jnp.take(
        input_full.reshape(tokens_here, rep_count, block_rows), inverse[0], axis=1
    )
    send_grads = jnp.take(grad_full.reshape(tokens_here, rep_count, block_rows), inverse[1], axis=1)
    got_inputs, got_grads = (
        lax.all_to_all(send_inputs, "rep", split_axis=1, concat_axis=0, tiled=True),
        lax.all_to_all(send_grads, "rep", split_axis=1, concat_axis=0, tiled=True),
    )
    all_dpre, all_hidden = (
        lax.all_gather(dpre, "rep", axis=0, tiled=True),
        lax.all_gather(hidden, "rep", axis=0, tiled=True),
    )
    up_block = contract_rows(got_inputs.reshape(-1, block_rows), all_dpre)
    down_block = contract_rows(got_grads.reshape(-1, block_rows), all_hidden)
    weight_grads = jnp.stack([up_block, down_block])[:, None]
    return (input_grads, weight_grads)


def solution(mesh):
    in_specs = (
        P("rep", ("section", "tp")),
        P("rep", ("section", "tp")),
        P("rep", ("section", "tp")),
        P(("section", "tp"), "rep"),
        P(),
    )
    out_specs = (P("rep", ("section", "tp")), P(None, "rep", None, ("section", "tp")))
    return jax.shard_map(body, mesh=mesh, in_specs=in_specs, out_specs=out_specs, check_vma=False)
```

profile of v0, /device:TPU:4, one launch (start us, length us, event | category | flops | bytes accessed | tf_op | source)
XLA Modules:
  0.0 1746.3 jit_solution(2386285231414660180)
XLA Ops:
  7.2 0.0 all-gather.9.cloned.1.call-start
  7.2 0.7 all-gather.9.cloned.1.call-update
  7.9 0.0 all-gather.11.cloned.1.call-start
  7.9 0.7 all-gather.11.cloned.1.call-update
  8.6 0.0 all-gather.5.cloned.1.call-start
  8.7 0.7 all-gather.5.cloned.1.call-update
  9.4 0.0 all-gather.7.cloned.1.call-start
  9.4 0.5 all-gather.7.cloned.1.call-update
  10.0 0.0 reduce-scatter.2.cloned.1.call-start
  10.0 507.7 %all-gather.9.cloned.1.call-done = bf16[128,6144]{0,1:T(8,128)(2,1)} async-done(((bf16[128,96]{0,1:T(8,128)(2,1)}), bf16[128,6144]{0,1:T(8,128)(2,1)}) %all-gather.9.cloned.1.call-update) | async-done | bytes 1572880 | tf_op jit(solution)/shard_map/all_gather | solution.py:40
  517.7 36.0 %all-gather.11.cloned.1.call-done = bf16[6144,384]{1,0:T(8,128)(2,1)} async-done(((bf16[768,384]{1,0:T(8,128)(2,1)}), bf16[6144,384]{1,0:T(8,128)(2,1)}) %all-gather.11.cloned.1.call-update) | async-done | bytes 4718608 | tf_op jit(solution)/shard_map/all_gather | solution.py:49
  553.6 3.9 multiply_convert_fusion
  557.5 502.7 %all-gather.5.cloned.1.call-done = bf16[128,6144]{0,1:T(8,128)(2,1)} async-done(((bf16[128,96]{0,1:T(8,128)(2,1)}), bf16[128,6144]{0,1:T(8,128)(2,1)}) %all-gather.5.cloned.1.call-update) | async-done | bytes 1572880 | tf_op jit(solution)/shard_map/all_gather | solution.py:39
  1060.2 35.8 %all-gather.7.cloned.1.call-done = bf16[384,6144]{1,0:T(8,128)(2,1)} async-done(((bf16[384,768]{1,0:T(8,128)(2,1)}), bf16[384,6144]{1,0:T(8,128)(2,1)}) %all-gather.7.cloned.1.call-update) | async-done | bytes 4718608 | tf_op jit(solution)/shard_map/all_gather | solution.py:45
  1096.0 0.0 copy-start
  1096.0 4.5 fusion
  1100.5 0.0 copy-done
  1100.5 3.0 fusion.6
  1103.6 0.0 copy-start.4
  1103.6 0.0 copy-start.2
  1103.6 0.0 reduce-scatter.2.cloned.1.call-update
  1103.6 0.7 copy-done.4
  1104.3 0.1 select_reduce_fusion
  1104.4 0.6 copy-done.2
  1105.0 0.7 copy.14
  1105.7 0.6 gather_fusion.1
  1106.4 1.4 select_bitcast_fusion
  1107.7 0.0 copy-start.1
  1107.7 6.1 all-to-all-start.1
  1113.9 0.0 copy-done.1
  1113.9 0.7 copy.13
  1114.6 0.6 gather_fusion
  1115.3 1.4 select_bitcast_fusion.1
  1116.7 15.7 all-to-all-done.1
  1132.4 6.7 all-to-all-start
  1139.1 27.7 %all_gather.24 = bf16[1024,384]{1,0:T(8,128)(2,1)S(1)} all-gather(bf16[128,384]{1,0:T(8,128)(2,1)S(1)} %get-tuple-element.19), channel_id=1, replica_groups=mesh['rep'=8,'section'=8,'tp'=8] {'rep'}, dimensions={0}, use_global_device_ids=true | all-gather | bytes 884736 | tf_op jit(solution)/shard_map/all_gather | solution.py:73
  1166.8 2.4 convolution_bitcast_fusion
  1169.2 14.5 all_gather.23
  1183.7 0.0 all-to-all-done
  1183.7 2.1 convolution_bitcast_fusion.1
  1185.8 0.0 copy-start.3
  1185.8 1.6 maximum_bitcast_fusion
  1187.4 550.9 %reduce-scatter.2.cloned.1.call-done = f32[128,96]{0,1:T(8,128)} async-done(((f32[128,6144]{0,1:T(8,128)}), f32[128,96]{0,1:T(8,128)}) %reduce-scatter.2.cloned.1.call-update) | async-done | bytes 49168 | tf_op jit(solution)/shard_map/reduce_scatter | solution.py:55
  1738.3 0.0 copy-done.3
  1738.3 1.4 add_convert_fusion
  (3 shorter events, 0.0 us)
Async XLA Ops:
  7.2 510.5 %all-gather.9.cloned.1.call-start = ((), (), s32[]{:S(2)}) async-start(), calls=%async_computation.5 | async-start | bytes 1597440 | tf_op jit(solution)/shard_map/all_gather | solution.py:40
  7.9 545.7 %all-gather.11.cloned.1.call-start = ((), (), s32[]{:S(2)}) async-start(), calls=%async_computation.6 | async-start | bytes 5308416 | tf_op jit(solution)/shard_map/all_gather | solution.py:49
  8.6 1051.6 %all-gather.5.cloned.1.call-start = ((), (), s32[]{:S(2)}) async-start(), calls=%async_computation.3 | async-start | bytes 1597440 | tf_op jit(solution)/shard_map/all_gather | solution.py:39
  9.4 1086.6 %all-gather.7.cloned.1.call-start = ((), (), s32[]{:S(2)}) async-start(), calls=%async_computation.4 | async-start | bytes 5308416 | tf_op jit(solution)/shard_map/all_gather | solution.py:45
  10.0 1728.3 %reduce-scatter.2.cloned.1.call-start = ((), (), s32[]{:S(2)}) async-start(), calls=%async_computation.7 | async-start | bytes 3194880 | tf_op jit(solution)/shard_map/reduce_scatter | solution.py:55
  1096.0 4.5 copy-start
  1103.6 0.7 copy-start.4
  1103.6 1.4 copy-start.2
  1107.7 6.2 copy-start.1
  1107.7 24.6 %all-to-all-start.1 = ((bf16[128,8,768]{2,0,1:T(8,128)(2,1)}), bf16[128,8,768]{2,0,1:T(8,128)(2,1)}, u32[]{:S(2)}, u32[]{:S(2)}) async-start(bf16[128,8,768]{2,0,1:T(8,128)(2,1)} %select_bitcast_fusion), calls=%async_computation.2 | async-start | bytes 3145728 | tf_op jit(solution)/shard_map/all_to_all | solution.py:69
  1132.4 51.3 %all-to-all-start = ((bf16[128,8,768]{2,0,1:T(8,128)(2,1)}), bf16[128,8,768]{2,0,1:T(8,128)(2,1)S(1)}, u32[]{:S(2)}, u32[]{:S(2)}) async-start(bf16[128,8,768]{2,0,1:T(8,128)(2,1)} %select_bitcast_fusion.1), calls=%async_computation.1 | async-start | bytes 3145728 | tf_op jit(solution)/shard_map/all_to_all | solution.py:68
  1185.8 552.5 %copy-start.3 = (bf16[128,96]{0,1:T(8,128)(2,1)S(1)}, bf16[128,96]{0,1:T(8,128)(2,1)}, u32[]{:S(2)}) copy-start(bf16[128,96]{0,1:T(8,128)(2,1)} %param.7) | copy-start | bytes 73732
Sparse Core Ops, SparseCore 0:
  10.1 507.5 all-gather.8
  519.8 33.7 all-gather.10
  555.7 504.4 all-gather.4
  1062.2 33.7 all-gather.6
  1103.7 634.5 reduce-scatter.1
where the time goes:
time: 1750 us
  waiting for transfers between devices  1650 us (94%)
  blocking collectives  42.2 us (2%)
    reduce_scatter x1, waiting for transfers between devices, body(): lax.psum_scatter(partial_grad, ('section', 'tp'), scatter_dimension=1, ti...  551 us
    all_gather x1, waiting for transfers between devices, body(): lax.all_gather(saved_inputs, ('section', 'tp'), axis=1, tiled=True)  508 us
    all_gather x1, waiting for transfers between devices, body(): lax.all_gather(cotangent, ('section', 'tp'), axis=1, tiled=True)  503 us
    all_gather x1, waiting for transfers between devices, body(): lax.all_gather(up_weight, 'rep', axis=0, tiled=True)  36 us
    all_gather x1, waiting for transfers between devices, body(): lax.all_gather(down_weight, 'rep', axis=1, tiled=True)  35.8 us
  transfers between devices with their start and end apart: 7, of which 6 were waited for; matrix products, arithmetic and copies ran while one was open for 1% of the time, Pallas kernels for 0%

commit v1 on v0

v1 whole, which is shorter than its diff:
```python
import math

import jax
import jax.numpy as jnp
from jax import lax
from jax.sharding import Mesh
from jax.sharding import PartitionSpec as P

GELU_SCALE = math.sqrt(2.0 / math.pi)
GELU_CUBIC = 0.044715

REP = ("x", "core")
COL = ("section", "zh")
SHARD = ("section", "y", "zh")


def gelu_pair(values):
    tanh_part = jnp.tanh(GELU_SCALE * (values + GELU_CUBIC * values * values * values))
    value = 0.5 * values * (1.0 + tanh_part)
    deriv = 0.5 * (1.0 + tanh_part) + 0.5 * values * (1.0 - tanh_part * tanh_part) * GELU_SCALE * (
        1.0 + 3.0 * GELU_CUBIC * values * values
    )
    return value, deriv


def spread(block, axes, count):
    copies = lax.optimization_barrier(jnp.broadcast_to(block[None], (count,) + block.shape))
    return lax.all_to_all(copies, axes, split_axis=0, concat_axis=0, tiled=True)


def body(cotangent, saved_inputs, up_weight, down_weight, block_owner):
    n_rep = lax.axis_size(REP)
    n_col = lax.axis_size(COL)
    n_sec = lax.axis_size("section")
    n_y = lax.axis_size("y")
    n_zh = lax.axis_size("zh")
    tokens, width = cotangent.shape
    block = up_weight.shape[0]
    hidden_here = up_weight.shape[1]

    up_full = lax.all_gather(up_weight, REP, axis=0, tiled=True)
    down_full = lax.all_gather(down_weight, REP, axis=1, tiled=True)

    pair = jnp.stack([saved_inputs.T, cotangent.T])
    column = spread(pair, COL, n_col)
    column = column.reshape(n_sec, n_zh, 2, width, tokens)

    owners = jnp.arange(n_rep, dtype=jnp.int32)
    inverse = jnp.sum(
        jnp.where(block_owner[:, None, :] == owners[None, :, None], owners[None, None, :], 0),
        axis=2,
    )
    picked = jnp.stack(
        [jnp.take(column[:, :, j], inverse[j], axis=0) for j in range(2)], axis=1
    )
    owned = lax.all_to_all(picked, REP, split_axis=0, concat_axis=0, tiled=True)
    owned = owned.reshape(n_rep, 2, n_zh * width, tokens)
    owned = owned.transpose(1, 2, 0, 3).reshape(2, n_zh * width, n_rep * tokens)
    own_inputs = lax.all_gather(owned[0], "y", axis=0, tiled=True)
    own_grads = lax.all_gather(owned[1], "y", axis=0, tiled=True)

    full = spread(column, "y", n_y)
    full = full.transpose(3, 1, 0, 2, 4, 5).reshape(2, n_rep * block, tokens)

    pre_act = lax.dot_general(
        full[0], up_full, (((0,), (0,)), ((), ())), preferred_element_type=jnp.float32
    )
    back_grad = lax.dot_general(
        full[1], down_full, (((0,), (1,)), ((), ())), preferred_element_type=jnp.float32
    )
    value, deriv = gelu_pair(pre_act)
    hidden = value.astype(jnp.bfloat16)
    dpre = (back_grad * deriv).astype(jnp.bfloat16)

    both = lax.all_gather(jnp.concatenate([dpre, hidden], axis=1), REP, axis=0, tiled=True)

    partial_grad = lax.dot_general(
        up_full, dpre, (((1,), (1,)), ((), ())), preferred_element_type=jnp.float32
    ).astype(jnp.bfloat16)
    partial_grad = partial_grad.reshape(n_sec, n_y, n_zh * width, tokens).transpose(1, 0, 2, 3)
    parts = lax.all_to_all(partial_grad, "y", split_axis=0, concat_axis=0, tiled=True)
    parts = jnp.sum(parts.astype(jnp.float32), axis=0).astype(jnp.bfloat16)
    parts = parts.reshape(n_col, width, tokens)
    parts = lax.all_to_all(parts, COL, split_axis=0, concat_axis=0, tiled=True)
    summed = jnp.sum(parts.astype(jnp.float32), axis=0).T
    input_grads = (cotangent.astype(jnp.float32) + summed).astype(jnp.bfloat16)

    up_block = jnp.dot(own_inputs, both[:, :hidden_here], preferred_element_type=jnp.float32)
    down_block = jnp.dot(own_grads, both[:, hidden_here:], preferred_element_type=jnp.float32)
    weight_grads = jnp.stack([up_block, down_block])[:, None]
    return (input_grads, weight_grads)


def solution(mesh):
    fine = Mesh(mesh.devices.reshape(4, 2, 8, 4, 2), ("x", "core", "section", "y", "zh"))
    in_specs = (
        P(REP, SHARD),
        P(REP, SHARD),
        P(REP, SHARD),
        P(SHARD, REP),
        P(),
    )
    out_specs = (P(REP, SHARD), P(None, REP, None, SHARD))
    return jax.shard_map(body, mesh=fine, in_specs=in_specs, out_specs=out_specs, check_vma=False)
```

time: 1750 us -> 234 us (0.13)
  the two profiles are of different devices: /device:TPU:4 before, /device:TPU:1 now
where the time goes in v1:
time: 234 us; the launch traced here: 231 us
  waiting for transfers between devices  117 us (50%)
  blocking collectives  35.5 us (15%)
  starting transfers between devices  30.5 us (13%)
  matrix products  17.1 us (7%)
  between operations  14 us (6%)
  local copies, waits for them, and re-layouts  11.9 us (5%)
  other arithmetic  5.44 us (2%)
    all_to_all x2, waiting for transfers between devices, spread(): return lax.all_to_all(copies, axes, split_axis=0, concat_axis=0, tiled=True)  81.8 us
    all_to_all x1, blocking collectives, body(): parts = lax.all_to_all(parts, COL, split_axis=0, concat_axis=0, tiled=True)  35.5 us
    all_to_all x2, starting transfers between devices, spread(): return lax.all_to_all(copies, axes, split_axis=0, concat_axis=0, tiled=True)  20.2 us
    all_to_all x1, waiting for transfers between devices, body(): owned = lax.all_to_all(picked, REP, split_axis=0, concat_axis=0, tiled=True)  16 us
    all_to_all x1, waiting for transfers between devices, body(): lax.all_to_all(partial_grad, 'y', split_axis=0, concat_axis=0, tiled=True)  12.8 us
    all_to_all x1, starting transfers between devices, body(): owned = lax.all_to_all(picked, REP, split_axis=0, concat_axis=0, tiled=True)  6.66 us
  transfers between devices with their start and end apart: 9, of which 5 were waited for; matrix products, arithmetic and copies ran while one was open for 13% of the time, Pallas kernels for 0%

profile of v1, /device:TPU:1, one launch (start us, length us, event | category | flops | bytes accessed | tf_op | source)
XLA Modules:
  0.0 231.2 jit_solution(12760003619800135840)
XLA Ops:
  7.2 0.0 all-gather.8.cloned.1.call-start
  7.2 0.7 all-gather.8.cloned.1.call-update
  7.9 0.0 copy-start.4
  7.9 0.0 all-gather.6.cloned.1.call-start
  8.0 0.7 all-gather.6.cloned.1.call-update
  8.7 0.8 pad_maximum_fusion.2
  9.4 1.0 broadcast_in_dim.40
  10.5 15.7 %all-to-all-start = ((bf16[16,2,96,128]{3,2,1,0:T(8,128)(2,1)}), bf16[16,2,96,128]{3,2,1,0:T(8,128)(2,1)S(1)}, u32[]{:S(2)}, u32[]{:S(2)}) async-start(bf16[16,2,96,128]{3,2,1,0:T(8,128)(2,1)} %broadcast_in_dim.40), calls=%async_computation | async-start | bytes 1572864 | tf_op jit(solution)/shard_map/all_to_all | solution.py:28
  26.2 0.0 copy-done.4
  26.2 0.1 select_reduce_fusion
  26.4 40.0 %all-to-all-done = bf16[16,2,96,128]{3,2,1,0:T(8,128)(2,1)S(1)} async-done(((bf16[16,2,96,128]{3,2,1,0:T(8,128)(2,1)}), bf16[16,2,96,128]{3,2,1,0:T(8,128)(2,1)S(1)}, u32[]{:S(2)}, u32[]{:S(2)}) %all-to-all-start) | async-done | bytes 786464 | tf_op jit(solution)/shard_map/all_to_all | solution.py:28
  66.4 0.1 slice_bitcast_fusion.1
  66.4 0.6 gather_fusion
  67.1 0.6 gather_fusion.1
  67.7 0.1 select_bitcast_fusion
  67.9 1.0 pad_maximum_fusion
  68.8 6.7 %all-to-all-start.4 = ((bf16[8,2,2,96,128]{4,3,2,1,0:T(8,128)(2,1)}), bf16[8,2,2,96,128]{4,3,2,1,0:T(8,128)(2,1)S(1)}, u32[]{:S(2)}, u32[]{:S(2)}) async-start(bf16[8,2,2,96,128]{4,3,2,1,0:T(8,128)(2,1)} %pad_maximum_fusion), calls=%async_computation.4 | async-start | bytes 1572864 | tf_op jit(solution)/shard_map/all_to_all | solution.py:56
  75.5 0.1 copy.17
  75.6 2.4 %broadcast_in_dim.42 = bf16[4,8,2,2,96,128]{5,4,2,1,3,0:T(8,128)(2,1)} broadcast(bf16[8,2,2,96,128]{4,3,1,0,2:T(8,128)(2,1)S(1)} %copy.17), dimensions={1,2,3,4,5} | broadcast | bytes 3932160 | tf_op jit(solution)/shard_map/broadcast_in_dim | solution.py:27
  78.0 16.0 %all-to-all-done.4 = bf16[8,2,2,96,128]{4,3,2,1,0:T(8,128)(2,1)S(1)} async-done(((bf16[8,2,2,96,128]{4,3,2,1,0:T(8,128)(2,1)}), bf16[8,2,2,96,128]{4,3,2,1,0:T(8,128)(2,1)S(1)}, u32[]{:S(2)}, u32[]{:S(2)}) %all-to-all-start.4) | async-done | bytes 786464 | tf_op jit(solution)/shard_map/all_to_all | solution.py:56
  94.0 0.0 copy-start
  94.0 0.9 copy-done
  94.8 4.4 %all-to-all-start.1 = ((bf16[4,8,2,2,96,128]{5,4,2,1,3,0:T(8,128)(2,1)}), bf16[4,8,2,2,96,128]{5,4,2,1,3,0:T(8,128)(2,1)S(1)}, u32[]{:S(2)}, u32[]{:S(2)}) async-start(bf16[4,8,2,2,96,128]{5,4,2,1,3,0:T(8,128)(2,1)} %broadcast_in_dim.42), calls=%async_computation.1 | async-start | bytes 6291456 | tf_op jit(solution)/shard_map/all_to_all | solution.py:28
  99.2 0.0 all-gather.10.cloned.1.call-start
  99.2 1.7 copy.30
  101.0 0.1 fusion.11
  101.0 0.8 copy.32
  101.9 0.0 all-gather.10.cloned.1.call-update
  101.9 0.0 all-gather.12.cloned.1.call-start
  101.9 41.8 %all-to-all-done.1 = bf16[4,8,2,2,96,128]{5,4,2,1,3,0:T(8,128)(2,1)S(1)} async-done(((bf16[4,8,2,2,96,128]{5,4,2,1,3,0:T(8,128)(2,1)}), bf16[4,8,2,2,96,128]{5,4,2,1,3,0:T(8,128)(2,1)S(1)}, u32[]{:S(2)}, u32[]{:S(2)}) %all-to-all-start.1) | async-done | bytes 3145760 | tf_op jit(solution)/shard_map/all_to_all | solution.py:28
  143.8 0.3 copy.29
  144.0 0.3 fusion.10
  144.3 0.0 all-gather.8.cloned.1.call-done
  144.4 4.1 %multiply_convert_fusion = (bf16[128,384]{1,0:T(8,128)(2,1)}, f32[128,384]{1,0:T(8,128)}) fusion(bf16[6144,128]{1,0:T(8,128)(2,1)S(1)} %bitcast.71, bf16[6144,384]{1,0:T(8,128)(2,1)} %all-gather.8.cloned.1.call-done), kind=kOutput, calls=%fused_computation.29 | convolution fusion | flops 604422144 | bytes 6586368 | tf_op jit(solution)/shard_map/dot_general | solution.py:65
  148.5 0.0 all-gather.6.cloned.1.call-done
  148.5 0.0 copy-start.2
  148.5 3.9 %fusion.1 = bf16[128,384]{1,0:T(8,128)(2,1)S(1)} fusion(bf16[6144,128]{1,0:T(8,128)(2,1)S(1)} %bitcast.70, bf16[384,6144]{1,0:T(8,128)(2,1)} %all-gather.6.cloned.1.call-done, f32[128,384]{1,0:T(8,128)} %get-tuple-element.24), kind=kOutput, calls=%fused_computation.9 | convolution fusion | flops 604913664 | bytes 6586368 | tf_op jit(solution)/shard_map/dot_general | solution.py:68
  152.4 0.0 copy-start.1
  152.4 0.0 copy-done.2
  152.4 0.7 pad_maximum_fusion.1
  153.1 0.0 copy-done.1
  153.1 0.0 all-gather.12.cloned.1.call-update
  153.1 4.0 %fusion = bf16[6144,128]{0,1:T(8,128)(2,1)S(1)} fusion(bf16[128,384]{1,0:T(8,128)(2,1)} %copy-done.1, bf16[6144,384]{1,0:T(8,128)(2,1)} %all-gather.8.cloned.1.call-done), kind=kOutput, calls=%fused_computation.3 | convolution fusion | flops 604766208 | bytes 6389760 | tf_op jit(solution)/shard_map/dot_general | solution.py:77
  157.1 0.9 copy.19
  158.0 1.3 copy.20
  159.3 3.6 %all-to-all-start.2 = ((bf16[4,8,192,128]{3,2,1,0:T(8,128)(2,1)}), bf16[4,8,192,128]{3,2,1,0:T(8,128)(2,1)S(1)}, u32[]{:S(2)}, u32[]{:S(2)}) async-start(bf16[4,8,192,128]{3,2,1,0:T(8,128)(2,1)} %copy.20), calls=%async_computation.2 | async-start | bytes 3145728 | tf_op jit(solution)/shard_map/all_to_all | solution.py:81
  162.9 0.0 all-gather.14.cloned.1.call-start
  162.9 0.8 copy.31
  163.8 0.0 all-gather.14.cloned.1.call-update
  163.8 0.0 copy-start.3
  163.8 12.8 %all-to-all-done.2 = bf16[4,8,192,128]{3,2,1,0:T(8,128)(2,1)S(1)} async-done(((bf16[4,8,192,128]{3,2,1,0:T(8,128)(2,1)}), bf16[4,8,192,128]{3,2,1,0:T(8,128)(2,1)S(1)}, u32[]{:S(2)}, u32[]{:S(2)}) %all-to-all-start.2) | async-done | bytes 1572896 | tf_op jit(solution)/shard_map/all_to_all | solution.py:81
  176.6 0.3 reduce_sum.30
  177.0 35.5 %all_to_all.25 = bf16[16,96,128]{2,1,0:T(8,128)(2,1)S(1)} all-to-all(bf16[16,96,128]{2,1,0:T(8,128)(2,1)S(1)} %bitcast.78), channel_id=1, replica_groups=mesh['x'=4,'core'=2,'section'=8,'y'=4,'zh'=2] {'section','zh'}, dimensions={0} | all-to-all | bytes 786432 | tf_op jit(solution)/shard_map/all_to_all | solution.py:84
  212.5 0.1 convert_reduce_fusion
  212.6 0.0 copy-done.3
  212.6 0.6 fusion.9
  213.2 0.0 all-gather.10.cloned.1.call-done
  213.2 0.0 all-gather.12.cloned.1.call-done
  213.2 0.0 copy-start.5
  213.2 2.7 %convolution_bitcast_fusion.1 = f32[1,768,384]{2,1,0:T(8,128)S(1)} fusion(bf16[768,1024]{1,0:T(8,128)(2,1)} %all-gather.10.cloned.1.call-done, bf16[1024,768]{1,0:T(8,128)(2,1)} %all-gather.12.cloned.1.call-done), kind=kOutput, calls=%fused_computation.7 | convolution fusion | flops 603979776 | bytes 3538944 | tf_op jit(solution)/shard_map/dot_general | solution.py:88
  215.9 4.6 %all-gather.14.cloned.1.call-done = bf16[768,1024]{1,0:T(8,128)(2,1)} async-done(((bf16[192,1024]{1,0:T(8,128)(2,1)}), bf16[768,1024]{1,0:T(8,128)(2,1)}) %all-gather.14.cloned.1.call-update) | async-done | bytes 1572880 | tf_op jit(solution)/shard_map/all_gather | solution.py:60
  220.6 0.0 copy-done.5
  220.6 2.4 %convolution_bitcast_fusion = f32[1,768,384]{2,1,0:T(8,128)S(1)} fusion(bf16[768,1024]{1,0:T(8,128)(2,1)} %all-gather.14.cloned.1.call-done, bf16[1024,768]{1,0:T(8,128)(2,1)S(1)} %copy-done.5), kind=kOutput, calls=%fused_computation.6 | convolution fusion | flops 603979776 | bytes 3538944 | tf_op jit(solution)/shard_map/dot_general | solution.py:89
  222.9 1.7 maximum_bitcast_fusion
  (3 shorter events, 0.0 us)
Async XLA Ops:
  7.2 137.2 %all-gather.8.cloned.1.call-start = ((), (), s32[]{:S(2)}) async-start(), calls=%async_computation.6 | async-start | bytes 5308416 | tf_op jit(solution)/shard_map/all_gather | solution.py:41
  7.9 18.3 %copy-start.4 = (s32[2,8]{1,0:T(2,128)S(1)}, s32[2,8]{1,0:T(2,128)}, u32[]{:S(2)}) copy-start(s32[2,8]{1,0:T(2,128)} %param.11) | copy-start | bytes 196
  7.9 140.5 %all-gather.6.cloned.1.call-start = ((), (), s32[]{:S(2)}) async-start(), calls=%async_computation.5 | async-start | bytes 5308416 | tf_op jit(solution)/shard_map/all_gather | solution.py:42
  10.5 55.9 %all-to-all-start = ((bf16[16,2,96,128]{3,2,1,0:T(8,128)(2,1)}), bf16[16,2,96,128]{3,2,1,0:T(8,128)(2,1)S(1)}, u32[]{:S(2)}, u32[]{:S(2)}) async-start(bf16[16,2,96,128]{3,2,1,0:T(8,128)(2,1)} %broadcast_in_dim.40), calls=%async_computation | async-start | bytes 1572864 | tf_op jit(solution)/shard_map/all_to_all | solution.py:28
  68.8 25.1 %all-to-all-start.4 = ((bf16[8,2,2,96,128]{4,3,2,1,0:T(8,128)(2,1)}), bf16[8,2,2,96,128]{4,3,2,1,0:T(8,128)(2,1)S(1)}, u32[]{:S(2)}, u32[]{:S(2)}) async-start(bf16[8,2,2,96,128]{4,3,2,1,0:T(8,128)(2,1)} %pad_maximum_fusion), calls=%async_computation.4 | async-start | bytes 1572864 | tf_op jit(solution)/shard_map/all_to_all | solution.py:56
  94.0 0.9 copy-start
  94.8 48.9 %all-to-all-start.1 = ((bf16[4,8,2,2,96,128]{5,4,2,1,3,0:T(8,128)(2,1)}), bf16[4,8,2,2,96,128]{5,4,2,1,3,0:T(8,128)(2,1)S(1)}, u32[]{:S(2)}, u32[]{:S(2)}) async-start(bf16[4,8,2,2,96,128]{5,4,2,1,3,0:T(8,128)(2,1)} %broadcast_in_dim.42), calls=%async_computation.1 | async-start | bytes 6291456 | tf_op jit(solution)/shard_map/all_to_all | solution.py:28
  99.2 114.0 %all-gather.10.cloned.1.call-start = ((), (), s32[]{:S(2)}) async-start(), calls=%async_computation.7 | async-start | bytes 1966080 | tf_op jit(solution)/shard_map/all_gather | solution.py:59
  101.9 111.3 %all-gather.12.cloned.1.call-start = ((), (), s32[]{:S(2)}) async-start(), calls=%async_computation.8 | async-start | bytes 1769472 | tf_op jit(solution)/shard_map/all_gather | solution.py:75
  148.5 3.9 %copy-start.2 = (bf16[128,384]{1,0:T(8,128)(2,1)S(1)}, bf16[128,384]{1,0:T(8,128)(2,1)}, u32[]{:S(2)}) copy-start(bf16[128,384]{1,0:T(8,128)(2,1)} %get-tuple-element.23) | copy-start | bytes 294916
  152.4 0.7 copy-start.1
  159.3 17.3 %all-to-all-start.2 = ((bf16[4,8,192,128]{3,2,1,0:T(8,128)(2,1)}), bf16[4,8,192,128]{3,2,1,0:T(8,128)(2,1)S(1)}, u32[]{:S(2)}, u32[]{:S(2)}) async-start(bf16[4,8,192,128]{3,2,1,0:T(8,128)(2,1)} %copy.20), calls=%async_computation.2 | async-start | bytes 3145728 | tf_op jit(solution)/shard_map/all_to_all | solution.py:81
  162.9 57.7 %all-gather.14.cloned.1.call-start = ((), (), s32[]{:S(2)}) async-start(), calls=%async_computation.9 | async-start | bytes 1966080 | tf_op jit(solution)/shard_map/all_gather | solution.py:60
  163.8 48.8 %copy-start.3 = (bf16[128,96]{0,1:T(8,128)(2,1)S(1)}, bf16[128,96]{0,1:T(8,128)(2,1)}, u32[]{:S(2)}) copy-start(bf16[128,96]{0,1:T(8,128)(2,1)} %param.7) | copy-start | bytes 73732
  213.2 7.3 %copy-start.5 = (bf16[1024,768]{1,0:T(8,128)(2,1)S(1)}, bf16[1024,768]{1,0:T(8,128)(2,1)}, u32[]{:S(2)}) copy-start(bf16[1024,768]{1,0:T(8,128)(2,1)} %all-gather.12.cloned.1.call-done) | copy-start | bytes 4718596
Sparse Core Ops, SparseCore 0:
  10.1 47.6 all-gather.7
  60.0 48.7 all-gather.5
  110.8 38.6 all-gather.9
  153.3 31.1 all-gather.11
  186.4 34.0 all-gather.13

commit v2 on v1

v2 whole, which is shorter than its diff:
```python
import math

import jax
import jax.numpy as jnp
from jax import lax
from jax.sharding import Mesh
from jax.sharding import PartitionSpec as P

GELU_SCALE = math.sqrt(2.0 / math.pi)
GELU_CUBIC = 0.044715

REP = ("x", "core")
SHARD = ("sh", "sl", "y", "zh")


def gelu_pair(values):
    tanh_part = jnp.tanh(GELU_SCALE * (values + GELU_CUBIC * values * values * values))
    value = 0.5 * values * (1.0 + tanh_part)
    deriv = 0.5 * (1.0 + tanh_part) + 0.5 * values * (1.0 - tanh_part * tanh_part) * GELU_SCALE * (
        1.0 + 3.0 * GELU_CUBIC * values * values
    )
    return value, deriv


def spread(block, axes, count):
    copies = lax.optimization_barrier(jnp.broadcast_to(block[None], (count,) + block.shape))
    return lax.all_to_all(copies, axes, split_axis=0, concat_axis=0, tiled=True)


def shift(block, axis, step):
    size = lax.axis_size(axis)
    return lax.ppermute(block, axis, [(i, (i + step) % size) for i in range(size)])


def body(cotangent, saved_inputs, up_weight, down_weight, block_owner):
    n_x = lax.axis_size("x")
    n_core = lax.axis_size("core")
    n_rep = n_x * n_core
    n_sh = lax.axis_size("sh")
    n_sl = lax.axis_size("sl")
    n_y = lax.axis_size("y")
    n_zh = lax.axis_size("zh")
    tokens, width = cotangent.shape
    block = up_weight.shape[0]
    hidden_here = up_weight.shape[1]

    up_full = lax.all_gather(up_weight, REP, axis=0, tiled=True)
    down_full = lax.all_gather(down_weight, REP, axis=1, tiled=True)

    pair = jnp.stack([saved_inputs.T, cotangent.T])
    spaced = spread(pair, ("sh", "zh"), n_sh * n_zh)
    column = lax.all_gather(spaced, "sl", axis=0, tiled=False)
    full = spread(column, "y", n_y)
    full = full.reshape(n_y, n_sl, n_sh, n_zh, 2, width, tokens)
    full = full.transpose(4, 2, 1, 0, 3, 5, 6).reshape(2, n_rep, block, tokens)

    owners = jnp.arange(n_rep, dtype=jnp.int32)
    inverse = jnp.sum(
        jnp.where(block_owner[:, None, :] == owners[None, :, None], owners[None, None, :], 0),
        axis=2,
    )
    here = lax.axis_index("x")
    core = lax.axis_index("core")
    steps = jnp.arange(n_x, dtype=jnp.int32)
    ahead = ((here + steps) % n_x) * n_core
    keep, give = (
        jnp.stack(
            [jnp.take(full[j], jnp.take(inverse[j], ahead + c), axis=0) for j in range(2)], axis=1
        )
        for c in (core, 1 - core)
    )
    got = shift(give, "core", 1)
    message = jnp.stack([jnp.where(core == 0, keep, got), jnp.where(core == 0, got, keep)], axis=1)
    owned = [message[0]] + [shift(message[k], "x", k) for k in range(1, n_x)]

    flat = full.reshape(2, n_rep * block, tokens)
    pre_act = lax.dot_general(
        flat[0], up_full, (((0,), (0,)), ((), ())), preferred_element_type=jnp.float32
    )
    back_grad = lax.dot_general(
        flat[1], down_full, (((0,), (1,)), ((), ())), preferred_element_type=jnp.float32
    )
    value, deriv = gelu_pair(pre_act)
    hidden = value.astype(jnp.bfloat16)
    dpre = (back_grad * deriv).astype(jnp.bfloat16)

    both = lax.all_gather(jnp.concatenate([dpre, hidden], axis=1), REP, axis=0, tiled=True)

    partial_grad = lax.dot_general(
        up_full, dpre, (((1,), (1,)), ((), ())), preferred_element_type=jnp.float32
    ).astype(jnp.bfloat16)
    partial_grad = partial_grad.reshape(n_sh, n_sl, n_y, n_zh, width, tokens)
    partial_grad = partial_grad.transpose(2, 0, 1, 3, 4, 5).reshape(n_y, -1, width, tokens)
    parts = lax.all_to_all(partial_grad, "y", split_axis=0, concat_axis=0, tiled=True)
    parts = jnp.sum(parts.astype(jnp.float32), axis=0).astype(jnp.bfloat16)
    parts = lax.all_to_all(parts, ("sh", "sl", "zh"), split_axis=0, concat_axis=0, tiled=True)
    summed = jnp.sum(parts.astype(jnp.float32), axis=0).T
    input_grads = (cotangent.astype(jnp.float32) + summed).astype(jnp.bfloat16)

    rows = n_core * tokens
    ordered = jnp.take(
        both.reshape(n_x, rows, 2 * hidden_here), (here - steps) % n_x, axis=0
    ).reshape(n_x * rows, 2 * hidden_here)
    own_inputs, own_grads = (
        jnp.concatenate([owned[k][c, j] for k in range(n_x) for c in range(n_core)], axis=1)
        for j in range(2)
    )
    up_block = jnp.dot(own_inputs, ordered[:, :hidden_here], preferred_element_type=jnp.float32)
    down_block = jnp.dot(own_grads, ordered[:, hidden_here:], preferred_element_type=jnp.float32)
    weight_grads = jnp.stack([up_block, down_block])[:, None]
    return (input_grads, weight_grads)


def solution(mesh):
    fine = Mesh(mesh.devices.reshape(4, 2, 2, 4, 4, 2), ("x", "core", "sh", "sl", "y", "zh"))
    in_specs = (
        P(REP, SHARD),
        P(REP, SHARD),
        P(REP, SHARD),
        P(SHARD, REP),
        P(),
    )
    out_specs = (P(REP, SHARD), P(None, REP, None, SHARD))
    return jax.shard_map(body, mesh=fine, in_specs=in_specs, out_specs=out_specs, check_vma=False)
```

time: 234 us -> 209 us (0.89)
  waiting for transfers between devices: 117 us -> 55.9 us
  local copies, waits for them, and re-layouts: 11.9 us -> 29.4 us
  other arithmetic: 5.44 us -> 18.9 us
  blocking collectives: 35.5 us -> 48.4 us
  matrix products: 17.1 us -> 11 us
    all_to_all x2 -> x1, waiting for transfers between devices: 81.8 us -> 30.1 us  [spread(): return lax.all_to_all(copies, axes, split_axis=0, concat_axis=0, tiled=True)]
    ppermute x0 -> x4, waiting for transfers between devices: none -> 23.3 us  [shift(): lax.ppermute(block, axis, [(i, (i + step) % size) for i in range(size)])]
    all_gather x0 -> x1, blocking collectives: none -> 20 us  [body(): column = lax.all_gather(spaced, 'sl', axis=0, tiled=False)]
    ppermute x0 -> x4, starting transfers between devices: none -> 18 us  [shift(): lax.ppermute(block, axis, [(i, (i + step) % size) for i in range(size)])]
    all_to_all x1, waiting for transfers between devices: 16 us -> 0.01 us  [body(): lax.all_to_all(parts, ('sh', 'sl', 'zh'), split_axis=0, concat_axis=0, ti...]
    all_to_all x2 -> x1, starting transfers between devices: 20.2 us -> 4.31 us  [spread(): return lax.all_to_all(copies, axes, split_axis=0, concat_axis=0, tiled=True)]
    all_to_all x1, waiting for transfers between devices: 12.8 us -> 1.06 us  [body(): lax.all_to_all(partial_grad, 'y', split_axis=0, concat_axis=0, tiled=True)]
    unnamed x14 -> x21, local copies, waits for them, and re-layouts: 2.6 us -> 12.5 us
  transfers between devices with their start and end apart: 9 -> 10, of which waited for: 5 -> 4; matrix products, arithmetic and copies ran while one was open for 13% -> 25% of each run, Pallas kernels for 0% -> 0%
where the time goes in v2:
time: 209 us; the launch traced here: 208 us
  waiting for transfers between devices  55.9 us (27%)
  blocking collectives  48.4 us (23%)
  starting transfers between devices  30.2 us (14%)
  local copies, waits for them, and re-layouts  29.4 us (14%)
  other arithmetic  18.9 us (9%)
  between operations  14 us (7%)
  matrix products  11 us (5%)
    all_to_all x1, waiting for transfers between devices, spread(): return lax.all_to_all(copies, axes, split_axis=0, concat_axis=0, tiled=True)  30.1 us
    all_to_all x1, blocking collectives, spread(): return lax.all_to_all(copies, axes, split_axis=0, concat_axis=0, tiled=True)  28.3 us
    ppermute x4, waiting for transfers between devices, shift(): lax.ppermute(block, axis, [(i, (i + step) % size) for i in range(size)])  23.3 us
    all_gather x1, blocking collectives, body(): column = lax.all_gather(spaced, 'sl', axis=0, tiled=False)  20 us
    ppermute x4, starting transfers between devices, shift(): lax.ppermute(block, axis, [(i, (i + step) % size) for i in range(size)])  18 us
    unnamed x21, local copies, waits for them, and re-layouts  12.5 us
    another operation x5, other arithmetic, body(): jnp.stack([jnp.take(full[j], jnp.take(inverse[j], ahead + c), axis=0) for...  7.17 us
    gather x4, local copies, waits for them, and re-layouts, body(): jnp.take(full[j], jnp.take(inverse[j], ahead + c), axis=0)  6.12 us
  transfers between devices with their start and end apart: 10, of which 4 were waited for; matrix products, arithmetic and copies ran while one was open for 25% of the time, Pallas kernels for 0%

profile of v2, /device:TPU:1, one launch (start us, length us, event | category | flops | bytes accessed | tf_op | source)
XLA Modules:
  0.0 207.7 jit_solution(4654798653577155381)
XLA Ops:
  7.2 0.0 all-gather.7.cloned.1.call-start
  7.2 0.7 all-gather.7.cloned.1.call-update
  7.9 0.0 all-gather.5.cloned.1.call-start
  7.9 0.7 all-gather.5.cloned.1.call-update
  8.6 0.8 pad_maximum_fusion.4
  9.4 28.3 %all_to_all.20 = bf16[4,2,96,128]{3,2,1,0:T(8,128)(2,1)S(1)} all-to-all(bf16[4,2,96,128]{3,2,1,0:T(8,128)(2,1)S(1)} %broadcast_in_dim.56), channel_id=1, replica_groups=mesh['x'=4,'core'=2,'sh'=2,'sl'=4,'y'=4,'zh'=2] {'sh','zh'}, dimensions={0} | all-to-all | bytes 393216 | tf_op jit(solution)/shard_map/all_to_all | solution.py:27
  37.8 20.0 %all-gather = bf16[16,2,96,128]{3,2,1,0:T(8,128)(2,1)S(1)} all-gather(bf16[4,2,96,128]{3,2,1,0:T(8,128)(2,1)S(1)} %all_to_all.20), channel_id=2, replica_groups=mesh['x'=4,'core'=2,'sh'=2,'sl'=4,'y'=4,'zh'=2] {'sl'}, dimensions={0}, use_global_device_ids=true | all-gather | bytes 983040 | tf_op jit(solution)/shard_map/all_gather | solution.py:52
  57.8 2.4 %broadcast_in_dim.57 = bf16[4,4,4,2,96,128]{5,4,3,2,1,0:T(8,128)(2,1)} broadcast(bf16[4,4,2,96,128]{4,3,2,1,0:T(8,128)(2,1)S(1)} %bitcast.147), dimensions={1,2,3,4,5} | broadcast | bytes 3932160 | tf_op jit(solution)/shard_map/broadcast_in_dim | solution.py:26
  60.3 4.3 %all-to-all-start.1 = ((bf16[4,4,4,2,96,128]{5,4,3,2,1,0:T(8,128)(2,1)}), bf16[4,4,4,2,96,128]{5,4,3,2,1,0:T(8,128)(2,1)S(1)}, u32[]{:S(2)}, u32[]{:S(2)}) async-start(bf16[4,4,4,2,96,128]{5,4,3,2,1,0:T(8,128)(2,1)} %broadcast_in_dim.57), calls=%async_computation.1 | async-start | bytes 6291456 | tf_op jit(solution)/shard_map/all_to_all | solution.py:27
  64.6 0.1 select_reduce_fusion
  64.8 0.6 gather_fusion.5
  65.4 0.6 gather_fusion.7
  66.1 0.6 gather_fusion.1
  66.7 0.6 gather_fusion.3
  67.4 30.1 %all-to-all-done.1 = bf16[4,4,4,2,96,128]{5,4,3,2,1,0:T(8,128)(2,1)S(1)} async-done(((bf16[4,4,4,2,96,128]{5,4,3,2,1,0:T(8,128)(2,1)}), bf16[4,4,4,2,96,128]{5,4,3,2,1,0:T(8,128)(2,1)S(1)}, u32[]{:S(2)}, u32[]{:S(2)}) %all-to-all-start.1) | async-done | bytes 3145760 | tf_op jit(solution)/shard_map/all_to_all | solution.py:27
  97.6 0.4 fusion.38
  97.9 0.1 copy.37
  98.1 0.1 copy.38
  98.2 1.5 gather_fusion.8
  99.7 1.5 gather_fusion.6
  101.2 1.3 select_bitcast_fusion.2
  102.6 0.1 select_bitcast_fusion.3
  102.7 1.3 pad_maximum_fusion.1
  104.1 7.5 %collective-permute-start = (bf16[4,2,768,128]{3,2,0,1:T(8,128)(2,1)}, bf16[4,2,768,128]{3,2,0,1:T(8,128)(2,1)}, u32[]{:S(2)}, u32[]{:S(2)}) collective-permute-start(bf16[4,2,768,128]{3,2,0,1:T(8,128)(2,1)} %pad_maximum_fusion.1), channel_id=1, source_target_pairs={{0,64},{64,0},{1,65},{65,1},{2,66},{66,2},{3,67},{67,3},{4,68},{68... | collective-permute-start | bytes 4718600 | tf_op jit(solution)/shard_map/ppermute | solution.py:32
  111.5 1.5 gather_fusion.4
  113.1 2.2 %select_bitcast_fusion.4 = bf16[4,1,768,128]{3,2,0,1:T(8,128)(2,1)} fusion(bf16[4,768,128]{2,1,0:T(8,128)(2,1)} %gather_fusion.4, pred[4]{0:T(512)(128)(4,1)S(1)} %get-tuple-element.48), kind=kLoop, calls=%fused_computation.39 | loop fusion | flops 393216 | bytes 1572868 | tf_op jit(solution)/shard_map/stack | solution.py:67
  115.3 1.5 gather_fusion.2
  116.8 2.2 %select_bitcast_fusion.5 = bf16[4,1,768,128]{3,2,0,1:T(8,128)(2,1)} fusion(bf16[4,768,128]{2,1,0:T(8,128)(2,1)} %gather_fusion.2, pred[4]{0:T(512)(128)(4,1)S(1)} %get-tuple-element.14), kind=kLoop, calls=%fused_computation.40 | loop fusion | flops 393216 | bytes 1572868 | tf_op jit(solution)/shard_map/stack | solution.py:67
  119.0 3.4 %multiply_convert_fusion = (bf16[128,384]{1,0:T(8,128)(2,1)S(1)}, f32[128,384]{1,0:T(8,128)S(1)}) fusion(bf16[6144,128]{1,0:T(8,128)(2,1)S(1)} %bitcast.144, bf16[6144,384]{1,0:T(8,128)(2,1)} %all-gather.7.cloned.1.call-done), kind=kOutput, calls=%fused_computation.82 | convolution fusion | flops 604422144 | bytes 6586368 | tf_op jit(solution)/shard_map/dot_general | solution.py:77
  122.4 4.0 %fusion.1 = bf16[128,384]{1,0:T(8,128)(2,1)S(1)} fusion(bf16[6144,128]{1,0:T(8,128)(2,1)S(1)} %bitcast.141, bf16[384,6144]{1,0:T(8,128)(2,1)} %all-gather.5.cloned.1.call-done, f32[128,384]{1,0:T(8,128)S(1)} %get-tuple-element.53), kind=kOutput, calls=%fused_computation.26 | convolution fusion | flops 604913664 | bytes 6586368 | tf_op jit(solution)/shard_map/dot_general | solution.py:80
  126.4 1.6 fusion
  128.0 0.9 copy.39
  128.9 1.3 copy.40
  130.2 3.6 %all-to-all-start.2 = ((bf16[4,16,96,128]{3,2,1,0:T(8,128)(2,1)}), bf16[4,16,96,128]{3,2,1,0:T(8,128)(2,1)S(1)}, u32[]{:S(2)}, u32[]{:S(2)}) async-start(bf16[4,16,96,128]{3,2,1,0:T(8,128)(2,1)} %bitcast.13), calls=%async_computation.2 | async-start | bytes 3145728 | tf_op jit(solution)/shard_map/all_to_all | solution.py:94
  133.8 0.0 all-gather.9.cloned.1.call-start
  133.8 3.2 %select_bitcast_fusion = (bf16[4,1,2,768,128]{4,3,0,2,1:T(8,128)(2,1)S(1)}, bf16[4,1,2,768,128]{4,3,0,2,1:T(8,128)(2,1)}) fusion(bf16[4,2,768,128]{3,2,0,1:T(8,128)(2,1)} %collective-permute-done, pred[]{:T(512)S(6)} %eq.20, bf16[4,1,768,128]{3,2,0,1:T(8,128)(2,1)} %select_bitcast_fusion.4, bf16[4,1,768,128]{3,2,0,1:T(8,128)(2,1)} %select_bitcast_fusion.5), kind=kLoop, calls=%fused_computation.21 | loop fusion | flops 2359296 | bytes 6291457 | tf_op jit(solution)/shard_map/stack | solution.py:73
  137.0 0.7 pad_maximum_fusion.3
  137.8 3.2 %fusion.10 = (bf16[2,2,768,128]{3,2,1,0:T(8,128)(2,1)}, bf16[2,2,768,128]{3,2,1,0:T(8,128)(2,1)}, bf16[2,2,768,128]{3,2,1,0:T(8,128)(2,1)}, bf16[2,2,768,128]{3,2,1,0:T(8,128)(2,1)}) fusion(bf16[4,1,2,768,128]{4,3,0,2,1:T(8,128)(2,1)S(1)} %get-tuple-element.26, bf16[4,1,2,768,128]{4,3,0,2,1:T(8,128)(2,1)} %get-tuple-element.27), kind=kLoop, calls=%fused_computation.36 | loop fusion | flops 1572864 | bytes 6291456 | tf_op jit(solution)/shard_map/squeeze | solution.py:74
  140.9 3.1 %collective-permute-start.1 = (bf16[2,2,768,128]{3,2,1,0:T(8,128)(2,1)}, bf16[2,2,768,128]{3,2,1,0:T(8,128)(2,1)}, u32[]{:S(2)}, u32[]{:S(2)}) collective-permute-start(bf16[2,2,768,128]{3,2,1,0:T(8,128)(2,1)} %get-tuple-element.24), channel_id=1, source_target_pairs={{0,128},{128,256},{256,384},{384,0},{1,129},{129,257},{257,385},{3... | collective-permute-start | bytes 2359304 | tf_op jit(solution)/shard_map/ppermute | solution.py:32
  144.0 0.1 broadcast_in_dim.60
  144.1 4.4 %collective-permute-start.2 = (bf16[2,2,768,128]{3,2,1,0:T(8,128)(2,1)}, bf16[2,2,768,128]{3,2,1,0:T(8,128)(2,1)}, u32[]{:S(2)}, u32[]{:S(2)}) collective-permute-start(bf16[2,2,768,128]{3,2,1,0:T(8,128)(2,1)} %get-tuple-element.25), channel_id=1, source_target_pairs={{0,256},{128,384},{256,0},{384,128},{1,257},{129,385},{257,1},{385... | collective-permute-start | bytes 2359304 | tf_op jit(solution)/shard_map/ppermute | solution.py:32
  148.6 1.9 fusion.31
  150.5 3.0 %collective-permute-start.3 = (bf16[2,2,768,128]{3,2,1,0:T(8,128)(2,1)}, bf16[2,2,768,128]{3,2,1,0:T(8,128)(2,1)S(1)}, u32[]{:S(2)}, u32[]{:S(2)}) collective-permute-start(bf16[2,2,768,128]{3,2,1,0:T(8,128)(2,1)} %get-tuple-element.22), channel_id=1, source_target_pairs={{0,384},{128,0},{256,128},{384,256},{1,385},{129,1},{257,129},{385... | collective-permute-start | bytes 2359304 | tf_op jit(solution)/shard_map/ppermute | solution.py:32
  153.5 1.1 all-to-all-done.2
  154.6 1.1 reduce_sum.30
  155.7 4.3 %all-to-all-start.3 = ((bf16[16,96,128]{2,1,0:T(8,128)(2,1)}), bf16[16,96,128]{2,1,0:T(8,128)(2,1)S(1)}, u32[]{:S(2)}, u32[]{:S(2)}) async-start(bf16[16,96,128]{2,1,0:T(8,128)(2,1)} %reduce_sum.30), calls=%async_computation.3 | async-start | bytes 786432 | tf_op jit(solution)/shard_map/all_to_all | solution.py:96
  160.0 0.8 fusion.30
  160.8 8.3 %collective-permute-done.1 = bf16[2,2,768,128]{3,2,1,0:T(8,128)(2,1)} collective-permute-done((bf16[2,2,768,128]{3,2,1,0:T(8,128)(2,1)}, bf16[2,2,768,128]{3,2,1,0:T(8,128)(2,1)}, u32[]{:S(2)}, u32[]{:S(2)}) %collective-permute-start.1) | collective-permute-done | bytes 786464 | tf_op jit(solution)/shard_map/ppermute | solution.py:32
  169.0 1.9 fusion.29
  170.9 1.8 fusion.28
  172.8 15.0 %collective-permute-done.2 = bf16[2,2,768,128]{3,2,1,0:T(8,128)(2,1)} collective-permute-done((bf16[2,2,768,128]{3,2,1,0:T(8,128)(2,1)}, bf16[2,2,768,128]{3,2,1,0:T(8,128)(2,1)}, u32[]{:S(2)}, u32[]{:S(2)}) %collective-permute-start.2) | collective-permute-done | bytes 786464 | tf_op jit(solution)/shard_map/ppermute | solution.py:32
  187.7 1.8 fusion.27
  189.6 1.8 fusion.26
  191.4 0.8 fusion.25
  192.2 0.8 fusion.24
  193.0 0.1 convert_reduce_fusion
  193.1 0.6 fusion.32
  193.7 2.1 gather_fusion
  195.8 0.3 bitcast_select_fusion
  196.1 1.1 copy-done.5
  197.2 1.0 convolution_bitcast_fusion
  198.2 0.4 copy-done.4
  198.6 1.0 convolution_bitcast_fusion.1
  199.6 1.6 maximum_bitcast_fusion
  (34 shorter events, 0.2 us)
Async XLA Ops:
  7.2 111.8 %all-gather.7.cloned.1.call-start = ((), (), s32[]{:S(2)}) async-start(), calls=%async_computation.5 | async-start | bytes 5308416 | tf_op jit(solution)/shard_map/all_gather | solution.py:47
  7.9 114.5 %all-gather.5.cloned.1.call-start = ((), (), s32[]{:S(2)}) async-start(), calls=%async_computation.4 | async-start | bytes 5308416 | tf_op jit(solution)/shard_map/all_gather | solution.py:48
  60.3 4.3 %copy-start.6 = (s32[2,8]{1,0:T(2,128)S(1)}, s32[2,8]{1,0:T(2,128)}, u32[]{:S(2)}) copy-start(s32[2,8]{1,0:T(2,128)} %param.13) | copy-start | bytes 196
  60.3 37.3 %all-to-all-start.1 = ((bf16[4,4,4,2,96,128]{5,4,3,2,1,0:T(8,128)(2,1)}), bf16[4,4,4,2,96,128]{5,4,3,2,1,0:T(8,128)(2,1)S(1)}, u32[]{:S(2)}, u32[]{:S(2)}) async-start(bf16[4,4,4,2,96,128]{5,4,3,2,1,0:T(8,128)(2,1)} %broadcast_in_dim.57), calls=%async_computation.1 | async-start | bytes 6291456 | tf_op jit(solution)/shard_map/all_to_all | solution.py:27
  101.2 1.4 copy-start.2
  104.1 29.7 %collective-permute-start = (bf16[4,2,768,128]{3,2,0,1:T(8,128)(2,1)}, bf16[4,2,768,128]{3,2,0,1:T(8,128)(2,1)}, u32[]{:S(2)}, u32[]{:S(2)}) collective-permute-start(bf16[4,2,768,128]{3,2,0,1:T(8,128)(2,1)} %pad_maximum_fusion.1), channel_id=1, source_target_pairs={{0,64},{64,0},{1,65},{65,1},{2,66},{66,2},{3,67},{67,3},{4,68},{68... | collective-permute-start | bytes 4718600 | tf_op jit(solution)/shard_map/ppermute | solution.py:32
  122.4 4.0 %copy-start = (bf16[6144,384]{1,0:T(8,128)(2,1)S(1)}, bf16[6144,384]{1,0:T(8,128)(2,1)}, u32[]{:S(2)}) copy-start(bf16[6144,384]{1,0:T(8,128)(2,1)} %all-gather.7.cloned.1.call-done) | copy-start | bytes 14155780
  130.2 24.4 %all-to-all-start.2 = ((bf16[4,16,96,128]{3,2,1,0:T(8,128)(2,1)}), bf16[4,16,96,128]{3,2,1,0:T(8,128)(2,1)S(1)}, u32[]{:S(2)}, u32[]{:S(2)}) async-start(bf16[4,16,96,128]{3,2,1,0:T(8,128)(2,1)} %bitcast.13), calls=%async_computation.2 | async-start | bytes 3145728 | tf_op jit(solution)/shard_map/all_to_all | solution.py:94
  133.8 59.9 %all-gather.9.cloned.1.call-start = ((), (), s32[]{:S(2)}) async-start(), calls=%async_computation.6 | async-start | bytes 1769472 | tf_op jit(solution)/shard_map/all_gather | solution.py:87
  140.9 28.1 %collective-permute-start.1 = (bf16[2,2,768,128]{3,2,1,0:T(8,128)(2,1)}, bf16[2,2,768,128]{3,2,1,0:T(8,128)(2,1)}, u32[]{:S(2)}, u32[]{:S(2)}) collective-permute-start(bf16[2,2,768,128]{3,2,1,0:T(8,128)(2,1)} %get-tuple-element.24), channel_id=1, source_target_pairs={{0,128},{128,256},{256,384},{384,0},{1,129},{129,257},{257,385},{3... | collective-permute-start | bytes 2359304 | tf_op jit(solution)/shard_map/ppermute | solution.py:32
  144.1 43.6 %collective-permute-start.2 = (bf16[2,2,768,128]{3,2,1,0:T(8,128)(2,1)}, bf16[2,2,768,128]{3,2,1,0:T(8,128)(2,1)}, u32[]{:S(2)}, u32[]{:S(2)}) collective-permute-start(bf16[2,2,768,128]{3,2,1,0:T(8,128)(2,1)} %get-tuple-element.25), channel_id=1, source_target_pairs={{0,256},{128,384},{256,0},{384,128},{1,257},{129,385},{257,1},{385... | collective-permute-start | bytes 2359304 | tf_op jit(solution)/shard_map/ppermute | solution.py:32
  150.5 9.4 %copy-start.1 = (bf16[2,2,768,128]{3,2,1,0:T(8,128)(2,1)S(1)}, bf16[2,2,768,128]{3,2,1,0:T(8,128)(2,1)}, u32[]{:S(2)}) copy-start(bf16[2,2,768,128]{3,2,1,0:T(8,128)(2,1)} %get-tuple-element.23) | copy-start | bytes 2359300
  150.5 40.9 %collective-permute-start.3 = (bf16[2,2,768,128]{3,2,1,0:T(8,128)(2,1)}, bf16[2,2,768,128]{3,2,1,0:T(8,128)(2,1)S(1)}, u32[]{:S(2)}, u32[]{:S(2)}) collective-permute-start(bf16[2,2,768,128]{3,2,1,0:T(8,128)(2,1)} %get-tuple-element.22), channel_id=1, source_target_pairs={{0,384},{128,0},{256,128},{384,256},{1,385},{129,1},{257,129},{385... | collective-permute-start | bytes 2359304 | tf_op jit(solution)/shard_map/ppermute | solution.py:32
  155.7 37.3 %all-to-all-start.3 = ((bf16[16,96,128]{2,1,0:T(8,128)(2,1)}), bf16[16,96,128]{2,1,0:T(8,128)(2,1)S(1)}, u32[]{:S(2)}, u32[]{:S(2)}) async-start(bf16[16,96,128]{2,1,0:T(8,128)(2,1)} %reduce_sum.30), calls=%async_computation.3 | async-start | bytes 786432 | tf_op jit(solution)/shard_map/all_to_all | solution.py:96
  189.6 3.5 %copy-start.3 = (bf16[128,96]{0,1:T(8,128)(2,1)S(1)}, bf16[128,96]{0,1:T(8,128)(2,1)}, u32[]{:S(2)}) copy-start(bf16[128,96]{0,1:T(8,128)(2,1)} %param.9) | copy-start | bytes 73732
  195.8 1.4 copy-start.5
  197.2 1.4 copy-start.4
Sparse Core Ops, SparseCore 0:
  10.1 47.6 all-gather.6
  60.0 42.0 all-gather.4
  137.9 52.2 all-gather.8

commit v3 on v2

v3 whole, which is shorter than its diff:
```python
import math

import jax
import jax.numpy as jnp
from jax import lax
from jax.experimental import pallas as pl
from jax.experimental.pallas import tpu as pltpu
from jax.sharding import Mesh
from jax.sharding import PartitionSpec as P

GELU_SCALE = math.sqrt(2.0 / math.pi)
GELU_CUBIC = 0.044715

REP = ("x", "core")
SHARD = ("sh", "sl", "y", "zh")


def gelu_pair(values):
    tanh_part = jnp.tanh(GELU_SCALE * (values + GELU_CUBIC * values * values * values))
    value = 0.5 * values * (1.0 + tanh_part)
    deriv = 0.5 * (1.0 + tanh_part) + 0.5 * values * (1.0 - tanh_part * tanh_part) * GELU_SCALE * (
        1.0 + 3.0 * GELU_CUBIC * values * values
    )
    return value, deriv


def spread(block, axes, count):
    copies = lax.optimization_barrier(jnp.broadcast_to(block[None], (count,) + block.shape))
    return lax.all_to_all(copies, axes, split_axis=0, concat_axis=0, tiled=True)


def shift(block, axis, step):
    size = lax.axis_size(axis)
    return lax.ppermute(block, axis, [(i, (i + step) % size) for i in range(size)])


def end_of(position, e):
    return jnp.where(e == 0, position[1], 1 - position[1])


def arrange_kernel(steps, owner, position, plain, *refs):
    del owner, position
    chosen, flats, messages = refs[:steps], refs[steps : steps + 2], refs[steps + 2 :]
    for j in range(2):

        @pl.when(pl.program_id(0) == j)
        def _(j=j):
            for b in range(plain.shape[1]):
                flats[j][b] = plain[:, b, 0, :, 0]

    for k in range(steps):
        messages[k][0, 0] = chosen[k][:, 0, 0, :, 0]


def arrange(gathered, owner, position, n_x, n_core):
    n_y, n_sl, n_sh, n_zh, _, width, tokens = gathered.shape
    n_blocks = n_sl * n_sh
    piece = (n_y, 1, 1, n_zh, 1, width, tokens)

    def chosen_at(k):
        def index(j, e, owner, position):
            target = lax.rem(position[0] + k, n_x) * n_core + end_of(position, e)
            b = sum(jnp.where(owner[j, i] == target, i, 0) for i in range(n_blocks))
            return (0, lax.rem(b, n_sl), lax.div(b, n_sl), 0, j, 0, 0)

        return index

    out = (n_y, n_zh, width, tokens)
    return pl.pallas_call(
        lambda *refs: arrange_kernel(n_x, *refs),
        grid_spec=pltpu.PrefetchScalarGridSpec(
            num_scalar_prefetch=2,
            grid=(2, n_sh),
            in_specs=[
                pl.BlockSpec(
                    (n_y, n_sl, 1, n_zh, 1, width, tokens), lambda j, h, *_: (0, 0, h, 0, j, 0, 0)
                )
            ]
            + [pl.BlockSpec(piece, chosen_at(k)) for k in range(n_x)],
            out_specs=[
                pl.BlockSpec(
                    (n_sl,) + out, lambda j, h, *_: (jnp.where(j == 0, h, n_sh - 1), 0, 0, 0, 0)
                ),
                pl.BlockSpec((n_sl,) + out, lambda j, h, *_: (jnp.where(j == 0, 0, h), 0, 0, 0, 0)),
            ]
            + [pl.BlockSpec((1, 1) + out, lambda j, e, *_: (e, j, 0, 0, 0, 0))] * n_x,
        ),
        out_shape=[jax.ShapeDtypeStruct((n_blocks,) + out, gathered.dtype)] * 2
        + [jax.ShapeDtypeStruct((n_core, 2) + out, gathered.dtype)] * n_x,
        compiler_params=pltpu.CompilerParams(vmem_limit_bytes=24 * 1024 * 1024),
        cost_estimate=pl.CostEstimate(
            flops=0, bytes_accessed=8 * gathered.size, transcendentals=0
        ),
    )(owner, position, gathered, *([gathered] * n_x))


def collect_kernel(steps, *refs):
    for k in range(steps):
        refs[-1][k, 0] = refs[k][0, 0]


def collect(pieces, after):
    steps = len(pieces)
    rows, tokens = pieces[0].shape[2:]
    return pl.pallas_call(
        lambda *refs: collect_kernel(steps, *refs),
        grid=(2,),
        in_specs=[pl.BlockSpec((1, 1, rows, tokens), lambda j: (1, j, 0, 0))] * steps
        + [pl.BlockSpec(memory_space=pl.ANY)],
        out_specs=pl.BlockSpec((steps, 1, rows, tokens), lambda j: (0, j, 0, 0)),
        out_shape=jax.ShapeDtypeStruct((steps, 2, rows, tokens), pieces[0].dtype),
        compiler_params=pltpu.CompilerParams(vmem_limit_bytes=24 * 1024 * 1024),
        cost_estimate=pl.CostEstimate(
            flops=0, bytes_accessed=8 * steps * rows * tokens, transcendentals=0
        ),
    )(*pieces, after)


def grads_kernel(steps, n_core, position, *refs):
    mine, (theirs, both, out) = refs[:steps], refs[steps:]
    total = None
    for k in range(steps):
        row = lax.rem(position[0] + (steps - k), steps) * n_core
        left = jnp.concatenate([mine[k][0, 0], theirs[k, 0]], axis=1)
        right = jnp.concatenate([both[row + position[1]], both[row + 1 - position[1]]], axis=0)
        term = jnp.dot(left, right, preferred_element_type=jnp.float32)
        total = term if total is None else total + term
    out[0, 0] = total


def block_grads(mine, theirs, both, position, n_core):
    steps = len(mine)
    rows, tokens = mine[0].shape[2:]
    groups, _, columns = both.shape
    hidden_here = columns // 2
    return pl.pallas_call(
        lambda *refs: grads_kernel(steps, n_core, *refs),
        grid_spec=pltpu.PrefetchScalarGridSpec(
            num_scalar_prefetch=1,
            grid=(2,),
            in_specs=[pl.BlockSpec((1, 1, rows, tokens), lambda j, *_: (0, j, 0, 0))] * steps
            + [
                pl.BlockSpec((steps, 1, rows, tokens), lambda j, *_: (0, j, 0, 0)),
                pl.BlockSpec((groups, tokens, hidden_here), lambda j, *_: (0, 0, j)),
            ],
            out_specs=pl.BlockSpec((1, 1, rows, hidden_here), lambda j, *_: (j, 0, 0, 0)),
        ),
        out_shape=jax.ShapeDtypeStruct((2, 1, rows, hidden_here), jnp.float32),
        compiler_params=pltpu.CompilerParams(vmem_limit_bytes=32 * 1024 * 1024),
        cost_estimate=pl.CostEstimate(
            flops=4 * rows * groups * tokens * hidden_here,
            bytes_accessed=4 * rows * groups * tokens + 16 * rows * hidden_here,
            transcendentals=0,
        ),
    )(position, *mine, theirs, both)


def body(cotangent, saved_inputs, up_weight, down_weight, block_owner):
    n_x = lax.axis_size("x")
    n_core = lax.axis_size("core")
    n_rep = n_x * n_core
    n_sh = lax.axis_size("sh")
    n_sl = lax.axis_size("sl")
    n_y = lax.axis_size("y")
    n_zh = lax.axis_size("zh")
    tokens, width = cotangent.shape
    block = up_weight.shape[0]
    hidden_here = up_weight.shape[1]

    up_full = lax.all_gather(up_weight, REP, axis=0, tiled=True)
    down_full = lax.all_gather(down_weight, REP, axis=1, tiled=True)

    pair = jnp.stack([saved_inputs.T, cotangent.T])
    spaced = spread(pair, ("sh", "zh"), n_sh * n_zh)
    column = lax.all_gather(spaced, "sl", axis=0, tiled=False)
    full = spread(column, "y", n_y)
    full = full.reshape(n_y, n_sl, n_sh, n_zh, 2, width, tokens)

    position = jnp.stack([lax.axis_index("x"), lax.axis_index("core")])
    inputs_flat, grads_flat, *messages = arrange(full, block_owner, position, n_x, n_core)
    messages = [piece.reshape(n_core, 2, block, tokens) for piece in messages]
    mine = [messages[0]] + [shift(messages[k], "x", k) for k in range(1, n_x)]

    inputs_flat = inputs_flat.reshape(n_rep * block, tokens)
    grads_flat = grads_flat.reshape(n_rep * block, tokens)
    pre_act = lax.dot_general(
        inputs_flat, up_full, (((0,), (0,)), ((), ())), preferred_element_type=jnp.float32
    )
    back_grad = lax.dot_general(
        grads_flat, down_full, (((0,), (1,)), ((), ())), preferred_element_type=jnp.float32
    )
    value, deriv = gelu_pair(pre_act)
    hidden = value.astype(jnp.bfloat16)
    dpre = (back_grad * deriv).astype(jnp.bfloat16)

    both = lax.all_gather(jnp.concatenate([dpre, hidden], axis=1), REP, axis=0, tiled=True)

    partial_grad = lax.dot_general(
        up_full, dpre, (((1,), (1,)), ((), ())), preferred_element_type=jnp.float32
    ).astype(jnp.bfloat16)
    partial_grad = partial_grad.reshape(n_sh, n_sl, n_y, n_zh, width, tokens)
    partial_grad = partial_grad.transpose(2, 1, 0, 3, 4, 5)
    parts = lax.all_to_all(partial_grad, "y", split_axis=0, concat_axis=0, tiled=True)
    parts = jnp.sum(parts.astype(jnp.float32), axis=0).astype(jnp.bfloat16)
    theirs = shift(collect(mine, parts), "core", 1)
    parts = lax.all_to_all(parts, "sl", split_axis=0, concat_axis=0, tiled=True)
    parts = jnp.sum(parts.astype(jnp.float32), axis=0).reshape(n_sh * n_zh, width, tokens)
    parts = lax.all_to_all(parts, ("sh", "zh"), split_axis=0, concat_axis=0, tiled=True)
    summed = jnp.sum(parts, axis=0).T
    input_grads = (cotangent.astype(jnp.float32) + summed).astype(jnp.bfloat16)

    weight_grads = block_grads(
        mine, theirs, both.reshape(n_rep, tokens, 2 * hidden_here), position, n_core
    )
    return (input_grads, weight_grads)


def solution(mesh):
    fine = Mesh(mesh.devices.reshape(4, 2, 2, 4, 4, 2), ("x", "core", "sh", "sl", "y", "zh"))
    in_specs = (
        P(REP, SHARD),
        P(REP, SHARD),
        P(REP, SHARD),
        P(SHARD, REP),
        P(),
    )
    out_specs = (P(REP, SHARD), P(None, REP, None, SHARD))
    return jax.shard_map(body, mesh=fine, in_specs=in_specs, out_specs=out_specs, check_vma=False)
```

time: 209 us -> 206 us (0.986)
  the two profiles are of different devices: /device:TPU:1 before, /device:TPU:42 now
where the time goes in v3:
time: 206 us
  waiting for transfers between devices  74.7 us (36%)
  blocking collectives  48.9 us (24%)
  starting transfers between devices  33.6 us (16%)
  between operations  13.9 us (7%)
  local copies, waits for them, and re-layouts  10.9 us (5%)
  matrix products  9.66 us (5%)
  Pallas kernels  9.4 us (5%)
  other arithmetic  4.57 us (2%)
    all_to_all x1, waiting for transfers between devices, spread(): return lax.all_to_all(copies, axes, split_axis=0, concat_axis=0, tiled=True)  33.6 us
    all_to_all x1, blocking collectives, spread(): return lax.all_to_all(copies, axes, split_axis=0, concat_axis=0, tiled=True)  33.2 us
    ppermute x4, waiting for transfers between devices, shift(): lax.ppermute(block, axis, [(i, (i + step) % size) for i in range(size)])  22.1 us
    all_gather x1, blocking collectives, body(): column = lax.all_gather(spaced, 'sl', axis=0, tiled=False)  15.7 us
    all_to_all x1, waiting for transfers between devices, body(): lax.all_to_all(parts, ('sh', 'zh'), split_axis=0, concat_axis=0, tiled=True)  12.9 us
    ppermute x4, starting transfers between devices, shift(): lax.ppermute(block, axis, [(i, (i + step) % size) for i in range(size)])  12.5 us
    all_to_all x1, starting transfers between devices, body(): lax.all_to_all(partial_grad, 'y', split_axis=0, concat_axis=0, tiled=True)  5.8 us
    unnamed x20, local copies, waits for them, and re-layouts  5.48 us
  transfers between devices with their start and end apart: 11, of which 6 were waited for; matrix products, arithmetic and copies ran while one was open for 5% of the time, Pallas kernels for 5%

profile of v3, /device:TPU:42, one launch (start us, length us, event | category | flops | bytes accessed | tf_op | source)
XLA Modules:
  0.0 205.6 jit_solution(11548950144496241443)
XLA Ops:
  7.2 0.0 all-gather.7.cloned.1.call-start
  7.2 0.7 all-gather.7.cloned.1.call-update
  7.9 0.0 all-gather.5.cloned.1.call-start
  7.9 0.7 all-gather.5.cloned.1.call-update
  8.6 0.8 pad_maximum_fusion.1
  9.4 33.2 %all_to_all.25 = bf16[4,2,96,128]{3,2,1,0:T(8,128)(2,1)S(1)} all-to-all(bf16[4,2,96,128]{3,2,1,0:T(8,128)(2,1)S(1)} %broadcast_in_dim.4), channel_id=1, replica_groups=mesh['x'=4,'core'=2,'sh'=2,'sl'=4,'y'=4,'zh'=2] {'sh','zh'}, dimensions={0} | all-to-all | bytes 393216 | tf_op jit(solution)/shard_map/all_to_all | solution.py:29
  42.6 15.7 %all-gather = bf16[16,2,96,128]{3,2,1,0:T(8,128)(2,1)S(1)} all-gather(bf16[4,2,96,128]{3,2,1,0:T(8,128)(2,1)S(1)} %all_to_all.25), channel_id=2, replica_groups=mesh['x'=4,'core'=2,'sh'=2,'sl'=4,'y'=4,'zh'=2] {'sl'}, dimensions={0}, use_global_device_ids=true | all-gather | bytes 983040 | tf_op jit(solution)/shard_map/all_gather | solution.py:175
  58.4 2.4 %broadcast_in_dim.5 = bf16[4,4,4,2,96,128]{5,4,3,2,1,0:T(8,128)(2,1)} broadcast(bf16[4,4,2,96,128]{4,3,2,1,0:T(8,128)(2,1)S(1)} %bitcast.45), dimensions={1,2,3,4,5} | broadcast | bytes 3932160 | tf_op jit(solution)/shard_map/broadcast_in_dim | solution.py:28
  60.8 0.0 copy-start.6
  60.8 5.0 %all-to-all-start.1 = ((bf16[4,4,4,2,96,128]{5,4,3,2,1,0:T(8,128)(2,1)}), bf16[4,4,4,2,96,128]{5,4,3,2,1,0:T(8,128)(2,1)S(1)}, u32[]{:S(2)}, u32[]{:S(2)}) async-start(bf16[4,4,4,2,96,128]{5,4,3,2,1,0:T(8,128)(2,1)} %broadcast_in_dim.5), calls=%async_computation.1 | async-start | bytes 6291456 | tf_op jit(solution)/shard_map/all_to_all | solution.py:29
  65.8 0.1 pad_add_fusion.refs_1_.refs_0_
  65.9 33.6 %all-to-all-done.1 = bf16[4,4,4,2,96,128]{5,4,3,2,1,0:T(8,128)(2,1)S(1)} async-done(((bf16[4,4,4,2,96,128]{5,4,3,2,1,0:T(8,128)(2,1)}), bf16[4,4,4,2,96,128]{5,4,3,2,1,0:T(8,128)(2,1)S(1)}, u32[]{:S(2)}, u32[]{:S(2)}) %all-to-all-start.1) | async-done | bytes 3145760 | tf_op jit(solution)/shard_map/all_to_all | solution.py:29
  99.5 0.0 copy-done.6
  99.5 3.5 %shard_map.68 = (bf16[8,4,2,96,128]{4,3,2,1,0:T(8,128)(2,1)S(1)}, bf16[8,4,2,96,128]{4,3,2,1,0:T(8,128)(2,1)S(1)}, bf16[2,2,4,2,96,128]{5,4,3,2,1,0:T(8,128)(2,1...) custom-call(s32[2,8]{1,0:T(2,128)S(1)} %copy-done.6, ...), custom_call_target="tpu_custom_call" | custom-call | bytes 12582912 | tf_op jit(solution)/shard_map/pallas_call | solution.py:69
  103.1 0.0 copy-start
  103.1 0.9 copy-done
  103.9 0.0 copy-start.2
  103.9 1.1 copy-done.2
  105.1 0.0 copy-start.4
  105.1 1.1 copy-done.4
  106.2 0.0 copy-start.7
  106.2 0.9 copy-done.7
  107.1 0.0 all-gather.7.cloned.1.call-done
  107.1 0.0 copy-start.3
  107.1 4.0 %multiply_convert_fusion = (bf16[128,384]{1,0:T(8,128)(2,1)S(1)}, f32[128,384]{1,0:T(8,128)S(1)}) fusion(bf16[6144,128]{1,0:T(8,128)(2,1)} %bitcast.41, bf16[6144,384]{1,0:T(8,128)(2,1)} %all-gather.7.cloned.1.call-done), kind=kOutput, calls=%fused_computation.13 | convolution fusion | flops 604422144 | bytes 6586368 | tf_op jit(solution)/shard_map/dot_general | solution.py:186
  111.1 0.0 all-gather.5.cloned.1.call-done
  111.1 0.0 copy-done.3
  111.2 0.0 copy-start.8
  111.2 4.1 %fusion.1 = bf16[128,384]{1,0:T(8,128)(2,1)S(1)} fusion(bf16[6144,128]{1,0:T(8,128)(2,1)S(1)} %bitcast.40, bf16[384,6144]{1,0:T(8,128)(2,1)} %all-gather.5.cloned.1.call-done, f32[128,384]{1,0:T(8,128)S(1)} %get-tuple-element.15), kind=kOutput, calls=%fused_computation.3 | convolution fusion | flops 604913664 | bytes 6586368 | tf_op jit(solution)/shard_map/dot_general | solution.py:189
  115.3 0.0 copy-done.8
  115.3 1.6 fusion
  116.9 0.9 copy.17
  117.8 1.3 copy.18
  119.0 5.8 %all-to-all-start.2 = ((bf16[4,4,2,2,96,128]{5,4,3,1,2,0:T(8,128)(2,1)}), bf16[4,4,2,2,96,128]{5,4,3,1,2,0:T(8,128)(2,1)}, u32[]{:S(2)}, u32[]{:S(2)}) async-start(bf16[4,4,2,2,96,128]{5,4,3,1,2,0:T(8,128)(2,1)} %copy.18), calls=%async_computation.2 | async-start | bytes 3145728 | tf_op jit(solution)/shard_map/all_to_all | solution.py:203
  124.8 0.0 all-gather.9.cloned.1.call-start
  124.9 0.7 pad_maximum_fusion
  125.6 0.0 all-gather.9.cloned.1.call-update
  125.6 3.4 %collective-permute-start = (bf16[2,2,768,128]{3,2,1,0:T(8,128)(2,1)}, bf16[2,2,768,128]{3,2,1,0:T(8,128)(2,1)S(1)}, u32[]{:S(2)}, u32[]{:S(2)}) collective-permute-start(bf16[2,2,768,128]{3,2,1,0:T(8,128)(2,1)} %bitcast.16), channel_id=1, source_target_pairs={{0,128},{128,256},{256,384},{384,0},{1,129},{129,257},{257,385},{3... | collective-permute-start | bytes 2359304 | tf_op jit(solution)/shard_map/ppermute | solution.py:34
  129.0 3.0 %collective-permute-start.1 = (bf16[2,2,768,128]{3,2,1,0:T(8,128)(2,1)}, bf16[2,2,768,128]{3,2,1,0:T(8,128)(2,1)S(1)}, u32[]{:S(2)}, u32[]{:S(2)}) collective-permute-start(bf16[2,2,768,128]{3,2,1,0:T(8,128)(2,1)} %bitcast.17), channel_id=1, source_target_pairs={{0,256},{128,384},{256,0},{384,128},{1,257},{129,385},{257,1},{385... | collective-permute-start | bytes 2359304 | tf_op jit(solution)/shard_map/ppermute | solution.py:34
  132.0 0.0 copy-start.1
  132.0 4.2 %collective-permute-start.2 = (bf16[2,2,768,128]{3,2,1,0:T(8,128)(2,1)}, bf16[2,2,768,128]{3,2,1,0:T(8,128)(2,1)S(1)}, u32[]{:S(2)}, u32[]{:S(2)}) collective-permute-start(bf16[2,2,768,128]{3,2,1,0:T(8,128)(2,1)} %bitcast.43), channel_id=1, source_target_pairs={{0,384},{128,0},{256,128},{384,256},{1,385},{129,1},{257,129},{385... | collective-permute-start | bytes 2359304 | tf_op jit(solution)/shard_map/ppermute | solution.py:34
  136.2 4.6 %all-to-all-done.2 = bf16[4,4,2,2,96,128]{5,4,3,1,2,0:T(8,128)(2,1)} async-done(((bf16[4,4,2,2,96,128]{5,4,3,1,2,0:T(8,128)(2,1)}), bf16[4,4,2,2,96,128]{5,4,3,1,2,0:T(8,128)(2,1)}, u32[]{:S(2)}, u32[]{:S(2)}) %all-to-all-start.2) | async-done | bytes 1572896 | tf_op jit(solution)/shard_map/all_to_all | solution.py:203
  140.9 1.7 reduce_sum.30
  142.5 0.8 copy.20.refs_4_
  143.3 5.5 %all-to-all-start.3 = ((bf16[4,2,2,96,128]{4,3,2,1,0:T(8,128)(2,1)}), bf16[4,2,2,96,128]{4,3,2,1,0:T(8,128)(2,1)S(1)}, u32[]{:S(2)}, u32[]{:S(2)}) async-start(bf16[4,2,2,96,128]{4,3,2,1,0:T(8,128)(2,1)} %copy.20.refs_4_), calls=%async_computation.3 | async-start | bytes 786432 | tf_op jit(solution)/shard_map/all_to_all | solution.py:206
  148.8 5.5 %collective-permute-done.refs_1_.refs_2_ = bf16[2,2,768,128]{3,2,1,0:T(8,128)(2,1)S(1)} collective-permute-done((bf16[2,2,768,128]{3,2,1,0:T(8,128)(2,1)}, bf16[2,2,768,128]{3,2,1,0:T(8,128)(2,1)S(1)}, u32[]{:S(2)}, u32[]{:S(2)}) %collective-permute-start) | collective-permute-done | bytes 786464 | tf_op jit(solution)/shard_map/ppermute | solution.py:34
  154.2 5.1 %collective-permute-done.1.refs_2_.refs_3_ = bf16[2,2,768,128]{3,2,1,0:T(8,128)(2,1)S(1)} collective-permute-done((bf16[2,2,768,128]{3,2,1,0:T(8,128)(2,1)}, bf16[2,2,768,128]{3,2,1,0:T(8,128)(2,1)S(1)}, u32[]{:S(2)}, u32[]{:S(2)}) %collective-permute-start.1) | collective-permute-done | bytes 786464 | tf_op jit(solution)/shard_map/ppermute | solution.py:34
  159.4 11.5 %collective-permute-done.2.refs_3_.refs_4_ = bf16[2,2,768,128]{3,2,1,0:T(8,128)(2,1)S(1)} collective-permute-done((bf16[2,2,768,128]{3,2,1,0:T(8,128)(2,1)}, bf16[2,2,768,128]{3,2,1,0:T(8,128)(2,1)S(1)}, u32[]{:S(2)}, u32[]{:S(2)}) %collective-permute-start.2) | collective-permute-done | bytes 786464 | tf_op jit(solution)/shard_map/ppermute | solution.py:34
  170.9 0.0 copy-done.1
  170.9 1.2 shard_map.69
  172.1 1.9 collective-permute-start.3
  174.0 0.0 all-to-all-done.3
  174.0 0.7 convert_reduce_fusion
  174.7 4.7 %all-to-all-start.4 = ((f32[4,96,128]{2,1,0:T(8,128)}), f32[4,96,128]{2,1,0:T(8,128)S(1)}, u32[]{:S(2)}, u32[]{:S(2)}) async-start(f32[4,96,128]{2,1,0:T(8,128)} %bitcast.46), calls=%async_computation.4 | async-start | bytes 393216 | tf_op jit(solution)/shard_map/all_to_all | solution.py:208
  179.4 0.0 collective-permute-done.3.refs_5_
  179.5 0.0 all-gather.9.cloned.1.call-done
  179.5 0.0 copy-start.5
  179.5 1.4 copy-done.5
  180.9 0.0 copy-start.9
  180.9 4.7 %shard_map.70 = f32[2,1,768,384]{3,2,1,0:T(8,128)} custom-call(s32[2]{0:T(128)S(1)} %pad_add_fusion.refs_1_.refs_0_, bf16[2,2,768,128]{3,2,1,0:T(8,128)(2,1)S(1)} %bitcast.39, bf16[2,2,768,128]{3,2,1,0:T(8,128)(2,1)S(1)} %collective-permute-done.refs_1_.refs_2_, bf16[2,2,768,128]{3,2,1,0:T(8,128)(2,1)S(1)} %collective-permute-done.1.refs_2_.refs_3_, ...), custom_call_target="tpu_custom_call" | custom-call | flops 1207959552 | bytes 7864320 | tf_op jit(solution)/shard_map/pallas_call | solution.py:136
  185.6 12.9 %all-to-all-done.4 = f32[4,96,128]{2,1,0:T(8,128)S(1)} async-done(((f32[4,96,128]{2,1,0:T(8,128)}), f32[4,96,128]{2,1,0:T(8,128)S(1)}, u32[]{:S(2)}, u32[]{:S(2)}) %all-to-all-start.4) | async-done | bytes 196640 | tf_op jit(solution)/shard_map/all_to_all | solution.py:208
  198.5 0.0 copy-done.9
  198.5 0.6 fusion.7
  (2 shorter events, 0.0 us)
Async XLA Ops:
  7.2 100.0 %all-gather.7.cloned.1.call-start = ((), (), s32[]{:S(2)}) async-start(), calls=%async_computation.6 | async-start | bytes 5308416 | tf_op jit(solution)/shard_map/all_gather | solution.py:170
  7.9 103.2 %all-gather.5.cloned.1.call-start = ((), (), s32[]{:S(2)}) async-start(), calls=%async_computation.5 | async-start | bytes 5308416 | tf_op jit(solution)/shard_map/all_gather | solution.py:171
  60.8 38.7 %copy-start.6 = (s32[2,8]{1,0:T(2,128)S(1)}, s32[2,8]{1,0:T(2,128)}, u32[]{:S(2)}) copy-start(s32[2,8]{1,0:T(2,128)} %refs_0_.1) | copy-start | bytes 196
  60.8 38.7 %all-to-all-start.1 = ((bf16[4,4,4,2,96,128]{5,4,3,2,1,0:T(8,128)(2,1)}), bf16[4,4,4,2,96,128]{5,4,3,2,1,0:T(8,128)(2,1)S(1)}, u32[]{:S(2)}, u32[]{:S(2)}) async-start(bf16[4,4,4,2,96,128]{5,4,3,2,1,0:T(8,128)(2,1)} %broadcast_in_dim.5), calls=%async_computation.1 | async-start | bytes 6291456 | tf_op jit(solution)/shard_map/all_to_all | solution.py:29
  103.1 0.9 copy-start
  103.9 1.1 copy-start.2
  105.1 1.1 copy-start.4
  106.2 0.9 copy-start.7
  107.1 4.0 %copy-start.3 = (bf16[8,4,2,96,128]{4,3,2,1,0:T(8,128)(2,1)S(1)}, bf16[8,4,2,96,128]{4,3,2,1,0:T(8,128)(2,1)}, u32[]{:S(2)}) copy-start(bf16[8,4,2,96,128]{4,3,2,1,0:T(8,128)(2,1)} %copy-done.2) | copy-start | bytes 4718596
  111.2 4.1 %copy-start.8 = (bf16[6144,384]{1,0:T(8,128)(2,1)S(1)}, bf16[6144,384]{1,0:T(8,128)(2,1)}, u32[]{:S(2)}) copy-start(bf16[6144,384]{1,0:T(8,128)(2,1)} %all-gather.7.cloned.1.call-done) | copy-start | bytes 14155780
  119.0 21.8 %all-to-all-start.2 = ((bf16[4,4,2,2,96,128]{5,4,3,1,2,0:T(8,128)(2,1)}), bf16[4,4,2,2,96,128]{5,4,3,1,2,0:T(8,128)(2,1)}, u32[]{:S(2)}, u32[]{:S(2)}) async-start(bf16[4,4,2,2,96,128]{5,4,3,1,2,0:T(8,128)(2,1)} %copy.18), calls=%async_computation.2 | async-start | bytes 3145728 | tf_op jit(solution)/shard_map/all_to_all | solution.py:203
  124.8 54.6 %all-gather.9.cloned.1.call-start = ((), (), s32[]{:S(2)}) async-start(), calls=%async_computation.7 | async-start | bytes 1769472 | tf_op jit(solution)/shard_map/all_gather | solution.py:196
  125.6 28.7 %collective-permute-start = (bf16[2,2,768,128]{3,2,1,0:T(8,128)(2,1)}, bf16[2,2,768,128]{3,2,1,0:T(8,128)(2,1)S(1)}, u32[]{:S(2)}, u32[]{:S(2)}) collective-permute-start(bf16[2,2,768,128]{3,2,1,0:T(8,128)(2,1)} %bitcast.16), channel_id=1, source_target_pairs={{0,128},{128,256},{256,384},{384,0},{1,129},{129,257},{257,385},{3... | collective-permute-start | bytes 2359304 | tf_op jit(solution)/shard_map/ppermute | solution.py:34
  129.0 30.4 %collective-permute-start.1 = (bf16[2,2,768,128]{3,2,1,0:T(8,128)(2,1)}, bf16[2,2,768,128]{3,2,1,0:T(8,128)(2,1)S(1)}, u32[]{:S(2)}, u32[]{:S(2)}) collective-permute-start(bf16[2,2,768,128]{3,2,1,0:T(8,128)(2,1)} %bitcast.17), channel_id=1, source_target_pairs={{0,256},{128,384},{256,0},{384,128},{1,257},{129,385},{257,1},{385... | collective-permute-start | bytes 2359304 | tf_op jit(solution)/shard_map/ppermute | solution.py:34
  132.0 38.9 %copy-start.1 = (bf16[2,2,4,2,96,128]{5,4,3,2,1,0:T(8,128)(2,1)S(1)}, bf16[2,2,4,2,96,128]{5,4,3,2,1,0:T(8,128)(2,1)}, u32[]{:S(2)}) copy-start(bf16[2,2,4,2,96,128]{5,4,3,2,1,0:T(8,128)(2,1)} %copy-done) | copy-start | bytes 2359300
  132.0 38.8 %collective-permute-start.2 = (bf16[2,2,768,128]{3,2,1,0:T(8,128)(2,1)}, bf16[2,2,768,128]{3,2,1,0:T(8,128)(2,1)S(1)}, u32[]{:S(2)}, u32[]{:S(2)}) collective-permute-start(bf16[2,2,768,128]{3,2,1,0:T(8,128)(2,1)} %bitcast.43), channel_id=1, source_target_pairs={{0,384},{128,0},{256,128},{384,256},{1,385},{129,1},{257,129},{385... | collective-permute-start | bytes 2359304 | tf_op jit(solution)/shard_map/ppermute | solution.py:34
  143.3 30.7 %all-to-all-start.3 = ((bf16[4,2,2,96,128]{4,3,2,1,0:T(8,128)(2,1)}), bf16[4,2,2,96,128]{4,3,2,1,0:T(8,128)(2,1)S(1)}, u32[]{:S(2)}, u32[]{:S(2)}) async-start(bf16[4,2,2,96,128]{4,3,2,1,0:T(8,128)(2,1)} %copy.20.refs_4_), calls=%async_computation.3 | async-start | bytes 786432 | tf_op jit(solution)/shard_map/all_to_all | solution.py:206
  172.1 7.4 %collective-permute-start.3 = (bf16[4,2,768,128]{3,2,1,0:T(8,128)(2,1)}, bf16[4,2,768,128]{3,2,1,0:T(8,128)(2,1)}, u32[]{:S(2)}, u32[]{:S(2)}) collective-permute-start(bf16[4,2,768,128]{3,2,1,0:T(8,128)(2,1)} %shard_map.69), channel_id=1, source_target_pairs={{0,64},{64,0},{1,65},{65,1},{2,66},{66,2},{3,67},{67,3},{4,68},{68... | collective-permute-start | bytes 4718600 | tf_op jit(solution)/shard_map/ppermute | solution.py:34
  174.7 23.7 %all-to-all-start.4 = ((f32[4,96,128]{2,1,0:T(8,128)}), f32[4,96,128]{2,1,0:T(8,128)S(1)}, u32[]{:S(2)}, u32[]{:S(2)}) async-start(f32[4,96,128]{2,1,0:T(8,128)} %bitcast.46), calls=%async_computation.4 | async-start | bytes 393216 | tf_op jit(solution)/shard_map/all_to_all | solution.py:208
  179.5 1.4 copy-start.5
  180.9 17.6 %copy-start.9 = (bf16[128,96]{0,1:T(8,128)(2,1)S(1)}, bf16[128,96]{0,1:T(8,128)(2,1)}, u32[]{:S(2)}) copy-start(bf16[128,96]{0,1:T(8,128)(2,1)} %param.5) | copy-start | bytes 73732
Sparse Core Ops, SparseCore 0:
  10.1 44.9 all-gather.6
  57.3 42.0 all-gather.4
  127.8 38.0 all-gather.8

commit v4 on v3

--- a/solution.py
+++ b/solution.py
@@ -13,6 +13,8 @@
 
 REP = ("x", "core")
 SHARD = ("sh", "sl", "y", "zh")
+VMEM = 60 * 1024 * 1024
+SMALL = 24 * 1024 * 1024
 
 
 def gelu_pair(values):
@@ -38,9 +40,9 @@
     return jnp.where(e == 0, position[1], 1 - position[1])
 
 
-def arrange_kernel(steps, owner, position, plain, *refs):
+def arrange_kernel(owner, position, plain, here, ahead, across, behind, *refs):
     del owner, position
-    chosen, flats, messages = refs[:steps], refs[steps : steps + 2], refs[steps + 2 :]
+    flats, (own, up, down) = refs[:2], refs[2:]
     for j in range(2):
 
         @pl.when(pl.program_id(0) == j)
@@ -48,8 +50,14 @@
             for b in range(plain.shape[1]):
                 flats[j][b] = plain[:, b, 0, :, 0]
 
-    for k in range(steps):
-        messages[k][0, 0] = chosen[k][:, 0, 0, :, 0]
+    own[0, 0] = here[:, 0, 0, :, 0]
+    for e in range(2):
+
+        @pl.when(pl.program_id(1) == e)
+        def _(e=e):
+            up[e, 0] = ahead[:, 0, 0, :, 0]
+            down[e, 0] = behind[:, 0, 0, :, 0]
+            (up, down)[e][2, 0] = across[:, 0, 0, :, 0]
 
 
 def arrange(gathered, owner, position, n_x, n_core):
@@ -67,7 +75,7 @@
 
     out = (n_y, n_zh, width, tokens)
     return pl.pallas_call(
-        lambda *refs: arrange_kernel(n_x, *refs),
+        arrange_kernel,
         grid_spec=pltpu.PrefetchScalarGridSpec(
             num_scalar_prefetch=2,
             grid=(2, n_sh),
@@ -83,37 +91,117 @@
                 ),
                 pl.BlockSpec((n_sl,) + out, lambda j, h, *_: (jnp.where(j == 0, 0, h), 0, 0, 0, 0)),
             ]
-            + [pl.BlockSpec((1, 1) + out, lambda j, e, *_: (e, j, 0, 0, 0, 0))] * n_x,
+            + [pl.BlockSpec((1, 1) + out, lambda j, e, *_: (e, j, 0, 0, 0, 0))]
+            + [pl.BlockSpec((3, 1) + out, lambda j, e, *_: (0, j, 0, 0, 0, 0))] * 2,
         ),
         out_shape=[jax.ShapeDtypeStruct((n_blocks,) + out, gathered.dtype)] * 2
-        + [jax.ShapeDtypeStruct((n_core, 2) + out, gathered.dtype)] * n_x,
-        compiler_params=pltpu.CompilerParams(vmem_limit_bytes=24 * 1024 * 1024),
+        + [jax.ShapeDtypeStruct((n_core, 2) + out, gathered.dtype)]
+        + [jax.ShapeDtypeStruct((3, 2) + out, gathered.dtype)] * 2,
+        compiler_params=pltpu.CompilerParams(vmem_limit_bytes=VMEM),
         cost_estimate=pl.CostEstimate(
             flops=0, bytes_accessed=8 * gathered.size, transcendentals=0
         ),
     )(owner, position, gathered, *([gathered] * n_x))
 
 
-def collect_kernel(steps, *refs):
-    for k in range(steps):
+def collect_kernel(count, *refs):
+    for k in range(count):
         refs[-1][k, 0] = refs[k][0, 0]
 
 
-def collect(pieces, after):
-    steps = len(pieces)
+def collect(pieces, places, after):
+    count = len(pieces)
     rows, tokens = pieces[0].shape[2:]
     return pl.pallas_call(
-        lambda *refs: collect_kernel(steps, *refs),
+        lambda *refs: collect_kernel(count, *refs),
         grid=(2,),
-        in_specs=[pl.BlockSpec((1, 1, rows, tokens), lambda j: (1, j, 0, 0))] * steps
+        in_specs=[
+            pl.BlockSpec((1, 1, rows, tokens), lambda j, place=place: (place, j, 0, 0))
+            for place in places
+        ]
         + [pl.BlockSpec(memory_space=pl.ANY)],
-        out_specs=pl.BlockSpec((steps, 1, rows, tokens), lambda j: (0, j, 0, 0)),
-        out_shape=jax.ShapeDtypeStruct((steps, 2, rows, tokens), pieces[0].dtype),
-        compiler_params=pltpu.CompilerParams(vmem_limit_bytes=24 * 1024 * 1024),
+        out_specs=pl.BlockSpec((count, 1, rows, tokens), lambda j: (0, j, 0, 0)),
+        out_shape=jax.ShapeDtypeStruct((count, 2, rows, tokens), pieces[0].dtype),
+        compiler_params=pltpu.CompilerParams(vmem_limit_bytes=SMALL),
         cost_estimate=pl.CostEstimate(
-            flops=0, bytes_accessed=8 * steps * rows * tokens, transcendentals=0
+            flops=0, bytes_accessed=8 * count * rows * tokens, transcendentals=0
         ),
     )(*pieces, after)
+
+
+def middle_kernel(n_blocks, saved, grad, up, down, both, partial, pre, back, kept, turned):
+    step = pl.program_id(0)
+
+    @pl.when(step < n_blocks)
+    def _():
+        more = lax.dot_general(
+            saved[...], up[...], (((0,), (0,)), ((), ())), preferred_element_type=jnp.float32
+        )
+        extra = jnp.dot(down[...], grad[...], preferred_element_type=jnp.float32)
+        pre[...] = jnp.where(step == 0, 0.0, pre[...]) + more
+        back[...] = jnp.where(step == 0, 0.0, back[...]) + extra
+        kept[step] = up[...]
+
+    @pl.when(step == n_blocks - 1)
+    def _():
+        value, deriv = gelu_pair(pre[...])
+        dpre = (back[...].T * deriv).astype(jnp.bfloat16)
+        columns = dpre.shape[1]
+        both[:, :columns] = dpre
+        both[:, columns:] = value.astype(jnp.bfloat16)
+        turned[...] = dpre.T
+
+    @pl.when(step >= n_blocks)
+    def _():
+        rows = jnp.dot(kept[step - n_blocks], turned[...], preferred_element_type=jnp.float32)
+        shape = partial.shape
+        partial[:, 0, 0] = rows.astype(jnp.bfloat16).reshape(shape[0], *shape[3:])
+
+
+def middle(saved, grad, up_full, down_full, layout):
+    n_y, n_sl, n_sh, n_zh, width = layout
+    n_blocks = n_sl * n_sh
+    features, tokens = saved.shape
+    block = features // n_blocks
+    hidden_here = up_full.shape[1]
+
+    def first(i):
+        return jnp.minimum(i, n_blocks - 1)
+
+    def out_at(i):
+        b = jnp.maximum(i - n_blocks, 0)
+        return (0, lax.rem(b, n_sl), lax.div(b, n_sl), 0, 0, 0)
+
+    return pl.pallas_call(
+        lambda *refs: middle_kernel(n_blocks, *refs),
+        grid=(2 * n_blocks,),
+        in_specs=[
+            pl.BlockSpec((block, tokens), lambda i: (first(i), 0)),
+            pl.BlockSpec((block, tokens), lambda i: (first(i), 0)),
+            pl.BlockSpec((block, hidden_here), lambda i: (first(i), 0)),
+            pl.BlockSpec((hidden_here, block), lambda i: (0, first(i))),
+        ],
+        out_specs=[
+            pl.BlockSpec((tokens, 2 * hidden_here), lambda i: (0, 0)),
+            pl.BlockSpec((n_y, 1, 1, n_zh, width, tokens), out_at),
+        ],
+        out_shape=[
+            jax.ShapeDtypeStruct((tokens, 2 * hidden_here), jnp.bfloat16),
+            jax.ShapeDtypeStruct((n_y, n_sl, n_sh, n_zh, width, tokens), jnp.bfloat16),
+        ],
+        scratch_shapes=[
+            pltpu.VMEM((tokens, hidden_here), jnp.float32),
+            pltpu.VMEM((hidden_here, tokens), jnp.float32),
+            pltpu.VMEM((n_blocks, block, hidden_here), jnp.bfloat16),
+            pltpu.VMEM((hidden_here, tokens), jnp.bfloat16),
+        ],
+        compiler_params=pltpu.CompilerParams(vmem_limit_bytes=VMEM),
+        cost_estimate=pl.CostEstimate(
+            flops=6 * tokens * features * hidden_here,
+            bytes_accessed=4 * features * hidden_here + 6 * features * tokens,
+            transcendentals=tokens * hidden_here,
+        ),
+    )(saved, grad, up_full, down_full)
 
 
 def grads_kernel(steps, n_core, position, *refs):
@@ -146,7 +234,7 @@
             out_specs=pl.BlockSpec((1, 1, rows, hidden_here), lambda j, *_: (j, 0, 0, 0)),
         ),
         out_shape=jax.ShapeDtypeStruct((2, 1, rows, hidden_here), jnp.float32),
-        compiler_params=pltpu.CompilerParams(vmem_limit_bytes=32 * 1024 * 1024),
+        compiler_params=pltpu.CompilerParams(vmem_limit_bytes=SMALL),
         cost_estimate=pl.CostEstimate(
             flops=4 * rows * groups * tokens * hidden_here,
             bytes_accessed=4 * rows * groups * tokens + 16 * rows * hidden_here,
@@ -165,7 +253,6 @@
     n_zh = lax.axis_size("zh")
     tokens, width = cotangent.shape
     block = up_weight.shape[0]
-    hidden_here = up_weight.shape[1]
 
     up_full = lax.all_gather(up_weight, REP, axis=0, tiled=True)
     down_full = lax.all_gather(down_weight, REP, axis=1, tiled=True)
@@ -177,40 +264,37 @@
     full = full.reshape(n_y, n_sl, n_sh, n_zh, 2, width, tokens)
 
     position = jnp.stack([lax.axis_index("x"), lax.axis_index("core")])
-    inputs_flat, grads_flat, *messages = arrange(full, block_owner, position, n_x, n_core)
-    messages = [piece.reshape(n_core, 2, block, tokens) for piece in messages]
-    mine = [messages[0]] + [shift(messages[k], "x", k) for k in range(1, n_x)]
-
-    inputs_flat = inputs_flat.reshape(n_rep * block, tokens)
-    grads_flat = grads_flat.reshape(n_rep * block, tokens)
-    pre_act = lax.dot_general(
-        inputs_flat, up_full, (((0,), (0,)), ((), ())), preferred_element_type=jnp.float32
-    )
-    back_grad = lax.dot_general(
-        grads_flat, down_full, (((0,), (1,)), ((), ())), preferred_element_type=jnp.float32
-    )
-    value, deriv = gelu_pair(pre_act)
-    hidden = value.astype(jnp.bfloat16)
-    dpre = (back_grad * deriv).astype(jnp.bfloat16)
-
-    both = lax.all_gather(jnp.concatenate([dpre, hidden], axis=1), REP, axis=0, tiled=True)
-
-    partial_grad = lax.dot_general(
-        up_full, dpre, (((1,), (1,)), ((), ())), preferred_element_type=jnp.float32
-    ).astype(jnp.bfloat16)
-    partial_grad = partial_grad.reshape(n_sh, n_sl, n_y, n_zh, width, tokens)
-    partial_grad = partial_grad.transpose(2, 1, 0, 3, 4, 5)
+    inputs_flat, grads_flat, own, up, down = arrange(full, block_owner, position, n_x, n_core)
+    own, up, down = (
+        piece.reshape(piece.shape[0], 2, block, tokens) for piece in (own, up, down)
+    )
+    below = shift(up, "x", 1)
+    above = shift(down, "x", n_x - 1)
+
+    both, partial_grad = middle(
+        inputs_flat.reshape(n_rep * block, tokens),
+        grads_flat.reshape(n_rep * block, tokens),
+        up_full,
+        down_full,
+        (n_y, n_sl, n_sh, n_zh, width),
+    )
+    both = lax.all_gather(both, REP, axis=0, tiled=True)
+
     parts = lax.all_to_all(partial_grad, "y", split_axis=0, concat_axis=0, tiled=True)
     parts = jnp.sum(parts.astype(jnp.float32), axis=0).astype(jnp.bfloat16)
-    theirs = shift(collect(mine, parts), "core", 1)
+    across = shift(collect([below], [2], parts), "x", 1)
+    return_across = shift(collect([above], [2], parts), "x", n_x - 1)
     parts = lax.all_to_all(parts, "sl", split_axis=0, concat_axis=0, tiled=True)
     parts = jnp.sum(parts.astype(jnp.float32), axis=0).reshape(n_sh * n_zh, width, tokens)
+    theirs = collect([own, below, return_across, above], [1, 1, 0, 1], parts)
+    theirs = shift(theirs, "core", 1)
     parts = lax.all_to_all(parts, ("sh", "zh"), split_axis=0, concat_axis=0, tiled=True)
     summed = jnp.sum(parts, axis=0).T
     input_grads = (cotangent.astype(jnp.float32) + summed).astype(jnp.bfloat16)
 
+    mine = [own, below, across, above]
     weight_grads = block_grads(
-        mine, theirs, both.reshape(n_rep, tokens, 2 * hidden_here), position, n_core
+        mine, theirs, both.reshape(n_rep, tokens, -1), position, n_core
     )
     return (input_grads, weight_grads)
 

time: 206 us -> 233 us (1.13)
  the two profiles are of different devices: /device:TPU:42 before, /device:TPU:32 now
where the time goes in v4:
time: 233 us; the launch traced here: 232 us
  waiting for transfers between devices  87.8 us (38%)
  blocking collectives  49 us (21%)
  starting transfers between devices  40.8 us (18%)
  Pallas kernels  27.7 us (12%)
  between operations  13.8 us (6%)
  other arithmetic  7.24 us (3%)
  local copies, waits for them, and re-layouts  5.53 us (2%)
    all_to_all x1, waiting for transfers between devices, spread(): return lax.all_to_all(copies, axes, split_axis=0, concat_axis=0, tiled=True)  34.4 us
    all_to_all x1, blocking collectives, spread(): return lax.all_to_all(copies, axes, split_axis=0, concat_axis=0, tiled=True)  33.2 us
    ppermute x5, waiting for transfers between devices, shift(): lax.ppermute(block, axis, [(i, (i + step) % size) for i in range(size)])  22.3 us
    all_to_all x1, waiting for transfers between devices, body(): lax.all_to_all(parts, ('sh', 'zh'), split_axis=0, concat_axis=0, tiled=True)  17 us
    ppermute x5, starting transfers between devices, shift(): lax.ppermute(block, axis, [(i, (i + step) % size) for i in range(size)])  16.5 us
    all_gather x1, blocking collectives, body(): column = lax.all_gather(spaced, 'sl', axis=0, tiled=False)  15.8 us
    pallas_call x1, Pallas kernels, middle(): pl.pallas_call(lambda *refs: middle_kernel(n_blocks, *refs), grid=(2 * n_...  13.2 us
    all_to_all x1, waiting for transfers between devices, body(): lax.all_to_all(partial_grad, 'y', split_axis=0, concat_axis=0, tiled=True)  12.6 us
  transfers between devices with their start and end apart: 12, of which 4 were waited for; matrix products, arithmetic and copies ran while one was open for 4% of the time, Pallas kernels for 4%

profile of v4, /device:TPU:32, one launch (start us, length us, event | category | flops | bytes accessed | tf_op | source)
XLA Modules:
  0.0 231.8 jit_solution(15740264635097391156)
XLA Ops:
  7.2 0.0 all-gather.5.cloned.1.call-start
  7.2 0.7 all-gather.5.cloned.1.call-update
  7.9 0.0 all-gather.7.cloned.1.call-start
  7.9 0.7 all-gather.7.cloned.1.call-update
  8.6 0.8 pad_maximum_fusion
  9.4 33.2 %all_to_all.25 = bf16[4,2,96,128]{3,2,1,0:T(8,128)(2,1)S(1)} all-to-all(bf16[4,2,96,128]{3,2,1,0:T(8,128)(2,1)S(1)} %broadcast_in_dim.4), channel_id=1, replica_groups=mesh['x'=4,'core'=2,'sh'=2,'sl'=4,'y'=4,'zh'=2] {'sh','zh'}, dimensions={0} | all-to-all | bytes 393216 | tf_op jit(solution)/shard_map/all_to_all | solution.py:31
  42.6 15.8 %all-gather = bf16[16,2,96,128]{3,2,1,0:T(8,128)(2,1)S(1)} all-gather(bf16[4,2,96,128]{3,2,1,0:T(8,128)(2,1)S(1)} %all_to_all.25), channel_id=2, replica_groups=mesh['x'=4,'core'=2,'sh'=2,'sl'=4,'y'=4,'zh'=2] {'sl'}, dimensions={0}, use_global_device_ids=true | all-gather | bytes 983040 | tf_op jit(solution)/shard_map/all_gather | solution.py:262
  58.4 2.4 %broadcast_in_dim.5 = bf16[4,4,4,2,96,128]{5,4,3,2,1,0:T(8,128)(2,1)} broadcast(bf16[4,4,2,96,128]{4,3,2,1,0:T(8,128)(2,1)S(1)} %bitcast.29), dimensions={1,2,3,4,5} | broadcast | bytes 3932160 | tf_op jit(solution)/shard_map/broadcast_in_dim | solution.py:30
  60.9 4.5 %all-to-all-start.1 = ((bf16[4,4,4,2,96,128]{5,4,3,2,1,0:T(8,128)(2,1)}), bf16[4,4,4,2,96,128]{5,4,3,2,1,0:T(8,128)(2,1)S(1)}, u32[]{:S(2)}, u32[]{:S(2)}) async-start(bf16[4,4,4,2,96,128]{5,4,3,2,1,0:T(8,128)(2,1)} %broadcast_in_dim.5), calls=%async_computation.1 | async-start | bytes 6291456 | tf_op jit(solution)/shard_map/all_to_all | solution.py:31
  65.3 0.6 pad_add_fusion.position.refs_0_
  66.0 34.4 %all-to-all-done.1 = bf16[4,4,4,2,96,128]{5,4,3,2,1,0:T(8,128)(2,1)S(1)} async-done(((bf16[4,4,4,2,96,128]{5,4,3,2,1,0:T(8,128)(2,1)}), bf16[4,4,4,2,96,128]{5,4,3,2,1,0:T(8,128)(2,1)S(1)}, u32[]{:S(2)}, u32[]{:S(2)}) %all-to-all-start.1) | async-done | bytes 3145760 | tf_op jit(solution)/shard_map/all_to_all | solution.py:31
  100.4 0.0 copy-start.3
  100.4 1.7 copy-done.3
  102.1 6.8 %shard_map.68 = (bf16[8,4,2,96,128]{4,3,2,1,0:T(8,128)(2,1)}, bf16[8,4,2,96,128]{4,3,2,1,0:T(8,128)(2,1)}, bf16[2,2,4,2,96,128]{5,4,3,2,1,0:T(8,128)(2,1)}, bf16...) custom-call(s32[2,8]{1,0:T(2,128)} %owner.1, s32[2]{0:T(128)} %pad_add_fusion.position.refs_0_, ...), custom_call_target="tpu_custom_call" | custom-call | bytes 12582912 | tf_op jit(solution)/shard_map/pallas_call | solution.py:77
  108.9 0.0 all-gather.5.cloned.1.call-done.refs_2_
  108.9 0.0 all-gather.7.cloned.1.call-done.refs_3_
  108.9 13.2 %shard_map.69 = (bf16[128,768]{1,0:T(8,128)(2,1)}, bf16[4,4,2,2,96,128]{5,4,3,2,1,0:T(8,128)(2,1)}) custom-call(bf16[6144,128]{1,0:T(8,128)(2,1)} %bitcast.30, bf16[6144,128]{1,0:T(8,128)(2,1)} %bitcast.31, bf16[6144,384]{1,0:T(8,128)(2,1)} %all-gather.5.cloned.1.call-done.refs_2_, bf16[384,6144]{1,0:T(8,128)(2,1)} %all-gather.7.cloned.1.call-done.refs_3_), custom_call_target="tpu_custom_call" | custom-call | flops 1811939328 | bytes 14155776 | tf_op jit(solution)/shard_map/pallas_call | solution.py:175
  122.1 3.6 %all-to-all-start.2 = ((bf16[4,4,2,2,96,128]{5,4,3,2,1,0:T(8,128)(2,1)}), bf16[4,4,2,2,96,128]{5,4,3,2,1,0:T(8,128)(2,1)S(1)}, u32[]{:S(2)}, u32[]{:S(2)}) async-start(bf16[4,4,2,2,96,128]{5,4,3,2,1,0:T(8,128)(2,1)} %get-tuple-element.11), calls=%async_computation.2 | async-start | bytes 3145728 | tf_op jit(solution)/shard_map/all_to_all | solution.py:283
  125.7 4.7 %collective-permute-start.2 = (bf16[3,2,768,128]{3,2,1,0:T(8,128)(2,1)}, bf16[3,2,768,128]{3,2,1,0:T(8,128)(2,1)S(1)}, u32[]{:S(2)}, u32[]{:S(2)}) collective-permute-start(bf16[3,2,768,128]{3,2,1,0:T(8,128)(2,1)} %bitcast.35), channel_id=1, source_target_pairs={{0,384},{128,0},{256,128},{384,256},{1,385},{129,1},{257,129},{385... | collective-permute-start | bytes 3538952 | tf_op jit(solution)/shard_map/ppermute | solution.py:36
  130.4 12.6 %all-to-all-done.2 = bf16[4,4,2,2,96,128]{5,4,3,2,1,0:T(8,128)(2,1)S(1)} async-done(((bf16[4,4,2,2,96,128]{5,4,3,2,1,0:T(8,128)(2,1)}), bf16[4,4,2,2,96,128]{5,4,3,2,1,0:T(8,128)(2,1)S(1)}, u32[]{:S(2)}, u32[]{:S(2)}) %all-to-all-start.2) | async-done | bytes 1572896 | tf_op jit(solution)/shard_map/all_to_all | solution.py:283
  143.0 1.1 reduce_sum.30.refs_1_
  144.1 5.6 %all-to-all-start.3 = ((bf16[4,2,2,96,128]{4,3,2,1,0:T(8,128)(2,1)}), bf16[4,2,2,96,128]{4,3,2,1,0:T(8,128)(2,1)}, u32[]{:S(2)}, u32[]{:S(2)}) async-start(bf16[4,2,2,96,128]{4,3,2,1,0:T(8,128)(2,1)} %reduce_sum.30.refs_1_), calls=%async_computation.3 | async-start | bytes 786432 | tf_op jit(solution)/shard_map/all_to_all | solution.py:287
  149.7 0.0 copy-start
  149.7 0.0 all-gather.9.cloned.1.call-start
  149.7 3.4 %collective-permute-start = (bf16[3,2,768,128]{3,2,1,0:T(8,128)(2,1)}, bf16[3,2,768,128]{3,2,1,0:T(8,128)(2,1)S(1)}, u32[]{:S(2)}, u32[]{:S(2)}) collective-permute-start(bf16[3,2,768,128]{3,2,1,0:T(8,128)(2,1)} %bitcast.34), channel_id=1, source_target_pairs={{0,128},{128,256},{256,384},{384,0},{1,129},{129,257},{257,385},{3... | collective-permute-start | bytes 3538952 | tf_op jit(solution)/shard_map/ppermute | solution.py:36
  153.1 0.0 all-gather.9.cloned.1.call-update
  153.2 0.0 collective-permute-done.2.refs_0_.refs_3_.refs_4_
  153.2 0.1 shard_map.71
  153.3 4.5 %collective-permute-start.3 = (bf16[1,2,768,128]{3,2,1,0:T(8,128)(2,1)S(1)}, bf16[1,2,768,128]{3,2,1,0:T(8,128)(2,1)}, u32[]{:S(2)}, u32[]{:S(2)}) collective-permute-start(bf16[1,2,768,128]{3,2,1,0:T(8,128)(2,1)S(1)} %shard_map.71), channel_id=1, source_target_pairs={{0,384},{128,0},{256,128},{384,256},{1,385},{129,1},{257,129},{385... | collective-permute-start | bytes 1179656 | tf_op jit(solution)/shard_map/ppermute | solution.py:36
  157.8 0.0 all-to-all-done.3
  157.8 1.7 convert_reduce_fusion
  159.5 22.3 %collective-permute-done.refs_0_.refs_1_.refs_2_ = bf16[3,2,768,128]{3,2,1,0:T(8,128)(2,1)S(1)} collective-permute-done((bf16[3,2,768,128]{3,2,1,0:T(8,128)(2,1)}, bf16[3,2,768,128]{3,2,1,0:T(8,128)(2,1)S(1)}, u32[]{:S(2)}, u32[]{:S(2)}) %collective-permute-start) | collective-permute-done | bytes 1179680 | tf_op jit(solution)/shard_map/ppermute | solution.py:36
  181.9 0.0 collective-permute-done.3.refs_2_
  181.9 0.0 copy-done
  181.9 2.1 shard_map.72
  184.0 0.0 copy-start.2
  184.0 2.0 collective-permute-start.4
  186.0 10.5 %all-to-all-start.4 = ((f32[4,96,128]{2,1,0:T(8,128)}), f32[4,96,128]{2,1,0:T(8,128)}, u32[]{:S(2)}, u32[]{:S(2)}) async-start(f32[4,96,128]{2,1,0:T(8,128)} %bitcast.10.refs_4_), calls=%async_computation.4 | async-start | bytes 393216 | tf_op jit(solution)/shard_map/all_to_all | solution.py:291
  196.6 0.8 shard_map.70
  197.3 1.9 collective-permute-start.1
  199.2 17.0 %all-to-all-done.4 = f32[4,96,128]{2,1,0:T(8,128)} async-done(((f32[4,96,128]{2,1,0:T(8,128)}), f32[4,96,128]{2,1,0:T(8,128)}, u32[]{:S(2)}, u32[]{:S(2)}) %all-to-all-start.4) | async-done | bytes 196640 | tf_op jit(solution)/shard_map/all_to_all | solution.py:291
  216.2 1.6 reduce_sum.32
  217.8 1.4 fusion
  219.2 0.0 collective-permute-done.1.refs_3_
  219.2 0.0 all-gather.9.cloned.1.call-done
  219.2 0.0 collective-permute-done.4.refs_5_
  219.2 0.0 copy-done.2
  219.2 0.0 copy-start.1
  219.2 1.4 copy-done.1
  220.6 4.7 %shard_map.73 = f32[2,1,768,384]{3,2,1,0:T(8,128)} custom-call(s32[2]{0:T(128)S(1)} %copy-done.2, bf16[2,2,768,128]{3,2,1,0:T(8,128)(2,1)S(1)} %bitcast.22, bf16[3,2,768,128]{3,2,1,0:T(8,128)(2,1)S(1)} %collective-permute-done.refs_0_.refs_1_.refs_2_, bf16[1,2,768,128]{3,2,1,0:T(8,128)(2,1)S(1)} %collective-permute-done.1.refs_3_, ...), custom_call_target="tpu_custom_call" | custom-call | flops 1207959552 | bytes 7864320 | tf_op jit(solution)/shard_map/pallas_call | solution.py:224
  (1 shorter events, 0.0 us)
Async XLA Ops:
  7.2 101.8 %all-gather.5.cloned.1.call-start = ((), (), s32[]{:S(2)}) async-start(), calls=%async_computation.5 | async-start | bytes 5308416 | tf_op jit(solution)/shard_map/all_gather | solution.py:257
  7.9 101.0 %all-gather.7.cloned.1.call-start = ((), (), s32[]{:S(2)}) async-start(), calls=%async_computation.6 | async-start | bytes 5308416 | tf_op jit(solution)/shard_map/all_gather | solution.py:258
  60.9 39.5 %all-to-all-start.1 = ((bf16[4,4,4,2,96,128]{5,4,3,2,1,0:T(8,128)(2,1)}), bf16[4,4,4,2,96,128]{5,4,3,2,1,0:T(8,128)(2,1)S(1)}, u32[]{:S(2)}, u32[]{:S(2)}) async-start(bf16[4,4,4,2,96,128]{5,4,3,2,1,0:T(8,128)(2,1)} %broadcast_in_dim.5), calls=%async_computation.1 | async-start | bytes 6291456 | tf_op jit(solution)/shard_map/all_to_all | solution.py:31
  100.4 1.7 copy-start.3
  122.1 20.8 %all-to-all-start.2 = ((bf16[4,4,2,2,96,128]{5,4,3,2,1,0:T(8,128)(2,1)}), bf16[4,4,2,2,96,128]{5,4,3,2,1,0:T(8,128)(2,1)S(1)}, u32[]{:S(2)}, u32[]{:S(2)}) async-start(bf16[4,4,2,2,96,128]{5,4,3,2,1,0:T(8,128)(2,1)} %get-tuple-element.11), calls=%async_computation.2 | async-start | bytes 3145728 | tf_op jit(solution)/shard_map/all_to_all | solution.py:283
  125.7 27.5 %collective-permute-start.2 = (bf16[3,2,768,128]{3,2,1,0:T(8,128)(2,1)}, bf16[3,2,768,128]{3,2,1,0:T(8,128)(2,1)S(1)}, u32[]{:S(2)}, u32[]{:S(2)}) collective-permute-start(bf16[3,2,768,128]{3,2,1,0:T(8,128)(2,1)} %bitcast.35), channel_id=1, source_target_pairs={{0,384},{128,0},{256,128},{384,256},{1,385},{129,1},{257,129},{385... | collective-permute-start | bytes 3538952 | tf_op jit(solution)/shard_map/ppermute | solution.py:36
  144.1 13.7 %all-to-all-start.3 = ((bf16[4,2,2,96,128]{4,3,2,1,0:T(8,128)(2,1)}), bf16[4,2,2,96,128]{4,3,2,1,0:T(8,128)(2,1)}, u32[]{:S(2)}, u32[]{:S(2)}) async-start(bf16[4,2,2,96,128]{4,3,2,1,0:T(8,128)(2,1)} %reduce_sum.30.refs_1_), calls=%async_computation.3 | async-start | bytes 786432 | tf_op jit(solution)/shard_map/all_to_all | solution.py:287
  149.7 32.2 %copy-start = (bf16[2,2,4,2,96,128]{5,4,3,2,1,0:T(8,128)(2,1)S(1)}, bf16[2,2,4,2,96,128]{5,4,3,2,1,0:T(8,128)(2,1)}, u32[]{:S(2)}) copy-start(bf16[2,2,4,2,96,128]{5,4,3,2,1,0:T(8,128)(2,1)} %get-tuple-element.12) | copy-start | bytes 2359300
  149.7 69.5 %all-gather.9.cloned.1.call-start = ((), (), s32[]{:S(2)}) async-start(), calls=%async_computation.7 | async-start | bytes 1769472 | tf_op jit(solution)/shard_map/all_gather | solution.py:281
  149.7 32.1 %collective-permute-start = (bf16[3,2,768,128]{3,2,1,0:T(8,128)(2,1)}, bf16[3,2,768,128]{3,2,1,0:T(8,128)(2,1)S(1)}, u32[]{:S(2)}, u32[]{:S(2)}) collective-permute-start(bf16[3,2,768,128]{3,2,1,0:T(8,128)(2,1)} %bitcast.34), channel_id=1, source_target_pairs={{0,128},{128,256},{256,384},{384,0},{1,129},{129,257},{257,385},{3... | collective-permute-start | bytes 3538952 | tf_op jit(solution)/shard_map/ppermute | solution.py:36
  153.3 28.6 %collective-permute-start.3 = (bf16[1,2,768,128]{3,2,1,0:T(8,128)(2,1)S(1)}, bf16[1,2,768,128]{3,2,1,0:T(8,128)(2,1)}, u32[]{:S(2)}, u32[]{:S(2)}) collective-permute-start(bf16[1,2,768,128]{3,2,1,0:T(8,128)(2,1)S(1)} %shard_map.71), channel_id=1, source_target_pairs={{0,384},{128,0},{256,128},{384,256},{1,385},{129,1},{257,129},{385... | collective-permute-start | bytes 1179656 | tf_op jit(solution)/shard_map/ppermute | solution.py:36
  184.0 35.2 %copy-start.2 = (s32[2]{0:T(128)S(1)}, s32[2]{0:T(128)}, u32[]{:S(2)}) copy-start(s32[2]{0:T(128)} %pad_add_fusion.position.refs_0_) | copy-start | bytes 28
  184.0 35.2 %collective-permute-start.4 = (bf16[4,2,768,128]{3,2,1,0:T(8,128)(2,1)}, bf16[4,2,768,128]{3,2,1,0:T(8,128)(2,1)}, u32[]{:S(2)}, u32[]{:S(2)}) collective-permute-start(bf16[4,2,768,128]{3,2,1,0:T(8,128)(2,1)} %shard_map.72), channel_id=1, source_target_pairs={{0,64},{64,0},{1,65},{65,1},{2,66},{66,2},{3,67},{67,3},{4,68},{68... | collective-permute-start | bytes 4718600 | tf_op jit(solution)/shard_map/ppermute | solution.py:36
  186.0 30.2 %all-to-all-start.4 = ((f32[4,96,128]{2,1,0:T(8,128)}), f32[4,96,128]{2,1,0:T(8,128)}, u32[]{:S(2)}, u32[]{:S(2)}) async-start(f32[4,96,128]{2,1,0:T(8,128)} %bitcast.10.refs_4_), calls=%async_computation.4 | async-start | bytes 393216 | tf_op jit(solution)/shard_map/all_to_all | solution.py:291
  197.3 21.9 %collective-permute-start.1 = (bf16[1,2,768,128]{3,2,1,0:T(8,128)(2,1)}, bf16[1,2,768,128]{3,2,1,0:T(8,128)(2,1)S(1)}, u32[]{:S(2)}, u32[]{:S(2)}) collective-permute-start(bf16[1,2,768,128]{3,2,1,0:T(8,128)(2,1)} %shard_map.70), channel_id=1, source_target_pairs={{0,128},{128,256},{256,384},{384,0},{1,129},{129,257},{257,385},{3... | collective-permute-start | bytes 1179656 | tf_op jit(solution)/shard_map/ppermute | solution.py:36
  219.2 1.4 copy-start.1
Sparse Core Ops, SparseCore 0:
  10.1 46.0 all-gather.4
  58.3 42.0 all-gather.6
  153.3 27.1 all-gather.8

commit v5 on v2

v5 whole, which is shorter than its diff:
```python
import math

import jax
import jax.numpy as jnp
from jax import lax
from jax.experimental import pallas as pl
from jax.experimental.pallas import tpu as pltpu
from jax.sharding import Mesh
from jax.sharding import PartitionSpec as P

GELU_SCALE = math.sqrt(2.0 / math.pi)
GELU_CUBIC = 0.044715

REP = ("x", "core")
SHARD = ("sh", "sl", "y", "zh")
SMALL = 24 * 1024 * 1024
LARGE = 60 * 1024 * 1024


def gelu_pair(values):
    tanh_part = jnp.tanh(GELU_SCALE * (values + GELU_CUBIC * values * values * values))
    value = 0.5 * values * (1.0 + tanh_part)
    deriv = 0.5 * (1.0 + tanh_part) + 0.5 * values * (1.0 - tanh_part * tanh_part) * GELU_SCALE * (
        1.0 + 3.0 * GELU_CUBIC * values * values
    )
    return value, deriv


def spread(block, axes, count):
    copies = lax.optimization_barrier(jnp.broadcast_to(block[None], (count,) + block.shape))
    return lax.all_to_all(copies, axes, split_axis=0, concat_axis=0, tiled=True)


def arrange_kernel(owner, plain, *refs):
    del owner
    count = plain.shape[1]
    chosen, (first, second, message) = refs[:count], refs[-3:]
    for j, flat in enumerate((first, second)):

        @pl.when(pl.program_id(0) == j)
        def _(flat=flat):
            for b in range(count):
                flat[b] = plain[:, b, 0, :, 0]

    for k in range(count):
        message[k, 0] = chosen[k][:, 0, 0, :, 0]


def arrange(gathered, owner, after):
    n_y, n_sl, n_sh, n_zh, _, width, tokens = gathered.shape
    n_blocks = n_sl * n_sh
    piece = (n_y, 1, 1, n_zh, 1, width, tokens)

    def chosen_at(k):
        def index(j, h, owner):
            target = h * n_sl + k
            b = sum(jnp.where(owner[j, i] == target, i, 0) for i in range(n_blocks))
            return (0, lax.rem(b, n_sl), lax.div(b, n_sl), 0, j, 0, 0)

        return index

    out = (n_y, n_zh, width, tokens)
    return pl.pallas_call(
        arrange_kernel,
        grid_spec=pltpu.PrefetchScalarGridSpec(
            num_scalar_prefetch=1,
            grid=(2, n_sh),
            in_specs=[
                pl.BlockSpec(
                    (n_y, n_sl, 1, n_zh, 1, width, tokens), lambda j, h, _: (0, 0, h, 0, j, 0, 0)
                )
            ]
            + [pl.BlockSpec(piece, chosen_at(k)) for k in range(n_sl)]
            + [pl.BlockSpec(memory_space=pl.ANY)] * len(after),
            out_specs=[
                pl.BlockSpec(
                    (n_sl,) + out, lambda j, h, _: (jnp.where(j == 0, h, n_sh - 1), 0, 0, 0, 0)
                ),
                pl.BlockSpec((n_sl,) + out, lambda j, h, _: (jnp.where(j == 0, 0, h), 0, 0, 0, 0)),
                pl.BlockSpec((n_sl, 1) + out, lambda j, h, _: (h, j, 0, 0, 0, 0)),
            ],
        ),
        out_shape=[jax.ShapeDtypeStruct((n_blocks,) + out, gathered.dtype)] * 2
        + [jax.ShapeDtypeStruct((n_blocks, 2) + out, gathered.dtype)],
        compiler_params=pltpu.CompilerParams(vmem_limit_bytes=SMALL),
        cost_estimate=pl.CostEstimate(
            flops=0, bytes_accessed=8 * gathered.size, transcendentals=0
        ),
    )(owner, gathered, *([gathered] * n_sl), *after)


def share_kernel(mine, up, dpre, *refs):
    outs, rows = refs[:-1], refs[-1]
    n_y = rows.shape[0]
    product = lax.dot_general(
        up[...], dpre[...], (((1,), (1,)), ((), ())), preferred_element_type=jnp.float32
    )
    rows[...] = product.astype(rows.dtype).reshape(rows.shape)
    for k in range(n_y):
        outs[k][0, 0] = rows[lax.rem(mine[0] + k, n_y)]


def share(up_full, dpre, mine, layout):
    n_y, n_sl, n_sh, n_zh, width = layout
    n_blocks = n_sl * n_sh
    tokens, hidden_here = dpre.shape
    block = up_full.shape[0] // n_blocks
    return pl.pallas_call(
        share_kernel,
        grid_spec=pltpu.PrefetchScalarGridSpec(
            num_scalar_prefetch=1,
            grid=(n_blocks,),
            in_specs=[
                pl.BlockSpec((block, hidden_here), lambda i, _: (i, 0)),
                pl.BlockSpec((tokens, hidden_here), lambda i, _: (0, 0)),
            ],
            out_specs=[
                pl.BlockSpec(
                    (1, 1, n_zh, width, tokens),
                    lambda i, _: (lax.rem(i, n_sl), lax.div(i, n_sl), 0, 0, 0),
                )
            ]
            * n_y,
            scratch_shapes=[pltpu.VMEM((n_y, n_zh, width, tokens), jnp.bfloat16)],
        ),
        out_shape=[jax.ShapeDtypeStruct((n_sl, n_sh, n_zh, width, tokens), jnp.bfloat16)] * n_y,
        compiler_params=pltpu.CompilerParams(vmem_limit_bytes=LARGE),
        cost_estimate=pl.CostEstimate(
            flops=2 * tokens * hidden_here * block * n_blocks,
            bytes_accessed=2 * block * n_blocks * (hidden_here + tokens),
            transcendentals=0,
        ),
    )(mine, up_full, dpre)


def fold_kernel(count, mine, *refs):
    terms = refs[:count]
    size = terms[0].shape[0]
    outs = refs[-size:]
    for k in range(size):
        at = lax.rem(mine[0] + k, size)
        total = terms[0][at].astype(jnp.float32)
        for term in terms[1:]:
            total = total + term[at].astype(jnp.float32)
        outs[k][...] = total.astype(outs[k].dtype)


def fold(terms, mine, kind, after=()):
    size, *rest = terms[0].shape
    return pl.pallas_call(
        lambda *refs: fold_kernel(len(terms), *refs),
        grid_spec=pltpu.PrefetchScalarGridSpec(
            num_scalar_prefetch=1,
            grid=(1,),
            in_specs=[pl.BlockSpec((size, *rest), lambda i, _: (0,) * (len(rest) + 1))] * len(terms)
            + [pl.BlockSpec(memory_space=pl.ANY)] * len(after),
            out_specs=[pl.BlockSpec(tuple(rest), lambda i, _: (0,) * len(rest))] * size,
        ),
        out_shape=[jax.ShapeDtypeStruct(tuple(rest), kind)] * size,
        compiler_params=pltpu.CompilerParams(vmem_limit_bytes=SMALL),
    )(mine, *terms, *after)


def grads_kernel(pieces, both, out):
    total = None
    for r in range(0, pieces.shape[0], 2):
        left = jnp.concatenate([pieces[r, 0], pieces[r + 1, 0]], axis=1)
        right = jnp.concatenate([both[r], both[r + 1]], axis=0)
        term = jnp.dot(left, right, preferred_element_type=jnp.float32)
        total = term if total is None else total + term
    out[0, 0] = total


def block_grads(pieces, both):
    groups, _, rows, tokens = pieces.shape
    hidden_here = both.shape[2] // 2
    return pl.pallas_call(
        grads_kernel,
        grid=(2,),
        in_specs=[
            pl.BlockSpec((groups, 1, rows, tokens), lambda j: (0, j, 0, 0)),
            pl.BlockSpec((groups, tokens, hidden_here), lambda j: (0, 0, j)),
        ],
        out_specs=pl.BlockSpec((1, 1, rows, hidden_here), lambda j: (j, 0, 0, 0)),
        out_shape=jax.ShapeDtypeStruct((2, 1, rows, hidden_here), jnp.float32),
        compiler_params=pltpu.CompilerParams(vmem_limit_bytes=SMALL),
        cost_estimate=pl.CostEstimate(
            flops=4 * rows * groups * tokens * hidden_here,
            bytes_accessed=4 * rows * groups * tokens + 16 * rows * hidden_here,
            transcendentals=0,
        ),
    )(pieces, both)


def trade(steps, axes):
    size = lax.axis_size(axes)
    return [steps[0]] + [
        lax.ppermute(steps[k], axes, [(i, (i + k) % size) for i in range(size)])
        for k in range(1, size)
    ]


def place(axes):
    return jnp.reshape(lax.axis_index(axes), (1,))


def body(cotangent, saved_inputs, up_weight, down_weight, block_owner):
    n_x = lax.axis_size("x")
    n_core = lax.axis_size("core")
    n_rep = n_x * n_core
    n_sh = lax.axis_size("sh")
    n_sl = lax.axis_size("sl")
    n_y = lax.axis_size("y")
    n_zh = lax.axis_size("zh")
    tokens, width = cotangent.shape
    block = up_weight.shape[0]

    up_full = lax.all_gather(up_weight, REP, axis=0, tiled=True)
    down_full = lax.all_gather(down_weight, REP, axis=1, tiled=True)

    pair = jnp.stack([saved_inputs.T, cotangent.T])
    spaced = spread(pair, ("sh", "zh"), n_sh * n_zh)
    column = lax.all_gather(spaced, "sl", axis=0, tiled=False)
    full = spread(column, "y", n_y)
    full = full.reshape(n_y, n_sl, n_sh, n_zh, 2, width, tokens)

    inputs_flat, grads_flat, message = arrange(
        full, block_owner, (up_full[:16, :128], down_full[:16, :128])
    )
    message = message.reshape(n_rep, 2, block, tokens)
    owned = lax.all_to_all(message, REP, split_axis=0, concat_axis=0, tiled=True)

    inputs_flat = inputs_flat.reshape(n_rep * block, tokens)
    grads_flat = grads_flat.reshape(n_rep * block, tokens)
    pre_act = lax.dot_general(
        inputs_flat, up_full, (((0,), (0,)), ((), ())), preferred_element_type=jnp.float32
    )
    back_grad = lax.dot_general(
        grads_flat, down_full, (((0,), (1,)), ((), ())), preferred_element_type=jnp.float32
    )
    value, deriv = gelu_pair(pre_act)
    hidden = value.astype(jnp.bfloat16)
    dpre = (back_grad * deriv).astype(jnp.bfloat16)

    both = lax.all_gather(jnp.concatenate([dpre, hidden], axis=1), REP, axis=0, tiled=True)

    layout = (n_y, n_sl, n_sh, n_zh, width)
    parts = trade(share(up_full, dpre, place("y"), layout), "y")
    parts = trade(fold(parts, place("sl"), jnp.bfloat16), "sl")
    parts = [p.reshape(n_sh * n_zh, width, tokens) for p in parts]
    parts = trade(fold(parts, place(("sh", "zh")), jnp.float32, (owned,)), ("sh", "zh"))
    summed = sum(parts[1:], parts[0]).T
    input_grads = (cotangent.astype(jnp.float32) + summed).astype(jnp.bfloat16)

    weight_grads = block_grads(owned, both.reshape(n_rep, tokens, -1))
    return (input_grads, weight_grads)


def solution(mesh):
    fine = Mesh(mesh.devices.reshape(4, 2, 2, 4, 4, 2), ("x", "core", "sh", "sl", "y", "zh"))
    in_specs = (
        P(REP, SHARD),
        P(REP, SHARD),
        P(REP, SHARD),
        P(SHARD, REP),
        P(),
    )
    out_specs = (P(REP, SHARD), P(None, REP, None, SHARD))
    return jax.shard_map(body, mesh=fine, in_specs=in_specs, out_specs=out_specs, check_vma=False)
```

time: 209 us -> 211 us (level)
  the two profiles are of different devices: /device:TPU:1 before, /device:TPU:12 now
where the time goes in v5:
time: 211 us; the launch traced here: 210 us
  waiting for transfers between devices  60.1 us (28%)
  blocking collectives  51.2 us (24%)
  starting transfers between devices  49.1 us (23%)
  Pallas kernels  16.1 us (8%)
  between operations  13.9 us (7%)
  local copies, waits for them, and re-layouts  12.3 us (6%)
  matrix products  5.56 us (3%)
  other arithmetic  2.12 us (1%)
    ppermute x9, starting transfers between devices, trade(): lax.ppermute(steps[k], axes, [(i, (i + k) % size) for i in range(size)])  39.1 us
    all_to_all x1, blocking collectives, spread(): return lax.all_to_all(copies, axes, split_axis=0, concat_axis=0, tiled=True)  31.7 us
    all_gather x1, waiting for transfers between devices, body(): down_full = lax.all_gather(down_weight, REP, axis=1, tiled=True)  30.6 us
    ppermute x9, waiting for transfers between devices, trade(): lax.ppermute(steps[k], axes, [(i, (i + k) % size) for i in range(size)])  27.6 us
    all_gather x1, blocking collectives, body(): column = lax.all_gather(spaced, 'sl', axis=0, tiled=False)  19.5 us
    unnamed x24, local copies, waits for them, and re-layouts  8.51 us
    pallas_call x1, Pallas kernels, share(): pl.pallas_call(share_kernel, grid_spec=pltpu.PrefetchScalarGridSpec(num_s...  7.29 us
    all_to_all x1, starting transfers between devices, spread(): return lax.all_to_all(copies, axes, split_axis=0, concat_axis=0, tiled=True)  5.04 us
  transfers between devices with their start and end apart: 14, of which 9 were waited for; matrix products, arithmetic and copies ran while one was open for 5% of the time, Pallas kernels for 6%

profile of v5, /device:TPU:12, one launch (start us, length us, event | category | flops | bytes accessed | tf_op | source)
XLA Modules:
  0.0 210.4 jit_solution(8173743473333013995)
XLA Ops:
  7.2 0.0 all-gather.5.cloned.1.call-start
  7.2 0.7 all-gather.5.cloned.1.call-update
  7.9 0.0 all-gather.7.cloned.1.call-start
  7.9 0.7 all-gather.7.cloned.1.call-update
  8.6 0.8 pad_maximum_fusion.1
  9.4 31.7 %all_to_all.15 = bf16[4,2,96,128]{3,2,1,0:T(8,128)(2,1)S(1)} all-to-all(bf16[4,2,96,128]{3,2,1,0:T(8,128)(2,1)S(1)} %broadcast_in_dim.4), channel_id=1, replica_groups=mesh['x'=4,'core'=2,'sh'=2,'sl'=4,'y'=4,'zh'=2] {'sh','zh'}, dimensions={0} | all-to-all | bytes 393216 | tf_op jit(solution)/shard_map/all_to_all | solution.py:31
  41.1 19.5 %all-gather = bf16[16,2,96,128]{3,2,1,0:T(8,128)(2,1)S(1)} all-gather(bf16[4,2,96,128]{3,2,1,0:T(8,128)(2,1)S(1)} %all_to_all.15), channel_id=2, replica_groups=mesh['x'=4,'core'=2,'sh'=2,'sl'=4,'y'=4,'zh'=2] {'sl'}, dimensions={0}, use_global_device_ids=true | all-gather | bytes 983040 | tf_op jit(solution)/shard_map/all_gather | solution.py:223
  60.6 2.4 %broadcast_in_dim.5 = bf16[4,4,4,2,96,128]{5,4,3,2,1,0:T(8,128)(2,1)} broadcast(bf16[4,4,2,96,128]{4,3,2,1,0:T(8,128)(2,1)S(1)} %bitcast.40), dimensions={1,2,3,4,5} | broadcast | bytes 3932160 | tf_op jit(solution)/shard_map/broadcast_in_dim | solution.py:30
  63.1 0.0 copy-start.8
  63.1 5.0 %all-to-all-start.1 = ((bf16[4,4,4,2,96,128]{5,4,3,2,1,0:T(8,128)(2,1)}), bf16[4,4,4,2,96,128]{5,4,3,2,1,0:T(8,128)(2,1)S(1)}, u32[]{:S(2)}, u32[]{:S(2)}) async-start(bf16[4,4,4,2,96,128]{5,4,3,2,1,0:T(8,128)(2,1)} %broadcast_in_dim.5), calls=%async_computation.1 | async-start | bytes 6291456 | tf_op jit(solution)/shard_map/all_to_all | solution.py:31
  68.1 0.0 all-gather.5.cloned.1.call-done.up
  68.1 0.7 slice.8.refs_4_
  68.8 30.6 %all-gather.7.cloned.1.call-done = bf16[384,6144]{1,0:T(8,128)(2,1)} async-done(((bf16[384,768]{1,0:T(8,128)(2,1)}), bf16[384,6144]{1,0:T(8,128)(2,1)}) %all-gather.7.cloned.1.call-update) | async-done | bytes 4718608 | tf_op jit(solution)/shard_map/all_gather | solution.py:219
  99.4 0.7 slice.9.refs_5_
  100.1 0.5 all-to-all-done.1
  100.5 0.0 copy-done.8
  100.5 2.8 %shard_map.68 = (bf16[8,4,2,96,128]{4,3,2,1,0:T(8,128)(2,1)S(1)}, bf16[8,4,2,96,128]{4,3,2,1,0:T(8,128)(2,1)S(1)}, bf16[8,2,4,2,96,128]{5,4,3,2,1,0:T(8,128)(2,1)S(1)}) custom-call(s32[2,8]{1,0:T(2,128)S(1)} %copy-done.8, bf16[4,4,2,2,2,96,128]{6,5,4,3,2,1,0:T(8,128)(2,1)S(1)} %bitcast.27, bf16[4,4,2,2,2,96,128]{6,5,4,3,2,1,0:T(8,128)(2,1)S(1)} %bitcast.28, ...), custom_call_target="tpu_custom_call" | custom-call | bytes 12582912 | tf_op jit(solution)/shard_map/pallas_call | solution.py:63
  103.4 0.0 copy-start
  103.4 1.7 copy-done
  105.1 0.0 copy-start.2
  105.1 1.1 copy-done.2
  106.2 0.0 copy-start.4
  106.2 1.1 copy-done.4
  107.3 4.9 %all-to-all-start.2 = ((bf16[8,2,768,128]{3,2,1,0:T(8,128)(2,1)}), bf16[8,2,768,128]{3,2,1,0:T(8,128)(2,1)S(1)}, u32[]{:S(2)}, u32[]{:S(2)}) async-start(bf16[8,2,768,128]{3,2,1,0:T(8,128)(2,1)} %bitcast.32), calls=%async_computation.2 | async-start | bytes 6291456 | tf_op jit(solution)/shard_map/all_to_all | solution.py:231
  112.3 0.0 all-gather.9.cloned.1.call-start
  112.3 4.0 %multiply_convert_fusion = (bf16[128,384]{1,0:T(8,128)(2,1)S(1)}, f32[128,384]{1,0:T(8,128)S(1)}) fusion(bf16[6144,128]{1,0:T(8,128)(2,1)} %bitcast.35, bf16[6144,384]{1,0:T(8,128)(2,1)} %all-gather.5.cloned.1.call-done.up), kind=kOutput, calls=%fused_computation.10 | convolution fusion | flops 604422144 | bytes 6586368 | tf_op jit(solution)/shard_map/dot_general | solution.py:235
  116.3 0.0 copy-done.3
  116.3 0.6 copy-done.9
  116.9 1.5 fusion.dpre
  118.5 0.0 copy-start.10
  118.5 0.7 pad_maximum_fusion
  119.2 0.0 all-gather.9.cloned.1.call-update
  119.2 0.0 copy-done.10
  119.3 7.3 %shard_map.69 = (bf16[4,2,2,96,128]{4,3,2,1,0:T(8,128)(2,1)}, bf16[4,2,2,96,128]{4,3,2,1,0:T(8,128)(2,1)}, bf16[4,2,2,96,128]{4,3,2,1,0:T(8,128)(2,1)}, bf16[4,2,2,96,128]{4,3,2,1,0:T(8,128)(2,1)}) custom-call(s32[1]{0:T(128)} %bitcast.2.mine, bf16[6144,384]{1,0:T(8,128)(2,1)} %all-gather.5.cloned.1.call-done.up, bf16[128,384]{1,0:T(8,128)(2,1)} %copy-done.10), custom_call_target="tpu_custom_call" | custom-call | flops 603979776 | bytes 6291456 | tf_op jit(solution)/shard_map/pallas_call | solution.py:108
  126.5 3.4 %collective-permute-start = (bf16[4,2,2,96,128]{4,3,2,1,0:T(8,128)(2,1)}, bf16[4,2,2,96,128]{4,3,2,1,0:T(8,128)(2,1)S(1)}, u32[]{:S(2)}, u32[]{:S(2)}) collective-permute-start(bf16[4,2,2,96,128]{4,3,2,1,0:T(8,128)(2,1)} %get-tuple-element.20), channel_id=1, source_target_pairs={{0,2},{2,4},{4,6},{6,0},{1,3},{3,5},{5,7},{7,1},{8,10},{10,12},{12... | collective-permute-start | bytes 1179656 | tf_op jit(solution)/shard_map/ppermute | solution.py:198
  130.0 3.8 %collective-permute-start.1 = (bf16[4,2,2,96,128]{4,3,2,1,0:T(8,128)(2,1)}, bf16[4,2,2,96,128]{4,3,2,1,0:T(8,128)(2,1)}, u32[]{:S(2)}, u32[]{:S(2)}) collective-permute-start(bf16[4,2,2,96,128]{4,3,2,1,0:T(8,128)(2,1)} %get-tuple-element.21), channel_id=1, source_target_pairs={{0,4},{2,6},{4,0},{6,2},{1,5},{3,7},{5,1},{7,3},{8,12},{10,14},{12... | collective-permute-start | bytes 1179656 | tf_op jit(solution)/shard_map/ppermute | solution.py:198
  133.8 3.3 %collective-permute-start.2 = (bf16[4,2,2,96,128]{4,3,2,1,0:T(8,128)(2,1)}, bf16[4,2,2,96,128]{4,3,2,1,0:T(8,128)(2,1)}, u32[]{:S(2)}, u32[]{:S(2)}) collective-permute-start(bf16[4,2,2,96,128]{4,3,2,1,0:T(8,128)(2,1)} %get-tuple-element.22), channel_id=1, source_target_pairs={{0,6},{2,0},{4,2},{6,4},{1,7},{3,1},{5,3},{7,5},{8,14},{10,8},{12,... | collective-permute-start | bytes 1179656 | tf_op jit(solution)/shard_map/ppermute | solution.py:198
  137.1 3.5 %collective-permute-done.refs_2_ = bf16[4,2,2,96,128]{4,3,2,1,0:T(8,128)(2,1)S(1)} collective-permute-done((bf16[4,2,2,96,128]{4,3,2,1,0:T(8,128)(2,1)}, bf16[4,2,2,96,128]{4,3,2,1,0:T(8,128)(2,1)S(1)}, u32[]{:S(2)}, u32[]{:S(2)}) %collective-permute-start) | collective-permute-done | bytes 393248 | tf_op jit(solution)/shard_map/ppermute | solution.py:198
  140.6 5.1 %collective-permute-done.1.refs_3_ = bf16[4,2,2,96,128]{4,3,2,1,0:T(8,128)(2,1)} collective-permute-done((bf16[4,2,2,96,128]{4,3,2,1,0:T(8,128)(2,1)}, bf16[4,2,2,96,128]{4,3,2,1,0:T(8,128)(2,1)}, u32[]{:S(2)}, u32[]{:S(2)}) %collective-permute-start.1) | collective-permute-done | bytes 393248 | tf_op jit(solution)/shard_map/ppermute | solution.py:198
  145.7 7.3 %collective-permute-done.2.refs_4_ = bf16[4,2,2,96,128]{4,3,2,1,0:T(8,128)(2,1)} collective-permute-done((bf16[4,2,2,96,128]{4,3,2,1,0:T(8,128)(2,1)}, bf16[4,2,2,96,128]{4,3,2,1,0:T(8,128)(2,1)}, u32[]{:S(2)}, u32[]{:S(2)}) %collective-permute-start.2) | collective-permute-done | bytes 393248 | tf_op jit(solution)/shard_map/ppermute | solution.py:198
  153.0 1.0 copy-done.5
  154.0 1.9 shard_map.70
  155.9 0.6 copy-done.6
  156.6 3.5 %collective-permute-start.3 = (bf16[2,2,96,128]{3,2,1,0:T(8,128)(2,1)}, bf16[2,2,96,128]{3,2,1,0:T(8,128)(2,1)S(1)}, u32[]{:S(2)}, u32[]{:S(2)}) collective-permute-start(bf16[2,2,96,128]{3,2,1,0:T(8,128)(2,1)} %get-tuple-element.24), channel_id=1, source_target_pairs={{0,8},{8,16},{16,24},{24,0},{1,9},{9,17},{17,25},{25,1},{2,10},{10... | collective-permute-start | bytes 294920 | tf_op jit(solution)/shard_map/ppermute | solution.py:198
  160.0 4.4 %collective-permute-start.4 = (bf16[2,2,96,128]{3,2,1,0:T(8,128)(2,1)}, bf16[2,2,96,128]{3,2,1,0:T(8,128)(2,1)S(1)}, u32[]{:S(2)}, u32[]{:S(2)}) collective-permute-start(bf16[2,2,96,128]{3,2,1,0:T(8,128)(2,1)} %get-tuple-element.25), channel_id=1, source_target_pairs={{0,16},{8,24},{16,0},{24,8},{1,17},{9,25},{17,1},{25,9},{2,18},{10... | collective-permute-start | bytes 294920 | tf_op jit(solution)/shard_map/ppermute | solution.py:198
  164.5 3.3 %collective-permute-start.5 = (bf16[2,2,96,128]{3,2,1,0:T(8,128)(2,1)}, bf16[2,2,96,128]{3,2,1,0:T(8,128)(2,1)S(1)}, u32[]{:S(2)}, u32[]{:S(2)}) collective-permute-start(bf16[2,2,96,128]{3,2,1,0:T(8,128)(2,1)} %get-tuple-element.26), channel_id=1, source_target_pairs={{0,24},{8,0},{16,8},{24,16},{1,25},{9,1},{17,9},{25,17},{2,26},{10... | collective-permute-start | bytes 294920 | tf_op jit(solution)/shard_map/ppermute | solution.py:198
  167.8 0.0 collective-permute-done.3
  167.8 2.8 %collective-permute-done.4 = bf16[2,2,96,128]{3,2,1,0:T(8,128)(2,1)S(1)} collective-permute-done((bf16[2,2,96,128]{3,2,1,0:T(8,128)(2,1)}, bf16[2,2,96,128]{3,2,1,0:T(8,128)(2,1)S(1)}, u32[]{:S(2)}, u32[]{:S(2)}) %collective-permute-start.4) | collective-permute-done | bytes 98336 | tf_op jit(solution)/shard_map/ppermute | solution.py:198
  170.5 1.1 collective-permute-done.5
  171.7 0.0 all-to-all-done.2.refs_5_.pieces
  171.7 0.9 copy-done.7
  172.6 0.7 shard_map.71
  173.2 12.5 %collective-permute-start.6 = (f32[96,128]{1,0:T(8,128)}, f32[96,128]{1,0:T(8,128)S(1)}, u32[]{:S(2)}, u32[]{:S(2)}) collective-permute-start(f32[96,128]{1,0:T(8,128)} %get-tuple-element.29), channel_id=1, source_target_pairs={{0,1},{1,32},{32,33},{33,0},{2,3},{3,34},{34,35},{35,2},{4,5},{5,3... | collective-permute-start | bytes 147464 | tf_op jit(solution)/shard_map/ppermute | solution.py:198
  185.7 2.8 %collective-permute-start.7 = (f32[96,128]{1,0:T(8,128)}, f32[96,128]{1,0:T(8,128)S(1)}, u32[]{:S(2)}, u32[]{:S(2)}) collective-permute-start(f32[96,128]{1,0:T(8,128)} %get-tuple-element.30), channel_id=1, source_target_pairs={{0,32},{1,33},{32,0},{33,1},{2,34},{3,35},{34,2},{35,3},{4,36},{5,... | collective-permute-start | bytes 147464 | tf_op jit(solution)/shard_map/ppermute | solution.py:198
  188.5 2.1 collective-permute-start.8
  190.6 0.0 all-gather.9.cloned.1.call-done
  190.6 0.0 copy-start.1
  190.7 1.4 copy-done.1
  192.1 3.4 %shard_map.72 = f32[2,1,768,384]{3,2,1,0:T(8,128)} custom-call(bf16[8,2,768,128]{3,2,1,0:T(8,128)(2,1)S(1)} %all-to-all-done.2.refs_5_.pieces, bf16[8,128,768]{2,1,0:T(8,128)(2,1)S(1)} %bitcast.33), custom_call_target="tpu_custom_call" | custom-call | flops 1207959552 | bytes 7864320 | tf_op jit(solution)/shard_map/pallas_call | solution.py:177
  195.4 0.0 collective-permute-done.6
  195.4 1.8 collective-permute-done.7
  197.2 6.1 %collective-permute-done.8 = f32[96,128]{1,0:T(8,128)S(1)} collective-permute-done((f32[96,128]{1,0:T(8,128)S(1)}, f32[96,128]{1,0:T(8,128)S(1)}, u32[]{:S(2)}, u32[]{:S(2)}) %collective-permute-start.8) | collective-permute-done | bytes 49184 | tf_op jit(solution)/shard_map/ppermute | solution.py:198
  203.2 0.0 copy-done.11
  203.2 0.6 fusion.6
  (7 shorter events, 0.0 us)
Async XLA Ops:
  7.2 61.0 %all-gather.5.cloned.1.call-start = ((), (), s32[]{:S(2)}) async-start(), calls=%async_computation.3 | async-start | bytes 5308416 | tf_op jit(solution)/shard_map/all_gather | solution.py:218
  7.9 91.5 %all-gather.7.cloned.1.call-start = ((), (), s32[]{:S(2)}) async-start(), calls=%async_computation.4 | async-start | bytes 5308416 | tf_op jit(solution)/shard_map/all_gather | solution.py:219
  63.1 37.5 %copy-start.8 = (s32[2,8]{1,0:T(2,128)S(1)}, s32[2,8]{1,0:T(2,128)}, u32[]{:S(2)}) copy-start(s32[2,8]{1,0:T(2,128)} %owner.1) | copy-start | bytes 196
  63.1 37.5 %all-to-all-start.1 = ((bf16[4,4,4,2,96,128]{5,4,3,2,1,0:T(8,128)(2,1)}), bf16[4,4,4,2,96,128]{5,4,3,2,1,0:T(8,128)(2,1)S(1)}, u32[]{:S(2)}, u32[]{:S(2)}) async-start(bf16[4,4,4,2,96,128]{5,4,3,2,1,0:T(8,128)(2,1)} %broadcast_in_dim.5), calls=%async_computation.1 | async-start | bytes 6291456 | tf_op jit(solution)/shard_map/all_to_all | solution.py:31
  103.4 1.7 copy-start
  105.1 1.1 copy-start.2
  106.2 1.1 copy-start.4
  107.3 64.3 %all-to-all-start.2 = ((bf16[8,2,768,128]{3,2,1,0:T(8,128)(2,1)}), bf16[8,2,768,128]{3,2,1,0:T(8,128)(2,1)S(1)}, u32[]{:S(2)}, u32[]{:S(2)}) async-start(bf16[8,2,768,128]{3,2,1,0:T(8,128)(2,1)} %bitcast.32), calls=%async_computation.2 | async-start | bytes 6291456 | tf_op jit(solution)/shard_map/all_to_all | solution.py:231
  112.3 78.4 %all-gather.9.cloned.1.call-start = ((), (), s32[]{:S(2)}) async-start(), calls=%async_computation.5 | async-start | bytes 1769472 | tf_op jit(solution)/shard_map/all_gather | solution.py:245
  112.3 4.0 %copy-start.3 = (bf16[8,4,2,96,128]{4,3,2,1,0:T(8,128)(2,1)S(1)}, bf16[8,4,2,96,128]{4,3,2,1,0:T(8,128)(2,1)}, u32[]{:S(2)}) copy-start(bf16[8,4,2,96,128]{4,3,2,1,0:T(8,128)(2,1)} %copy-done.2) | copy-start | bytes 4718596
  112.3 4.7 %copy-start.9 = (bf16[384,6144]{1,0:T(8,128)(2,1)S(1)}, bf16[384,6144]{1,0:T(8,128)(2,1)}, u32[]{:S(2)}) copy-start(bf16[384,6144]{1,0:T(8,128)(2,1)} %all-gather.7.cloned.1.call-done) | copy-start | bytes 14155780
  118.5 0.8 copy-start.10
  126.5 14.1 %collective-permute-start = (bf16[4,2,2,96,128]{4,3,2,1,0:T(8,128)(2,1)}, bf16[4,2,2,96,128]{4,3,2,1,0:T(8,128)(2,1)S(1)}, u32[]{:S(2)}, u32[]{:S(2)}) collective-permute-start(bf16[4,2,2,96,128]{4,3,2,1,0:T(8,128)(2,1)} %get-tuple-element.20), channel_id=1, source_target_pairs={{0,2},{2,4},{4,6},{6,0},{1,3},{3,5},{5,7},{7,1},{8,10},{10,12},{12... | collective-permute-start | bytes 1179656 | tf_op jit(solution)/shard_map/ppermute | solution.py:198
  130.0 15.8 %collective-permute-start.1 = (bf16[4,2,2,96,128]{4,3,2,1,0:T(8,128)(2,1)}, bf16[4,2,2,96,128]{4,3,2,1,0:T(8,128)(2,1)}, u32[]{:S(2)}, u32[]{:S(2)}) collective-permute-start(bf16[4,2,2,96,128]{4,3,2,1,0:T(8,128)(2,1)} %get-tuple-element.21), channel_id=1, source_target_pairs={{0,4},{2,6},{4,0},{6,2},{1,5},{3,7},{5,1},{7,3},{8,12},{10,14},{12... | collective-permute-start | bytes 1179656 | tf_op jit(solution)/shard_map/ppermute | solution.py:198
  133.8 19.2 %collective-permute-start.2 = (bf16[4,2,2,96,128]{4,3,2,1,0:T(8,128)(2,1)}, bf16[4,2,2,96,128]{4,3,2,1,0:T(8,128)(2,1)}, u32[]{:S(2)}, u32[]{:S(2)}) collective-permute-start(bf16[4,2,2,96,128]{4,3,2,1,0:T(8,128)(2,1)} %get-tuple-element.22), channel_id=1, source_target_pairs={{0,6},{2,0},{4,2},{6,4},{1,7},{3,1},{5,3},{7,5},{8,14},{10,8},{12,... | collective-permute-start | bytes 1179656 | tf_op jit(solution)/shard_map/ppermute | solution.py:198
  153.0 1.0 copy-start.5
  155.9 0.6 copy-start.6
  156.6 11.2 %collective-permute-start.3 = (bf16[2,2,96,128]{3,2,1,0:T(8,128)(2,1)}, bf16[2,2,96,128]{3,2,1,0:T(8,128)(2,1)S(1)}, u32[]{:S(2)}, u32[]{:S(2)}) collective-permute-start(bf16[2,2,96,128]{3,2,1,0:T(8,128)(2,1)} %get-tuple-element.24), channel_id=1, source_target_pairs={{0,8},{8,16},{16,24},{24,0},{1,9},{9,17},{17,25},{25,1},{2,10},{10... | collective-permute-start | bytes 294920 | tf_op jit(solution)/shard_map/ppermute | solution.py:198
  160.0 10.5 %collective-permute-start.4 = (bf16[2,2,96,128]{3,2,1,0:T(8,128)(2,1)}, bf16[2,2,96,128]{3,2,1,0:T(8,128)(2,1)S(1)}, u32[]{:S(2)}, u32[]{:S(2)}) collective-permute-start(bf16[2,2,96,128]{3,2,1,0:T(8,128)(2,1)} %get-tuple-element.25), channel_id=1, source_target_pairs={{0,16},{8,24},{16,0},{24,8},{1,17},{9,25},{17,1},{25,9},{2,18},{10... | collective-permute-start | bytes 294920 | tf_op jit(solution)/shard_map/ppermute | solution.py:198
  164.5 7.2 %collective-permute-start.5 = (bf16[2,2,96,128]{3,2,1,0:T(8,128)(2,1)}, bf16[2,2,96,128]{3,2,1,0:T(8,128)(2,1)S(1)}, u32[]{:S(2)}, u32[]{:S(2)}) collective-permute-start(bf16[2,2,96,128]{3,2,1,0:T(8,128)(2,1)} %get-tuple-element.26), channel_id=1, source_target_pairs={{0,24},{8,0},{16,8},{24,16},{1,25},{9,1},{17,9},{25,17},{2,26},{10... | collective-permute-start | bytes 294920 | tf_op jit(solution)/shard_map/ppermute | solution.py:198
  171.7 0.9 copy-start.7
  173.2 22.2 %collective-permute-start.6 = (f32[96,128]{1,0:T(8,128)}, f32[96,128]{1,0:T(8,128)S(1)}, u32[]{:S(2)}, u32[]{:S(2)}) collective-permute-start(f32[96,128]{1,0:T(8,128)} %get-tuple-element.29), channel_id=1, source_target_pairs={{0,1},{1,32},{32,33},{33,0},{2,3},{3,34},{34,35},{35,2},{4,5},{5,3... | collective-permute-start | bytes 147464 | tf_op jit(solution)/shard_map/ppermute | solution.py:198
  185.7 11.5 %collective-permute-start.7 = (f32[96,128]{1,0:T(8,128)}, f32[96,128]{1,0:T(8,128)S(1)}, u32[]{:S(2)}, u32[]{:S(2)}) collective-permute-start(f32[96,128]{1,0:T(8,128)} %get-tuple-element.30), channel_id=1, source_target_pairs={{0,32},{1,33},{32,0},{33,1},{2,34},{3,35},{34,2},{35,3},{4,36},{5,... | collective-permute-start | bytes 147464 | tf_op jit(solution)/shard_map/ppermute | solution.py:198
  188.5 14.7 %collective-permute-start.8 = (f32[96,128]{1,0:T(8,128)S(1)}, f32[96,128]{1,0:T(8,128)S(1)}, u32[]{:S(2)}, u32[]{:S(2)}) collective-permute-start(f32[96,128]{1,0:T(8,128)S(1)} %get-tuple-element.31), channel_id=1, source_target_pairs={{0,33},{1,0},{32,1},{33,32},{2,35},{3,2},{34,3},{35,34},{4,37},{5,... | collective-permute-start | bytes 147464 | tf_op jit(solution)/shard_map/ppermute | solution.py:198
  190.6 1.4 copy-start.1
  192.1 11.2 %copy-start.11 = (bf16[128,96]{0,1:T(8,128)(2,1)S(1)}, bf16[128,96]{0,1:T(8,128)(2,1)}, u32[]{:S(2)}) copy-start(bf16[128,96]{0,1:T(8,128)(2,1)} %param.5) | copy-start | bytes 73732
Sparse Core Ops, SparseCore 0:
  10.1 45.0 all-gather.4
  57.3 42.0 all-gather.6
  119.4 35.8 all-gather.8

commit v6 on v5

--- a/solution.py
+++ b/solution.py
@@ -14,7 +14,6 @@
 REP = ("x", "core")
 SHARD = ("sh", "sl", "y", "zh")
 SMALL = 24 * 1024 * 1024
-LARGE = 60 * 1024 * 1024
 
 
 def gelu_pair(values):
@@ -89,76 +88,54 @@
     )(owner, gathered, *([gathered] * n_sl), *after)
 
 
-def share_kernel(mine, up, dpre, *refs):
-    outs, rows = refs[:-1], refs[-1]
-    n_y = rows.shape[0]
-    product = lax.dot_general(
-        up[...], dpre[...], (((1,), (1,)), ((), ())), preferred_element_type=jnp.float32
-    )
-    rows[...] = product.astype(rows.dtype).reshape(rows.shape)
-    for k in range(n_y):
-        outs[k][0, 0] = rows[lax.rem(mine[0] + k, n_y)]
-
-
-def share(up_full, dpre, mine, layout):
-    n_y, n_sl, n_sh, n_zh, width = layout
-    n_blocks = n_sl * n_sh
-    tokens, hidden_here = dpre.shape
-    block = up_full.shape[0] // n_blocks
-    return pl.pallas_call(
-        share_kernel,
+def cut_kernel(mine, *refs):
+    del mine
+    count = len(refs) // 2
+    for k in range(count):
+        refs[count + k][...] = refs[k][:, 0]
+
+
+def cut(rows, mine):
+    n_blocks, n_y, *rest = rows.shape
+    zeros = (0,) * len(rest)
+    return pl.pallas_call(
+        cut_kernel,
         grid_spec=pltpu.PrefetchScalarGridSpec(
             num_scalar_prefetch=1,
-            grid=(n_blocks,),
+            grid=(2,),
             in_specs=[
-                pl.BlockSpec((block, hidden_here), lambda i, _: (i, 0)),
-                pl.BlockSpec((tokens, hidden_here), lambda i, _: (0, 0)),
+                pl.BlockSpec(
+                    (n_blocks // 2, 1, *rest),
+                    lambda i, mine, k=k: (i, lax.rem(mine[0] + k, n_y), *zeros),
+                )
+                for k in range(n_y)
             ],
-            out_specs=[
-                pl.BlockSpec(
-                    (1, 1, n_zh, width, tokens),
-                    lambda i, _: (lax.rem(i, n_sl), lax.div(i, n_sl), 0, 0, 0),
-                )
-            ]
-            * n_y,
-            scratch_shapes=[pltpu.VMEM((n_y, n_zh, width, tokens), jnp.bfloat16)],
-        ),
-        out_shape=[jax.ShapeDtypeStruct((n_sl, n_sh, n_zh, width, tokens), jnp.bfloat16)] * n_y,
-        compiler_params=pltpu.CompilerParams(vmem_limit_bytes=LARGE),
-        cost_estimate=pl.CostEstimate(
-            flops=2 * tokens * hidden_here * block * n_blocks,
-            bytes_accessed=2 * block * n_blocks * (hidden_here + tokens),
-            transcendentals=0,
-        ),
-    )(mine, up_full, dpre)
-
-
-def fold_kernel(count, mine, *refs):
-    terms = refs[:count]
-    size = terms[0].shape[0]
-    outs = refs[-size:]
-    for k in range(size):
-        at = lax.rem(mine[0] + k, size)
-        total = terms[0][at].astype(jnp.float32)
-        for term in terms[1:]:
-            total = total + term[at].astype(jnp.float32)
-        outs[k][...] = total.astype(outs[k].dtype)
-
-
-def fold(terms, mine, kind, after=()):
-    size, *rest = terms[0].shape
-    return pl.pallas_call(
-        lambda *refs: fold_kernel(len(terms), *refs),
-        grid_spec=pltpu.PrefetchScalarGridSpec(
-            num_scalar_prefetch=1,
-            grid=(1,),
-            in_specs=[pl.BlockSpec((size, *rest), lambda i, _: (0,) * (len(rest) + 1))] * len(terms)
-            + [pl.BlockSpec(memory_space=pl.ANY)] * len(after),
-            out_specs=[pl.BlockSpec(tuple(rest), lambda i, _: (0,) * len(rest))] * size,
-        ),
-        out_shape=[jax.ShapeDtypeStruct(tuple(rest), kind)] * size,
-        compiler_params=pltpu.CompilerParams(vmem_limit_bytes=SMALL),
-    )(mine, *terms, *after)
+            out_specs=[pl.BlockSpec((n_blocks // 2, *rest), lambda i, _: (i, *zeros))] * n_y,
+        ),
+        out_shape=[jax.ShapeDtypeStruct((n_blocks, *rest), rows.dtype)] * n_y,
+        compiler_params=pltpu.CompilerParams(vmem_limit_bytes=SMALL),
+    )(mine, *([rows] * n_y))
+
+
+def total_kernel(count, *refs):
+    total = refs[0][...].astype(jnp.float32)
+    for term in refs[1:count]:
+        total = total + term[...].astype(jnp.float32)
+    refs[-1][...] = total.astype(refs[-1].dtype)
+
+
+def total(terms, after):
+    shape = terms[0].shape
+    half = (shape[0] // 2, *shape[1:])
+    spec = pl.BlockSpec(half, lambda i: (i,) + (0,) * (len(shape) - 1))
+    return pl.pallas_call(
+        lambda *refs: total_kernel(len(terms), *refs),
+        grid=(2,),
+        in_specs=[spec] * len(terms) + [pl.BlockSpec(memory_space=pl.ANY)],
+        out_specs=spec,
+        out_shape=jax.ShapeDtypeStruct(shape, terms[0].dtype),
+        compiler_params=pltpu.CompilerParams(vmem_limit_bytes=SMALL),
+    )(*terms, after)
 
 
 def grads_kernel(pieces, both, out):
@@ -244,12 +221,13 @@
 
     both = lax.all_gather(jnp.concatenate([dpre, hidden], axis=1), REP, axis=0, tiled=True)
 
-    layout = (n_y, n_sl, n_sh, n_zh, width)
-    parts = trade(share(up_full, dpre, place("y"), layout), "y")
-    parts = trade(fold(parts, place("sl"), jnp.bfloat16), "sl")
-    parts = [p.reshape(n_sh * n_zh, width, tokens) for p in parts]
-    parts = trade(fold(parts, place(("sh", "zh")), jnp.float32, (owned,)), ("sh", "zh"))
-    summed = sum(parts[1:], parts[0]).T
+    partial_grad = lax.dot_general(
+        up_full, dpre, (((1,), (1,)), ((), ())), preferred_element_type=jnp.float32
+    ).astype(jnp.bfloat16)
+    parts = cut(partial_grad.reshape(n_rep, n_y, n_zh, width, tokens), place("y"))
+    parts = total(trade(parts, "y"), owned).reshape(n_rep * n_zh, width, tokens)
+    parts = lax.all_to_all(parts, ("sh", "sl", "zh"), split_axis=0, concat_axis=0, tiled=True)
+    summed = jnp.sum(parts.astype(jnp.float32), axis=0).T
     input_grads = (cotangent.astype(jnp.float32) + summed).astype(jnp.bfloat16)
 
     weight_grads = block_grads(owned, both.reshape(n_rep, tokens, -1))

time: 211 us -> 205 us (0.972)
  the two profiles are of different devices: /device:TPU:12 before, /device:TPU:32 now
where the time goes in v6:
time: 205 us; the launch traced here: 204 us
  waiting for transfers between devices  77.7 us (38%)
  blocking collectives  49 us (24%)
  starting transfers between devices  33.3 us (16%)
  between operations  13.9 us (7%)
  local copies, waits for them, and re-layouts  10.7 us (5%)
  matrix products  9.01 us (4%)
  Pallas kernels  8.52 us (4%)
  other arithmetic  2.14 us (1%)
    all_gather x1, waiting for transfers between devices, body(): down_full = lax.all_gather(down_weight, REP, axis=1, tiled=True)  34.3 us
    all_to_all x1, blocking collectives, spread(): return lax.all_to_all(copies, axes, split_axis=0, concat_axis=0, tiled=True)  33.2 us
    all_to_all x1, waiting for transfers between devices, body(): lax.all_to_all(parts, ('sh', 'sl', 'zh'), split_axis=0, concat_axis=0, ti...  20.4 us
    all_gather x1, blocking collectives, body(): column = lax.all_gather(spaced, 'sl', axis=0, tiled=False)  15.8 us
    ppermute x3, waiting for transfers between devices, trade(): lax.ppermute(steps[k], axes, [(i, (i + k) % size) for i in range(size)])  14 us
    all_to_all x1, starting transfers between devices, body(): lax.all_to_all(parts, ('sh', 'sl', 'zh'), split_axis=0, concat_axis=0, ti...  12.7 us
    ppermute x3, starting transfers between devices, trade(): lax.ppermute(steps[k], axes, [(i, (i + k) % size) for i in range(size)])  11.4 us
    all_to_all x1, waiting for transfers between devices, body(): lax.all_to_all(message, REP, split_axis=0, concat_axis=0, tiled=True)  7.53 us
  transfers between devices with their start and end apart: 9, of which 6 were waited for; matrix products, arithmetic and copies ran while one was open for 7% of the time, Pallas kernels for 3%

profile of v6, /device:TPU:32, one launch (start us, length us, event | category | flops | bytes accessed | tf_op | source)
XLA Modules:
  0.0 204.3 jit_solution(10102534361631004941)
XLA Ops:
  7.2 0.0 all-gather.5.cloned.1.call-start
  7.2 0.7 all-gather.5.cloned.1.call-update
  7.9 0.0 all-gather.7.cloned.1.call-start
  7.9 0.7 all-gather.7.cloned.1.call-update
  8.6 0.8 pad_maximum_fusion.1
  9.4 33.2 %all_to_all.20 = bf16[4,2,96,128]{3,2,1,0:T(8,128)(2,1)S(1)} all-to-all(bf16[4,2,96,128]{3,2,1,0:T(8,128)(2,1)S(1)} %broadcast_in_dim.4), channel_id=1, replica_groups=mesh['x'=4,'core'=2,'sh'=2,'sl'=4,'y'=4,'zh'=2] {'sh','zh'}, dimensions={0} | all-to-all | bytes 393216 | tf_op jit(solution)/shard_map/all_to_all | solution.py:30
  42.6 15.8 %all-gather = bf16[16,2,96,128]{3,2,1,0:T(8,128)(2,1)S(1)} all-gather(bf16[4,2,96,128]{3,2,1,0:T(8,128)(2,1)S(1)} %all_to_all.20), channel_id=2, replica_groups=mesh['x'=4,'core'=2,'sh'=2,'sl'=4,'y'=4,'zh'=2] {'sl'}, dimensions={0}, use_global_device_ids=true | all-gather | bytes 983040 | tf_op jit(solution)/shard_map/all_gather | solution.py:200
  58.4 2.4 %broadcast_in_dim.5 = bf16[4,4,4,2,96,128]{5,4,3,2,1,0:T(8,128)(2,1)} broadcast(bf16[4,4,2,96,128]{4,3,2,1,0:T(8,128)(2,1)S(1)} %bitcast.40), dimensions={1,2,3,4,5} | broadcast | bytes 3932160 | tf_op jit(solution)/shard_map/broadcast_in_dim | solution.py:29
  60.8 0.0 copy-start.6
  60.9 4.6 %all-to-all-start.1 = ((bf16[4,4,4,2,96,128]{5,4,3,2,1,0:T(8,128)(2,1)}), bf16[4,4,4,2,96,128]{5,4,3,2,1,0:T(8,128)(2,1)S(1)}, u32[]{:S(2)}, u32[]{:S(2)}) async-start(bf16[4,4,4,2,96,128]{5,4,3,2,1,0:T(8,128)(2,1)} %broadcast_in_dim.5), calls=%async_computation.1 | async-start | bytes 6291456 | tf_op jit(solution)/shard_map/all_to_all | solution.py:30
  65.4 0.0 all-gather.5.cloned.1.call-done
  65.4 0.7 slice.8.refs_4_
  66.1 34.3 %all-gather.7.cloned.1.call-done = bf16[384,6144]{1,0:T(8,128)(2,1)} async-done(((bf16[384,768]{1,0:T(8,128)(2,1)}), bf16[384,6144]{1,0:T(8,128)(2,1)}) %all-gather.7.cloned.1.call-update) | async-done | bytes 4718608 | tf_op jit(solution)/shard_map/all_gather | solution.py:196
  100.4 0.7 slice.9.refs_5_
  101.1 0.0 all-to-all-done.1
  101.1 0.0 copy-done.6
  101.1 2.8 %shard_map.68 = (bf16[8,4,2,96,128]{4,3,2,1,0:T(8,128)(2,1)S(1)}, bf16[8,4,2,96,128]{4,3,2,1,0:T(8,128)(2,1)S(1)}, bf16[8,2,4,2,96,128]{5,4,3,2,1,0:T(8,128)(2,1)S(1)}) custom-call(s32[2,8]{1,0:T(2,128)S(1)} %copy-done.6, bf16[4,4,2,2,2,96,128]{6,5,4,3,2,1,0:T(8,128)(2,1)S(1)} %bitcast.27, bf16[4,4,2,2,2,96,128]{6,5,4,3,2,1,0:T(8,128)(2,1)S(1)} %bitcast.28, ...), custom_call_target="tpu_custom_call" | custom-call | bytes 12582912 | tf_op jit(solution)/shard_map/pallas_call | solution.py:62
  104.0 0.0 copy-start
  104.0 1.6 copy-done
  105.6 0.0 copy-start.2
  105.6 1.1 copy-done.2
  106.7 0.0 copy-start.4
  106.7 1.1 copy-done.4
  107.9 0.0 copy-start.5
  107.9 4.6 %all-to-all-start.2 = ((bf16[8,2,768,128]{3,2,1,0:T(8,128)(2,1)}), bf16[8,2,768,128]{3,2,1,0:T(8,128)(2,1)}, u32[]{:S(2)}, u32[]{:S(2)}) async-start(bf16[8,2,768,128]{3,2,1,0:T(8,128)(2,1)} %bitcast.36), calls=%async_computation.2 | async-start | bytes 6291456 | tf_op jit(solution)/shard_map/all_to_all | solution.py:208
  112.5 0.0 all-gather.9.cloned.1.call-start
  112.5 0.0 copy-done.5
  112.5 0.0 copy-start.3
  112.6 0.0 copy-start.7
  112.6 3.5 %multiply_convert_fusion = (bf16[128,384]{1,0:T(8,128)(2,1)S(1)}, f32[128,384]{1,0:T(8,128)S(1)}) fusion(bf16[6144,128]{1,0:T(8,128)(2,1)S(1)} %bitcast.39, bf16[6144,384]{1,0:T(8,128)(2,1)} %all-gather.5.cloned.1.call-done), kind=kOutput, calls=%fused_computation.13 | convolution fusion | flops 604422144 | bytes 6586368 | tf_op jit(solution)/shard_map/dot_general | solution.py:212
  116.1 0.0 copy-done.3
  116.1 0.7 copy-done.7
  116.8 1.5 fusion.1
  118.3 0.7 pad_maximum_fusion
  119.0 0.0 all-gather.9.cloned.1.call-update
  119.1 3.9 %fusion = bf16[6144,128]{0,1:T(8,128)(2,1)S(1)} fusion(bf16[128,384]{1,0:T(8,128)(2,1)S(1)} %fusion.1, bf16[6144,384]{1,0:T(8,128)(2,1)} %all-gather.5.cloned.1.call-done), kind=kOutput, calls=%fused_computation.1 | convolution fusion | flops 604766208 | bytes 6389760 | tf_op jit(solution)/shard_map/dot_general | solution.py:224
  123.0 0.9 copy.8
  123.9 0.4 shard_map.69
  124.3 3.4 %collective-permute-start = (bf16[8,2,96,128]{3,2,1,0:T(8,128)(2,1)S(1)}, bf16[8,2,96,128]{3,2,1,0:T(8,128)(2,1)S(1)}, u32[]{:S(2)}, u32[]{:S(2)}) collective-permute-start(bf16[8,2,96,128]{3,2,1,0:T(8,128)(2,1)S(1)} %get-tuple-element.12), channel_id=1, source_target_pairs={{0,2},{2,4},{4,6},{6,0},{1,3},{3,5},{5,7},{7,1},{8,10},{10,12},{12... | collective-permute-start | bytes 1179656 | tf_op jit(solution)/shard_map/ppermute | solution.py:175
  127.7 4.6 %collective-permute-start.1 = (bf16[8,2,96,128]{3,2,1,0:T(8,128)(2,1)S(1)}, bf16[8,2,96,128]{3,2,1,0:T(8,128)(2,1)S(1)}, u32[]{:S(2)}, u32[]{:S(2)}) collective-permute-start(bf16[8,2,96,128]{3,2,1,0:T(8,128)(2,1)S(1)} %get-tuple-element.13), channel_id=1, source_target_pairs={{0,4},{2,6},{4,0},{6,2},{1,5},{3,7},{5,1},{7,3},{8,12},{10,14},{12... | collective-permute-start | bytes 1179656 | tf_op jit(solution)/shard_map/ppermute | solution.py:175
  132.3 3.3 %collective-permute-start.2 = (bf16[8,2,96,128]{3,2,1,0:T(8,128)(2,1)S(1)}, bf16[8,2,96,128]{3,2,1,0:T(8,128)(2,1)S(1)}, u32[]{:S(2)}, u32[]{:S(2)}) collective-permute-start(bf16[8,2,96,128]{3,2,1,0:T(8,128)(2,1)S(1)} %get-tuple-element.14), channel_id=1, source_target_pairs={{0,6},{2,0},{4,2},{6,4},{1,7},{3,1},{5,3},{7,5},{8,14},{10,8},{12,... | collective-permute-start | bytes 1179656 | tf_op jit(solution)/shard_map/ppermute | solution.py:175
  135.7 3.1 %collective-permute-done.refs_1_ = bf16[8,2,96,128]{3,2,1,0:T(8,128)(2,1)S(1)} collective-permute-done((bf16[8,2,96,128]{3,2,1,0:T(8,128)(2,1)S(1)}, bf16[8,2,96,128]{3,2,1,0:T(8,128)(2,1)S(1)}, u32[]{:S(2)}, u32[]{:S(2)}) %collective-permute-start) | collective-permute-done | bytes 393248 | tf_op jit(solution)/shard_map/ppermute | solution.py:175
  138.7 9.4 %collective-permute-done.1.refs_2_ = bf16[8,2,96,128]{3,2,1,0:T(8,128)(2,1)S(1)} collective-permute-done((bf16[8,2,96,128]{3,2,1,0:T(8,128)(2,1)S(1)}, bf16[8,2,96,128]{3,2,1,0:T(8,128)(2,1)S(1)}, u32[]{:S(2)}, u32[]{:S(2)}) %collective-permute-start.1) | collective-permute-done | bytes 393248 | tf_op jit(solution)/shard_map/ppermute | solution.py:175
  148.1 1.6 collective-permute-done.2.refs_3_
  149.7 7.5 %all-to-all-done.2.refs_4_.pieces = bf16[8,2,768,128]{3,2,1,0:T(8,128)(2,1)} async-done(((bf16[8,2,768,128]{3,2,1,0:T(8,128)(2,1)}), bf16[8,2,768,128]{3,2,1,0:T(8,128)(2,1)}, u32[]{:S(2)}, u32[]{:S(2)}) %all-to-all-start.2) | async-done | bytes 3145760 | tf_op jit(solution)/shard_map/all_to_all | solution.py:208
  157.2 0.9 shard_map.70
  158.1 12.7 %all-to-all-start.3 = ((bf16[16,96,128]{2,1,0:T(8,128)(2,1)}), bf16[16,96,128]{2,1,0:T(8,128)(2,1)S(1)}, u32[]{:S(2)}, u32[]{:S(2)}) async-start(bf16[16,96,128]{2,1,0:T(8,128)(2,1)} %bitcast.12), calls=%async_computation.3 | async-start | bytes 786432 | tf_op jit(solution)/shard_map/all_to_all | solution.py:229
  170.8 0.0 all-gather.9.cloned.1.call-done
  170.8 0.0 copy-start.1
  170.8 1.4 copy-done.1
  172.2 0.0 copy-start.8
  172.2 4.4 %shard_map.71 = f32[2,1,768,384]{3,2,1,0:T(8,128)} custom-call(bf16[8,2,768,128]{3,2,1,0:T(8,128)(2,1)} %all-to-all-done.2.refs_4_.pieces, bf16[8,128,768]{2,1,0:T(8,128)(2,1)S(1)} %bitcast.37), custom_call_target="tpu_custom_call" | custom-call | flops 1207959552 | bytes 7864320 | tf_op jit(solution)/shard_map/pallas_call | solution.py:154
  176.6 20.4 %all-to-all-done.3 = bf16[16,96,128]{2,1,0:T(8,128)(2,1)S(1)} async-done(((bf16[16,96,128]{2,1,0:T(8,128)(2,1)}), bf16[16,96,128]{2,1,0:T(8,128)(2,1)S(1)}, u32[]{:S(2)}, u32[]{:S(2)}) %all-to-all-start.3) | async-done | bytes 393248 | tf_op jit(solution)/shard_map/all_to_all | solution.py:229
  197.1 0.1 convert_reduce_fusion
  197.1 0.0 copy-done.8
  197.1 0.6 fusion.7
  (1 shorter events, 0.0 us)
Async XLA Ops:
  7.2 58.3 %all-gather.5.cloned.1.call-start = ((), (), s32[]{:S(2)}) async-start(), calls=%async_computation.4 | async-start | bytes 5308416 | tf_op jit(solution)/shard_map/all_gather | solution.py:195
  7.9 92.5 %all-gather.7.cloned.1.call-start = ((), (), s32[]{:S(2)}) async-start(), calls=%async_computation.5 | async-start | bytes 5308416 | tf_op jit(solution)/shard_map/all_gather | solution.py:196
  60.8 40.2 %copy-start.6 = (s32[2,8]{1,0:T(2,128)S(1)}, s32[2,8]{1,0:T(2,128)}, u32[]{:S(2)}) copy-start(s32[2,8]{1,0:T(2,128)} %owner.1) | copy-start | bytes 196
  60.9 40.2 %all-to-all-start.1 = ((bf16[4,4,4,2,96,128]{5,4,3,2,1,0:T(8,128)(2,1)}), bf16[4,4,4,2,96,128]{5,4,3,2,1,0:T(8,128)(2,1)S(1)}, u32[]{:S(2)}, u32[]{:S(2)}) async-start(bf16[4,4,4,2,96,128]{5,4,3,2,1,0:T(8,128)(2,1)} %broadcast_in_dim.5), calls=%async_computation.1 | async-start | bytes 6291456 | tf_op jit(solution)/shard_map/all_to_all | solution.py:30
  104.0 1.7 copy-start
  105.6 1.1 copy-start.2
  106.7 1.1 copy-start.4
  107.9 4.7 %copy-start.5 = (bf16[8,4,2,96,128]{4,3,2,1,0:T(8,128)(2,1)S(1)}, bf16[8,4,2,96,128]{4,3,2,1,0:T(8,128)(2,1)}, u32[]{:S(2)}) copy-start(bf16[8,4,2,96,128]{4,3,2,1,0:T(8,128)(2,1)} %copy-done.4) | copy-start | bytes 4718596
  107.9 49.4 %all-to-all-start.2 = ((bf16[8,2,768,128]{3,2,1,0:T(8,128)(2,1)}), bf16[8,2,768,128]{3,2,1,0:T(8,128)(2,1)}, u32[]{:S(2)}, u32[]{:S(2)}) async-start(bf16[8,2,768,128]{3,2,1,0:T(8,128)(2,1)} %bitcast.36), calls=%async_computation.2 | async-start | bytes 6291456 | tf_op jit(solution)/shard_map/all_to_all | solution.py:208
  112.5 58.3 %all-gather.9.cloned.1.call-start = ((), (), s32[]{:S(2)}) async-start(), calls=%async_computation.6 | async-start | bytes 1769472 | tf_op jit(solution)/shard_map/all_gather | solution.py:222
  112.5 3.6 %copy-start.3 = (bf16[8,4,2,96,128]{4,3,2,1,0:T(8,128)(2,1)S(1)}, bf16[8,4,2,96,128]{4,3,2,1,0:T(8,128)(2,1)}, u32[]{:S(2)}) copy-start(bf16[8,4,2,96,128]{4,3,2,1,0:T(8,128)(2,1)} %copy-done.2) | copy-start | bytes 4718596
  112.6 4.2 %copy-start.7 = (bf16[384,6144]{1,0:T(8,128)(2,1)S(1)}, bf16[384,6144]{1,0:T(8,128)(2,1)}, u32[]{:S(2)}) copy-start(bf16[384,6144]{1,0:T(8,128)(2,1)} %all-gather.7.cloned.1.call-done) | copy-start | bytes 14155780
  124.3 14.5 %collective-permute-start = (bf16[8,2,96,128]{3,2,1,0:T(8,128)(2,1)S(1)}, bf16[8,2,96,128]{3,2,1,0:T(8,128)(2,1)S(1)}, u32[]{:S(2)}, u32[]{:S(2)}) collective-permute-start(bf16[8,2,96,128]{3,2,1,0:T(8,128)(2,1)S(1)} %get-tuple-element.12), channel_id=1, source_target_pairs={{0,2},{2,4},{4,6},{6,0},{1,3},{3,5},{5,7},{7,1},{8,10},{10,12},{12... | collective-permute-start | bytes 1179656 | tf_op jit(solution)/shard_map/ppermute | solution.py:175
  127.7 20.4 %collective-permute-start.1 = (bf16[8,2,96,128]{3,2,1,0:T(8,128)(2,1)S(1)}, bf16[8,2,96,128]{3,2,1,0:T(8,128)(2,1)S(1)}, u32[]{:S(2)}, u32[]{:S(2)}) collective-permute-start(bf16[8,2,96,128]{3,2,1,0:T(8,128)(2,1)S(1)} %get-tuple-element.13), channel_id=1, source_target_pairs={{0,4},{2,6},{4,0},{6,2},{1,5},{3,7},{5,1},{7,3},{8,12},{10,14},{12... | collective-permute-start | bytes 1179656 | tf_op jit(solution)/shard_map/ppermute | solution.py:175
  132.3 17.4 %collective-permute-start.2 = (bf16[8,2,96,128]{3,2,1,0:T(8,128)(2,1)S(1)}, bf16[8,2,96,128]{3,2,1,0:T(8,128)(2,1)S(1)}, u32[]{:S(2)}, u32[]{:S(2)}) collective-permute-start(bf16[8,2,96,128]{3,2,1,0:T(8,128)(2,1)S(1)} %get-tuple-element.14), channel_id=1, source_target_pairs={{0,6},{2,0},{4,2},{6,4},{1,7},{3,1},{5,3},{7,5},{8,14},{10,8},{12,... | collective-permute-start | bytes 1179656 | tf_op jit(solution)/shard_map/ppermute | solution.py:175
  158.1 38.9 %all-to-all-start.3 = ((bf16[16,96,128]{2,1,0:T(8,128)(2,1)}), bf16[16,96,128]{2,1,0:T(8,128)(2,1)S(1)}, u32[]{:S(2)}, u32[]{:S(2)}) async-start(bf16[16,96,128]{2,1,0:T(8,128)(2,1)} %bitcast.12), calls=%async_computation.3 | async-start | bytes 786432 | tf_op jit(solution)/shard_map/all_to_all | solution.py:229
  170.8 1.4 copy-start.1
  172.2 24.9 %copy-start.8 = (bf16[128,96]{0,1:T(8,128)(2,1)S(1)}, bf16[128,96]{0,1:T(8,128)(2,1)}, u32[]{:S(2)}) copy-start(bf16[128,96]{0,1:T(8,128)(2,1)} %param.5) | copy-start | bytes 73732
Sparse Core Ops, SparseCore 0:
  10.1 46.0 all-gather.4
  58.3 42.0 all-gather.6
  119.2 37.6 all-gather.8

commit v7 on v6

--- a/solution.py
+++ b/solution.py
@@ -92,29 +92,54 @@
     del mine
     count = len(refs) // 2
     for k in range(count):
-        refs[count + k][...] = refs[k][:, 0]
-
-
-def cut(rows, mine):
+        refs[count + k][:, 0] = refs[k][:, 0]
+
+
+def cut(rows, mine, n_sh):
     n_blocks, n_y, *rest = rows.shape
+    n_sl = n_blocks // n_sh
     zeros = (0,) * len(rest)
     return pl.pallas_call(
         cut_kernel,
         grid_spec=pltpu.PrefetchScalarGridSpec(
             num_scalar_prefetch=1,
-            grid=(2,),
+            grid=(n_sh,),
             in_specs=[
                 pl.BlockSpec(
-                    (n_blocks // 2, 1, *rest),
-                    lambda i, mine, k=k: (i, lax.rem(mine[0] + k, n_y), *zeros),
+                    (n_sl, 1, *rest), lambda i, mine, k=k: (i, lax.rem(mine[0] + k, n_y), *zeros)
                 )
                 for k in range(n_y)
             ],
-            out_specs=[pl.BlockSpec((n_blocks // 2, *rest), lambda i, _: (i, *zeros))] * n_y,
-        ),
-        out_shape=[jax.ShapeDtypeStruct((n_blocks, *rest), rows.dtype)] * n_y,
+            out_specs=[pl.BlockSpec((n_sl, 1, *rest), lambda i, _: (0, i, *zeros))] * n_y,
+        ),
+        out_shape=[jax.ShapeDtypeStruct((n_sl, n_sh, *rest), rows.dtype)] * n_y,
         compiler_params=pltpu.CompilerParams(vmem_limit_bytes=SMALL),
     )(mine, *([rows] * n_y))
+
+
+def fold_kernel(count, mine, *refs):
+    terms, outs = refs[:count], refs[count:]
+    for k in range(len(outs)):
+        at = lax.rem(mine[0] + k, len(outs))
+        total = terms[0][at].astype(jnp.float32)
+        for term in terms[1:]:
+            total = total + term[at].astype(jnp.float32)
+        outs[k][...] = total.astype(outs[k].dtype)
+
+
+def fold(terms, mine):
+    size, *rest = terms[0].shape
+    return pl.pallas_call(
+        lambda *refs: fold_kernel(len(terms), *refs),
+        grid_spec=pltpu.PrefetchScalarGridSpec(
+            num_scalar_prefetch=1,
+            grid=(1,),
+            in_specs=[pl.BlockSpec((size, *rest), lambda i, _: (0,) * (len(rest) + 1))] * len(terms),
+            out_specs=[pl.BlockSpec(tuple(rest), lambda i, _: (0,) * len(rest))] * size,
+        ),
+        out_shape=[jax.ShapeDtypeStruct(tuple(rest), terms[0].dtype)] * size,
+        compiler_params=pltpu.CompilerParams(vmem_limit_bytes=SMALL),
+    )(mine, *terms)
 
 
 def total_kernel(count, *refs):
@@ -224,9 +249,11 @@
     partial_grad = lax.dot_general(
         up_full, dpre, (((1,), (1,)), ((), ())), preferred_element_type=jnp.float32
     ).astype(jnp.bfloat16)
-    parts = cut(partial_grad.reshape(n_rep, n_y, n_zh, width, tokens), place("y"))
-    parts = total(trade(parts, "y"), owned).reshape(n_rep * n_zh, width, tokens)
-    parts = lax.all_to_all(parts, ("sh", "sl", "zh"), split_axis=0, concat_axis=0, tiled=True)
+    parts = cut(partial_grad.reshape(n_rep, n_y, n_zh, width, tokens), place("y"), n_sh)
+    parts = fold(trade(parts, "y"), place("sl"))
+    parts = trade(parts, "sl")
+    parts = total(parts, owned).reshape(n_sh * n_zh, width, tokens)
+    parts = lax.all_to_all(parts, ("sh", "zh"), split_axis=0, concat_axis=0, tiled=True)
     summed = jnp.sum(parts.astype(jnp.float32), axis=0).T
     input_grads = (cotangent.astype(jnp.float32) + summed).astype(jnp.bfloat16)
 

time: 205 us -> 200 us (0.976)
  the two profiles are of different devices: /device:TPU:32 before, /device:TPU:42 now
where the time goes in v7:
time: 200 us
  waiting for transfers between devices  62.4 us (31%)
  blocking collectives  48.9 us (24%)
  starting transfers between devices  43.9 us (22%)
  between operations  13.9 us (7%)
  local copies, waits for them, and re-layouts  10.7 us (5%)
  matrix products  9 us (4%)
  Pallas kernels  8.67 us (4%)
  other arithmetic  2.09 us (1%)
    all_to_all x1, blocking collectives, spread(): return lax.all_to_all(copies, axes, split_axis=0, concat_axis=0, tiled=True)  33.2 us
    all_gather x1, waiting for transfers between devices, body(): down_full = lax.all_gather(down_weight, REP, axis=1, tiled=True)  32.8 us
    ppermute x6, starting transfers between devices, trade(): lax.ppermute(steps[k], axes, [(i, (i + k) % size) for i in range(size)])  20.8 us
    ppermute x6, waiting for transfers between devices, trade(): lax.ppermute(steps[k], axes, [(i, (i + k) % size) for i in range(size)])  19.3 us
    all_gather x1, blocking collectives, body(): column = lax.all_gather(spaced, 'sl', axis=0, tiled=False)  15.7 us
    all_to_all x1, starting transfers between devices, body(): lax.all_to_all(parts, ('sh', 'zh'), split_axis=0, concat_axis=0, tiled=True)  12 us
    all_to_all x1, waiting for transfers between devices, body(): lax.all_to_all(parts, ('sh', 'zh'), split_axis=0, concat_axis=0, tiled=True)  8.85 us
    unnamed x18, local copies, waits for them, and re-layouts  6.02 us
  transfers between devices with their start and end apart: 12, of which 7 were waited for; matrix products, arithmetic and copies ran while one was open for 8% of the time, Pallas kernels for 3%

profile of v7, /device:TPU:42, one launch (start us, length us, event | category | flops | bytes accessed | tf_op | source)
XLA Modules:
  0.0 199.6 jit_solution(8739048760377714798)
XLA Ops:
  7.2 0.0 all-gather.5.cloned.1.call-start
  7.2 0.7 all-gather.5.cloned.1.call-update
  7.9 0.0 all-gather.7.cloned.1.call-start
  7.9 0.7 all-gather.7.cloned.1.call-update
  8.6 0.8 pad_maximum_fusion.1
  9.4 33.2 %all_to_all.20 = bf16[4,2,96,128]{3,2,1,0:T(8,128)(2,1)S(1)} all-to-all(bf16[4,2,96,128]{3,2,1,0:T(8,128)(2,1)S(1)} %broadcast_in_dim.4), channel_id=1, replica_groups=mesh['x'=4,'core'=2,'sh'=2,'sl'=4,'y'=4,'zh'=2] {'sh','zh'}, dimensions={0} | all-to-all | bytes 393216 | tf_op jit(solution)/shard_map/all_to_all | solution.py:30
  42.6 15.7 %all-gather = bf16[16,2,96,128]{3,2,1,0:T(8,128)(2,1)S(1)} all-gather(bf16[4,2,96,128]{3,2,1,0:T(8,128)(2,1)S(1)} %all_to_all.20), channel_id=2, replica_groups=mesh['x'=4,'core'=2,'sh'=2,'sl'=4,'y'=4,'zh'=2] {'sl'}, dimensions={0}, use_global_device_ids=true | all-gather | bytes 983040 | tf_op jit(solution)/shard_map/all_gather | solution.py:225
  58.4 2.4 %broadcast_in_dim.5 = bf16[4,4,4,2,96,128]{5,4,3,2,1,0:T(8,128)(2,1)} broadcast(bf16[4,4,2,96,128]{4,3,2,1,0:T(8,128)(2,1)S(1)} %bitcast.41), dimensions={1,2,3,4,5} | broadcast | bytes 3932160 | tf_op jit(solution)/shard_map/broadcast_in_dim | solution.py:29
  60.8 0.0 copy-start.6
  60.8 5.0 %all-to-all-start.1 = ((bf16[4,4,4,2,96,128]{5,4,3,2,1,0:T(8,128)(2,1)}), bf16[4,4,4,2,96,128]{5,4,3,2,1,0:T(8,128)(2,1)S(1)}, u32[]{:S(2)}, u32[]{:S(2)}) async-start(bf16[4,4,4,2,96,128]{5,4,3,2,1,0:T(8,128)(2,1)} %broadcast_in_dim.5), calls=%async_computation.1 | async-start | bytes 6291456 | tf_op jit(solution)/shard_map/all_to_all | solution.py:30
  65.8 0.0 all-gather.5.cloned.1.call-done
  65.8 0.7 slice.8.refs_4_
  66.5 32.8 %all-gather.7.cloned.1.call-done = bf16[384,6144]{1,0:T(8,128)(2,1)} async-done(((bf16[384,768]{1,0:T(8,128)(2,1)}), bf16[384,6144]{1,0:T(8,128)(2,1)}) %all-gather.7.cloned.1.call-update) | async-done | bytes 4718608 | tf_op jit(solution)/shard_map/all_gather | solution.py:221
  99.3 0.7 slice.9.refs_5_
  100.0 0.0 all-to-all-done.1
  100.0 0.0 copy-done.6
  100.0 2.8 %shard_map.68 = (bf16[8,4,2,96,128]{4,3,2,1,0:T(8,128)(2,1)S(1)}, bf16[8,4,2,96,128]{4,3,2,1,0:T(8,128)(2,1)S(1)}, bf16[8,2,4,2,96,128]{5,4,3,2,1,0:T(8,128)(2,1)S(1)}) custom-call(s32[2,8]{1,0:T(2,128)S(1)} %copy-done.6, bf16[4,4,2,2,2,96,128]{6,5,4,3,2,1,0:T(8,128)(2,1)S(1)} %bitcast.28, bf16[4,4,2,2,2,96,128]{6,5,4,3,2,1,0:T(8,128)(2,1)S(1)} %bitcast.29, ...), custom_call_target="tpu_custom_call" | custom-call | bytes 12582912 | tf_op jit(solution)/shard_map/pallas_call | solution.py:62
  102.9 0.0 copy-start
  102.9 1.6 copy-done
  104.5 0.0 copy-start.2
  104.5 1.1 copy-done.2
  105.7 0.0 copy-start.4
  105.7 1.2 copy-done.4
  106.8 0.0 copy-start.5
  106.8 6.0 %all-to-all-start.2 = ((bf16[8,2,768,128]{3,2,1,0:T(8,128)(2,1)}), bf16[8,2,768,128]{3,2,1,0:T(8,128)(2,1)}, u32[]{:S(2)}, u32[]{:S(2)}) async-start(bf16[8,2,768,128]{3,2,1,0:T(8,128)(2,1)} %bitcast.37), calls=%async_computation.2 | async-start | bytes 6291456 | tf_op jit(solution)/shard_map/all_to_all | solution.py:233
  112.8 0.0 all-gather.9.cloned.1.call-start
  112.8 0.0 copy-done.5
  112.8 0.0 copy-start.3
  112.8 0.0 copy-start.7
  112.8 3.5 %multiply_convert_fusion = (bf16[128,384]{1,0:T(8,128)(2,1)S(1)}, f32[128,384]{1,0:T(8,128)S(1)}) fusion(bf16[6144,128]{1,0:T(8,128)(2,1)S(1)} %bitcast.40, bf16[6144,384]{1,0:T(8,128)(2,1)} %all-gather.5.cloned.1.call-done), kind=kOutput, calls=%fused_computation.12 | convolution fusion | flops 604422144 | bytes 6586368 | tf_op jit(solution)/shard_map/dot_general | solution.py:237
  116.4 0.0 copy-done.3
  116.4 0.7 copy-done.7
  117.1 1.5 fusion.1
  118.6 0.7 pad_maximum_fusion
  119.3 0.0 all-gather.9.cloned.1.call-update
  119.3 3.9 %fusion = bf16[6144,128]{0,1:T(8,128)(2,1)S(1)} fusion(bf16[128,384]{1,0:T(8,128)(2,1)S(1)} %fusion.1, bf16[6144,384]{1,0:T(8,128)(2,1)} %all-gather.5.cloned.1.call-done), kind=kOutput, calls=%fused_computation.1 | convolution fusion | flops 604766208 | bytes 6389760 | tf_op jit(solution)/shard_map/dot_general | solution.py:249
  123.3 0.9 copy.8
  124.2 0.5 shard_map.69
  124.7 3.4 %collective-permute-start = (bf16[4,2,2,96,128]{4,3,2,1,0:T(8,128)(2,1)S(1)}, bf16[4,2,2,96,128]{4,3,2,1,0:T(8,128)(2,1)S(1)}, u32[]{:S(2)}, u32[]{:S(2)}) collective-permute-start(bf16[4,2,2,96,128]{4,3,2,1,0:T(8,128)(2,1)S(1)} %get-tuple-element.16), channel_id=1, source_target_pairs={{0,2},{2,4},{4,6},{6,0},{1,3},{3,5},{5,7},{7,1},{8,10},{10,12},{12... | collective-permute-start | bytes 1179656 | tf_op jit(solution)/shard_map/ppermute | solution.py:200
  128.1 3.0 %collective-permute-start.1 = (bf16[4,2,2,96,128]{4,3,2,1,0:T(8,128)(2,1)S(1)}, bf16[4,2,2,96,128]{4,3,2,1,0:T(8,128)(2,1)S(1)}, u32[]{:S(2)}, u32[]{:S(2)}) collective-permute-start(bf16[4,2,2,96,128]{4,3,2,1,0:T(8,128)(2,1)S(1)} %get-tuple-element.17), channel_id=1, source_target_pairs={{0,4},{2,6},{4,0},{6,2},{1,5},{3,7},{5,1},{7,3},{8,12},{10,14},{12... | collective-permute-start | bytes 1179656 | tf_op jit(solution)/shard_map/ppermute | solution.py:200
  131.1 4.0 %collective-permute-start.2 = (bf16[4,2,2,96,128]{4,3,2,1,0:T(8,128)(2,1)S(1)}, bf16[4,2,2,96,128]{4,3,2,1,0:T(8,128)(2,1)S(1)}, u32[]{:S(2)}, u32[]{:S(2)}) collective-permute-start(bf16[4,2,2,96,128]{4,3,2,1,0:T(8,128)(2,1)S(1)} %get-tuple-element.18), channel_id=1, source_target_pairs={{0,6},{2,0},{4,2},{6,4},{1,7},{3,1},{5,3},{7,5},{8,14},{10,8},{12,... | collective-permute-start | bytes 1179656 | tf_op jit(solution)/shard_map/ppermute | solution.py:200
  135.2 3.4 %collective-permute-done.refs_2_ = bf16[4,2,2,96,128]{4,3,2,1,0:T(8,128)(2,1)S(1)} collective-permute-done((bf16[4,2,2,96,128]{4,3,2,1,0:T(8,128)(2,1)S(1)}, bf16[4,2,2,96,128]{4,3,2,1,0:T(8,128)(2,1)S(1)}, u32[]{:S(2)}, u32[]{:S(2)}) %collective-permute-start) | collective-permute-done | bytes 393248 | tf_op jit(solution)/shard_map/ppermute | solution.py:200
  138.6 5.0 %collective-permute-done.1.refs_3_ = bf16[4,2,2,96,128]{4,3,2,1,0:T(8,128)(2,1)S(1)} collective-permute-done((bf16[4,2,2,96,128]{4,3,2,1,0:T(8,128)(2,1)S(1)}, bf16[4,2,2,96,128]{4,3,2,1,0:T(8,128)(2,1)S(1)}, u32[]{:S(2)}, u32[]{:S(2)}) %collective-permute-start.1) | collective-permute-done | bytes 393248 | tf_op jit(solution)/shard_map/ppermute | solution.py:200
  143.5 7.3 %collective-permute-done.2.refs_4_ = bf16[4,2,2,96,128]{4,3,2,1,0:T(8,128)(2,1)S(1)} collective-permute-done((bf16[4,2,2,96,128]{4,3,2,1,0:T(8,128)(2,1)S(1)}, bf16[4,2,2,96,128]{4,3,2,1,0:T(8,128)(2,1)S(1)}, u32[]{:S(2)}, u32[]{:S(2)}) %collective-permute-start.2) | collective-permute-done | bytes 393248 | tf_op jit(solution)/shard_map/ppermute | solution.py:200
  150.8 0.2 shard_map.70
  151.0 3.5 %collective-permute-start.3 = (bf16[2,2,96,128]{3,2,1,0:T(8,128)(2,1)S(1)}, bf16[2,2,96,128]{3,2,1,0:T(8,128)(2,1)S(1)}, u32[]{:S(2)}, u32[]{:S(2)}) collective-permute-start(bf16[2,2,96,128]{3,2,1,0:T(8,128)(2,1)S(1)} %get-tuple-element.20), channel_id=1, source_target_pairs={{0,8},{8,16},{16,24},{24,0},{1,9},{9,17},{17,25},{25,1},{2,10},{10... | collective-permute-start | bytes 294920 | tf_op jit(solution)/shard_map/ppermute | solution.py:200
  154.5 3.2 %collective-permute-start.4 = (bf16[2,2,96,128]{3,2,1,0:T(8,128)(2,1)S(1)}, bf16[2,2,96,128]{3,2,1,0:T(8,128)(2,1)S(1)}, u32[]{:S(2)}, u32[]{:S(2)}) collective-permute-start(bf16[2,2,96,128]{3,2,1,0:T(8,128)(2,1)S(1)} %get-tuple-element.21), channel_id=1, source_target_pairs={{0,16},{8,24},{16,0},{24,8},{1,17},{9,25},{17,1},{25,9},{2,18},{10... | collective-permute-start | bytes 294920 | tf_op jit(solution)/shard_map/ppermute | solution.py:200
  157.7 3.6 %collective-permute-start.5 = (bf16[2,2,96,128]{3,2,1,0:T(8,128)(2,1)S(1)}, bf16[2,2,96,128]{3,2,1,0:T(8,128)(2,1)S(1)}, u32[]{:S(2)}, u32[]{:S(2)}) collective-permute-start(bf16[2,2,96,128]{3,2,1,0:T(8,128)(2,1)S(1)} %get-tuple-element.22), channel_id=1, source_target_pairs={{0,24},{8,0},{16,8},{24,16},{1,25},{9,1},{17,9},{25,17},{2,26},{10... | collective-permute-start | bytes 294920 | tf_op jit(solution)/shard_map/ppermute | solution.py:200
  161.3 0.0 collective-permute-done.3.refs_1_
  161.3 0.7 collective-permute-done.4.refs_2_
  162.0 3.0 %collective-permute-done.5.refs_3_ = bf16[2,2,96,128]{3,2,1,0:T(8,128)(2,1)S(1)} collective-permute-done((bf16[2,2,96,128]{3,2,1,0:T(8,128)(2,1)S(1)}, bf16[2,2,96,128]{3,2,1,0:T(8,128)(2,1)S(1)}, u32[]{:S(2)}, u32[]{:S(2)}) %collective-permute-start.5) | collective-permute-done | bytes 98336 | tf_op jit(solution)/shard_map/ppermute | solution.py:200
  165.0 0.0 all-to-all-done.2.refs_4_.pieces
  165.0 0.7 shard_map.71
  165.7 12.0 %all-to-all-start.3 = ((bf16[4,96,128]{2,1,0:T(8,128)(2,1)}), bf16[4,96,128]{2,1,0:T(8,128)(2,1)S(1)}, u32[]{:S(2)}, u32[]{:S(2)}) async-start(bf16[4,96,128]{2,1,0:T(8,128)(2,1)} %bitcast.13), calls=%async_computation.3 | async-start | bytes 196608 | tf_op jit(solution)/shard_map/all_to_all | solution.py:256
  177.8 0.0 all-gather.9.cloned.1.call-done
  177.8 0.0 copy-start.1
  177.8 1.4 copy-done.1
  179.2 0.0 copy-start.8
  179.2 4.4 %shard_map.72 = f32[2,1,768,384]{3,2,1,0:T(8,128)} custom-call(bf16[8,2,768,128]{3,2,1,0:T(8,128)(2,1)} %all-to-all-done.2.refs_4_.pieces, bf16[8,128,768]{2,1,0:T(8,128)(2,1)S(1)} %bitcast.38), custom_call_target="tpu_custom_call" | custom-call | flops 1207959552 | bytes 7864320 | tf_op jit(solution)/shard_map/pallas_call | solution.py:179
  183.6 8.9 %all-to-all-done.3 = bf16[4,96,128]{2,1,0:T(8,128)(2,1)S(1)} async-done(((bf16[4,96,128]{2,1,0:T(8,128)(2,1)}), bf16[4,96,128]{2,1,0:T(8,128)(2,1)S(1)}, u32[]{:S(2)}, u32[]{:S(2)}) %all-to-all-start.3) | async-done | bytes 98336 | tf_op jit(solution)/shard_map/all_to_all | solution.py:256
  192.5 0.0 copy-done.8
  192.5 0.6 fusion.7
  (2 shorter events, 0.0 us)
Async XLA Ops:
  7.2 58.7 %all-gather.5.cloned.1.call-start = ((), (), s32[]{:S(2)}) async-start(), calls=%async_computation.4 | async-start | bytes 5308416 | tf_op jit(solution)/shard_map/all_gather | solution.py:220
  7.9 91.4 %all-gather.7.cloned.1.call-start = ((), (), s32[]{:S(2)}) async-start(), calls=%async_computation.5 | async-start | bytes 5308416 | tf_op jit(solution)/shard_map/all_gather | solution.py:221
  60.8 39.2 %copy-start.6 = (s32[2,8]{1,0:T(2,128)S(1)}, s32[2,8]{1,0:T(2,128)}, u32[]{:S(2)}) copy-start(s32[2,8]{1,0:T(2,128)} %owner.1) | copy-start | bytes 196
  60.8 39.2 %all-to-all-start.1 = ((bf16[4,4,4,2,96,128]{5,4,3,2,1,0:T(8,128)(2,1)}), bf16[4,4,4,2,96,128]{5,4,3,2,1,0:T(8,128)(2,1)S(1)}, u32[]{:S(2)}, u32[]{:S(2)}) async-start(bf16[4,4,4,2,96,128]{5,4,3,2,1,0:T(8,128)(2,1)} %broadcast_in_dim.5), calls=%async_computation.1 | async-start | bytes 6291456 | tf_op jit(solution)/shard_map/all_to_all | solution.py:30
  102.9 1.6 copy-start
  104.5 1.1 copy-start.2
  105.7 1.2 copy-start.4
  106.8 6.0 %copy-start.5 = (bf16[8,4,2,96,128]{4,3,2,1,0:T(8,128)(2,1)S(1)}, bf16[8,4,2,96,128]{4,3,2,1,0:T(8,128)(2,1)}, u32[]{:S(2)}) copy-start(bf16[8,4,2,96,128]{4,3,2,1,0:T(8,128)(2,1)} %copy-done.4) | copy-start | bytes 4718596
  106.8 58.2 %all-to-all-start.2 = ((bf16[8,2,768,128]{3,2,1,0:T(8,128)(2,1)}), bf16[8,2,768,128]{3,2,1,0:T(8,128)(2,1)}, u32[]{:S(2)}, u32[]{:S(2)}) async-start(bf16[8,2,768,128]{3,2,1,0:T(8,128)(2,1)} %bitcast.37), calls=%async_computation.2 | async-start | bytes 6291456 | tf_op jit(solution)/shard_map/all_to_all | solution.py:233
  112.8 65.0 %all-gather.9.cloned.1.call-start = ((), (), s32[]{:S(2)}) async-start(), calls=%async_computation.6 | async-start | bytes 1769472 | tf_op jit(solution)/shard_map/all_gather | solution.py:247
  112.8 3.6 %copy-start.3 = (bf16[8,4,2,96,128]{4,3,2,1,0:T(8,128)(2,1)S(1)}, bf16[8,4,2,96,128]{4,3,2,1,0:T(8,128)(2,1)}, u32[]{:S(2)}) copy-start(bf16[8,4,2,96,128]{4,3,2,1,0:T(8,128)(2,1)} %copy-done.2) | copy-start | bytes 4718596
  112.8 4.2 %copy-start.7 = (bf16[384,6144]{1,0:T(8,128)(2,1)S(1)}, bf16[384,6144]{1,0:T(8,128)(2,1)}, u32[]{:S(2)}) copy-start(bf16[384,6144]{1,0:T(8,128)(2,1)} %all-gather.7.cloned.1.call-done) | copy-start | bytes 14155780
  124.7 13.9 %collective-permute-start = (bf16[4,2,2,96,128]{4,3,2,1,0:T(8,128)(2,1)S(1)}, bf16[4,2,2,96,128]{4,3,2,1,0:T(8,128)(2,1)S(1)}, u32[]{:S(2)}, u32[]{:S(2)}) collective-permute-start(bf16[4,2,2,96,128]{4,3,2,1,0:T(8,128)(2,1)S(1)} %get-tuple-element.16), channel_id=1, source_target_pairs={{0,2},{2,4},{4,6},{6,0},{1,3},{3,5},{5,7},{7,1},{8,10},{10,12},{12... | collective-permute-start | bytes 1179656 | tf_op jit(solution)/shard_map/ppermute | solution.py:200
  128.1 15.4 %collective-permute-start.1 = (bf16[4,2,2,96,128]{4,3,2,1,0:T(8,128)(2,1)S(1)}, bf16[4,2,2,96,128]{4,3,2,1,0:T(8,128)(2,1)S(1)}, u32[]{:S(2)}, u32[]{:S(2)}) collective-permute-start(bf16[4,2,2,96,128]{4,3,2,1,0:T(8,128)(2,1)S(1)} %get-tuple-element.17), channel_id=1, source_target_pairs={{0,4},{2,6},{4,0},{6,2},{1,5},{3,7},{5,1},{7,3},{8,12},{10,14},{12... | collective-permute-start | bytes 1179656 | tf_op jit(solution)/shard_map/ppermute | solution.py:200
  131.1 19.7 %collective-permute-start.2 = (bf16[4,2,2,96,128]{4,3,2,1,0:T(8,128)(2,1)S(1)}, bf16[4,2,2,96,128]{4,3,2,1,0:T(8,128)(2,1)S(1)}, u32[]{:S(2)}, u32[]{:S(2)}) collective-permute-start(bf16[4,2,2,96,128]{4,3,2,1,0:T(8,128)(2,1)S(1)} %get-tuple-element.18), channel_id=1, source_target_pairs={{0,6},{2,0},{4,2},{6,4},{1,7},{3,1},{5,3},{7,5},{8,14},{10,8},{12,... | collective-permute-start | bytes 1179656 | tf_op jit(solution)/shard_map/ppermute | solution.py:200
  151.0 10.3 %collective-permute-start.3 = (bf16[2,2,96,128]{3,2,1,0:T(8,128)(2,1)S(1)}, bf16[2,2,96,128]{3,2,1,0:T(8,128)(2,1)S(1)}, u32[]{:S(2)}, u32[]{:S(2)}) collective-permute-start(bf16[2,2,96,128]{3,2,1,0:T(8,128)(2,1)S(1)} %get-tuple-element.20), channel_id=1, source_target_pairs={{0,8},{8,16},{16,24},{24,0},{1,9},{9,17},{17,25},{25,1},{2,10},{10... | collective-permute-start | bytes 294920 | tf_op jit(solution)/shard_map/ppermute | solution.py:200
  154.5 7.5 %collective-permute-start.4 = (bf16[2,2,96,128]{3,2,1,0:T(8,128)(2,1)S(1)}, bf16[2,2,96,128]{3,2,1,0:T(8,128)(2,1)S(1)}, u32[]{:S(2)}, u32[]{:S(2)}) collective-permute-start(bf16[2,2,96,128]{3,2,1,0:T(8,128)(2,1)S(1)} %get-tuple-element.21), channel_id=1, source_target_pairs={{0,16},{8,24},{16,0},{24,8},{1,17},{9,25},{17,1},{25,9},{2,18},{10... | collective-permute-start | bytes 294920 | tf_op jit(solution)/shard_map/ppermute | solution.py:200
  157.7 7.4 %collective-permute-start.5 = (bf16[2,2,96,128]{3,2,1,0:T(8,128)(2,1)S(1)}, bf16[2,2,96,128]{3,2,1,0:T(8,128)(2,1)S(1)}, u32[]{:S(2)}, u32[]{:S(2)}) collective-permute-start(bf16[2,2,96,128]{3,2,1,0:T(8,128)(2,1)S(1)} %get-tuple-element.22), channel_id=1, source_target_pairs={{0,24},{8,0},{16,8},{24,16},{1,25},{9,1},{17,9},{25,17},{2,26},{10... | collective-permute-start | bytes 294920 | tf_op jit(solution)/shard_map/ppermute | solution.py:200
  165.7 26.7 %all-to-all-start.3 = ((bf16[4,96,128]{2,1,0:T(8,128)(2,1)}), bf16[4,96,128]{2,1,0:T(8,128)(2,1)S(1)}, u32[]{:S(2)}, u32[]{:S(2)}) async-start(bf16[4,96,128]{2,1,0:T(8,128)(2,1)} %bitcast.13), calls=%async_computation.3 | async-start | bytes 196608 | tf_op jit(solution)/shard_map/all_to_all | solution.py:256
  177.8 1.4 copy-start.1
  179.2 13.3 %copy-start.8 = (bf16[128,96]{0,1:T(8,128)(2,1)S(1)}, bf16[128,96]{0,1:T(8,128)(2,1)}, u32[]{:S(2)}) copy-start(bf16[128,96]{0,1:T(8,128)(2,1)} %param.5) | copy-start | bytes 73732
Sparse Core Ops, SparseCore 0:
  10.1 44.9 all-gather.4
  57.3 42.0 all-gather.6
  119.5 36.3 all-gather.8

commit v8 on v7

--- a/solution.py
+++ b/solution.py
@@ -30,62 +30,50 @@
     return lax.all_to_all(copies, axes, split_axis=0, concat_axis=0, tiled=True)
 
 
-def arrange_kernel(owner, plain, *refs):
-    del owner
-    count = plain.shape[1]
-    chosen, (first, second, message) = refs[:count], refs[-3:]
+def arrange_kernel(owner, gathered, first, second, message, sems):
+    _, n_sl, n_sh = gathered.shape[:3]
+    n_blocks = n_sl * n_sh
+    copies = []
     for j, flat in enumerate((first, second)):
-
-        @pl.when(pl.program_id(0) == j)
-        def _(flat=flat):
-            for b in range(count):
-                flat[b] = plain[:, b, 0, :, 0]
-
-    for k in range(count):
-        message[k, 0] = chosen[k][:, 0, 0, :, 0]
-
-
-def arrange(gathered, owner, after):
+        for r in range(n_blocks):
+            b = sum(jnp.where(owner[j, i] == r, i, 0) for i in range(n_blocks))
+            copies.append(
+                pltpu.make_async_copy(
+                    gathered.at[:, lax.rem(b, n_sl), lax.div(b, n_sl), :, j],
+                    message.at[r, j],
+                    sems.at[len(copies)],
+                )
+            )
+            copies.append(
+                pltpu.make_async_copy(
+                    gathered.at[:, r % n_sl, r // n_sl, :, j], flat.at[r], sems.at[len(copies)]
+                )
+            )
+    for copy in copies:
+        copy.start()
+    for copy in copies:
+        copy.wait()
+
+
+def arrange(gathered, owner):
     n_y, n_sl, n_sh, n_zh, _, width, tokens = gathered.shape
     n_blocks = n_sl * n_sh
-    piece = (n_y, 1, 1, n_zh, 1, width, tokens)
-
-    def chosen_at(k):
-        def index(j, h, owner):
-            target = h * n_sl + k
-            b = sum(jnp.where(owner[j, i] == target, i, 0) for i in range(n_blocks))
-            return (0, lax.rem(b, n_sl), lax.div(b, n_sl), 0, j, 0, 0)
-
-        return index
-
     out = (n_y, n_zh, width, tokens)
     return pl.pallas_call(
         arrange_kernel,
-        grid_spec=pltpu.PrefetchScalarGridSpec(
-            num_scalar_prefetch=1,
-            grid=(2, n_sh),
-            in_specs=[
-                pl.BlockSpec(
-                    (n_y, n_sl, 1, n_zh, 1, width, tokens), lambda j, h, _: (0, 0, h, 0, j, 0, 0)
-                )
-            ]
-            + [pl.BlockSpec(piece, chosen_at(k)) for k in range(n_sl)]
-            + [pl.BlockSpec(memory_space=pl.ANY)] * len(after),
-            out_specs=[
-                pl.BlockSpec(
-                    (n_sl,) + out, lambda j, h, _: (jnp.where(j == 0, h, n_sh - 1), 0, 0, 0, 0)
-                ),
-                pl.BlockSpec((n_sl,) + out, lambda j, h, _: (jnp.where(j == 0, 0, h), 0, 0, 0, 0)),
-                pl.BlockSpec((n_sl, 1) + out, lambda j, h, _: (h, j, 0, 0, 0, 0)),
-            ],
-        ),
+        in_specs=[
+            pl.BlockSpec(memory_space=pltpu.SMEM),
+            pl.BlockSpec(memory_space=pl.ANY),
+        ],
+        out_specs=[pl.BlockSpec(memory_space=pl.ANY)] * 3,
         out_shape=[jax.ShapeDtypeStruct((n_blocks,) + out, gathered.dtype)] * 2
         + [jax.ShapeDtypeStruct((n_blocks, 2) + out, gathered.dtype)],
-        compiler_params=pltpu.CompilerParams(vmem_limit_bytes=SMALL),
+        scratch_shapes=[pltpu.SemaphoreType.DMA((4 * n_blocks,))],
+        compiler_params=pltpu.CompilerParams(vmem_limit_bytes=60 * 1024 * 1024),
         cost_estimate=pl.CostEstimate(
             flops=0, bytes_accessed=8 * gathered.size, transcendentals=0
         ),
-    )(owner, gathered, *([gathered] * n_sl), *after)
+    )(owner, gathered)
 
 
 def cut_kernel(mine, *refs):
@@ -142,6 +130,23 @@
     )(mine, *terms)
 
 
+def join_kernel(first, second, _, out):
+    columns = first.shape[1]
+    out[:, :columns] = first[...]
+    out[:, columns:] = second[...]
+
+
+def join(first, second, after):
+    rows, columns = first.shape
+    return pl.pallas_call(
+        join_kernel,
+        in_specs=[pl.BlockSpec(memory_space=pltpu.VMEM)] * 2 + [pl.BlockSpec(memory_space=pl.ANY)],
+        out_specs=pl.BlockSpec(memory_space=pltpu.VMEM),
+        out_shape=jax.ShapeDtypeStruct((rows, 2 * columns), first.dtype),
+        compiler_params=pltpu.CompilerParams(vmem_limit_bytes=SMALL),
+    )(first, second, after)
+
+
 def total_kernel(count, *refs):
     total = refs[0][...].astype(jnp.float32)
     for term in refs[1:count]:
@@ -226,9 +231,7 @@
     full = spread(column, "y", n_y)
     full = full.reshape(n_y, n_sl, n_sh, n_zh, 2, width, tokens)
 
-    inputs_flat, grads_flat, message = arrange(
-        full, block_owner, (up_full[:16, :128], down_full[:16, :128])
-    )
+    inputs_flat, grads_flat, message = arrange(full, block_owner)
     message = message.reshape(n_rep, 2, block, tokens)
     owned = lax.all_to_all(message, REP, split_axis=0, concat_axis=0, tiled=True)
 
@@ -244,12 +247,11 @@
     hidden = value.astype(jnp.bfloat16)
     dpre = (back_grad * deriv).astype(jnp.bfloat16)
 
-    both = lax.all_gather(jnp.concatenate([dpre, hidden], axis=1), REP, axis=0, tiled=True)
-
     partial_grad = lax.dot_general(
         up_full, dpre, (((1,), (1,)), ((), ())), preferred_element_type=jnp.float32
     ).astype(jnp.bfloat16)
     parts = cut(partial_grad.reshape(n_rep, n_y, n_zh, width, tokens), place("y"), n_sh)
+    both = lax.all_gather(join(dpre, hidden, parts[0]), REP, axis=0, tiled=True)
     parts = fold(trade(parts, "y"), place("sl"))
     parts = trade(parts, "sl")
     parts = total(parts, owned).reshape(n_sh * n_zh, width, tokens)

time: 200 us -> 383 us (1.92)
  the two profiles are of different devices: /device:TPU:42 before, /device:TPU:1 now
where the time goes in v8:
time: 383 us; the launch traced here: 381 us
  Pallas kernels  199 us (52%)
  blocking collectives  63.3 us (17%)
  waiting for transfers between devices  56 us (15%)
  starting transfers between devices  31.8 us (8%)
  between operations  13.9 us (4%)
  matrix products  9.12 us (2%)
  local copies, waits for them, and re-layouts  6.45 us (2%)
    pallas_call x1, Pallas kernels, arrange(): pl.pallas_call(arrange_kernel, in_specs=[pl.BlockSpec(memory_space=pltpu....  193 us
    all_to_all x1, waiting for transfers between devices, spread(): return lax.all_to_all(copies, axes, split_axis=0, concat_axis=0, tiled=True)  33 us
    all_to_all x1, blocking collectives, spread(): return lax.all_to_all(copies, axes, split_axis=0, concat_axis=0, tiled=True)  28.3 us
    ppermute x6, waiting for transfers between devices, trade(): lax.ppermute(steps[k], axes, [(i, (i + k) % size) for i in range(size)])  21.7 us
    all_gather x1, blocking collectives, body(): column = lax.all_gather(spaced, 'sl', axis=0, tiled=False)  20 us
    ppermute x6, starting transfers between devices, trade(): lax.ppermute(steps[k], axes, [(i, (i + k) % size) for i in range(size)])  17.5 us
    all_to_all x1, blocking collectives, body(): lax.all_to_all(parts, ('sh', 'zh'), split_axis=0, concat_axis=0, tiled=True)  14.9 us
    all_to_all x1, starting transfers between devices, body(): lax.all_to_all(message, REP, split_axis=0, concat_axis=0, tiled=True)  10 us
  transfers between devices with their start and end apart: 11, of which 6 were waited for; matrix products, arithmetic and copies ran while one was open for 4% of the time, Pallas kernels for 51%

profile of v8, /device:TPU:1, one launch (start us, length us, event | category | flops | bytes accessed | tf_op | source)
XLA Modules:
  0.0 380.6 jit_solution(10645552749311479813)
XLA Ops:
  7.2 0.0 all-gather.7.cloned.1.call-start
  7.2 0.7 all-gather.7.cloned.1.call-update
  7.9 0.0 all-gather.5.cloned.1.call-start
  7.9 0.7 all-gather.5.cloned.1.call-update
  8.6 0.8 pad_maximum_fusion
  9.4 28.3 %all_to_all.20 = bf16[4,2,96,128]{3,2,1,0:T(8,128)(2,1)S(1)} all-to-all(bf16[4,2,96,128]{3,2,1,0:T(8,128)(2,1)S(1)} %broadcast_in_dim.4), channel_id=1, replica_groups=mesh['x'=4,'core'=2,'sh'=2,'sl'=4,'y'=4,'zh'=2] {'sh','zh'}, dimensions={0} | all-to-all | bytes 393216 | tf_op jit(solution)/shard_map/all_to_all | solution.py:30
  37.8 20.0 %all-gather = bf16[16,2,96,128]{3,2,1,0:T(8,128)(2,1)S(1)} all-gather(bf16[4,2,96,128]{3,2,1,0:T(8,128)(2,1)S(1)} %all_to_all.20), channel_id=2, replica_groups=mesh['x'=4,'core'=2,'sh'=2,'sl'=4,'y'=4,'zh'=2] {'sl'}, dimensions={0}, use_global_device_ids=true | all-gather | bytes 983040 | tf_op jit(solution)/shard_map/all_gather | solution.py:230
  57.8 2.4 broadcast_in_dim.5
  60.3 4.2 %all-to-all-start.1 = ((bf16[4,4,4,2,96,128]{5,4,3,2,1,0:T(8,128)(2,1)}), bf16[4,4,4,2,96,128]{5,4,3,2,1,0:T(8,128)(2,1)S(1)}, u32[]{:S(2)}, u32[]{:S(2)}) async-start(bf16[4,4,4,2,96,128]{5,4,3,2,1,0:T(8,128)(2,1)} %broadcast_in_dim.5), calls=%async_computation.1 | async-start | bytes 6291456 | tf_op jit(solution)/shard_map/all_to_all | solution.py:30
  64.4 33.0 %all-to-all-done.1 = bf16[4,4,4,2,96,128]{5,4,3,2,1,0:T(8,128)(2,1)S(1)} async-done(((bf16[4,4,4,2,96,128]{5,4,3,2,1,0:T(8,128)(2,1)}), bf16[4,4,4,2,96,128]{5,4,3,2,1,0:T(8,128)(2,1)S(1)}, u32[]{:S(2)}, u32[]{:S(2)}) %all-to-all-start.1) | async-done | bytes 3145760 | tf_op jit(solution)/shard_map/all_to_all | solution.py:30
  97.4 0.0 copy-start.2
  97.4 1.7 copy-done.2
  99.1 192.7 %shard_map.68 = (bf16[8,4,2,96,128]{4,3,2,1,0:T(8,128)(2,1)}, bf16[8,4,2,96,128]{4,3,2,1,0:T(8,128)(2,1)}, bf16[8,2,4,2,96,128]{5,4,3,2,1,0:T(8,128)(2,1)}) custom-call(s32[2,8]{1,0:T(2,128)} %owner.1, bf16[4,4,2,2,2,96,128]{6,5,4,3,2,1,0:T(8,128)(2,1)} %bitcast.34), custom_call_target="tpu_custom_call" | custom-call | bytes 12582912 | tf_op jit(solution)/shard_map/pallas_call | solution.py:62
  291.7 0.0 copy-start.4
  291.8 10.0 %all-to-all-start.2 = ((bf16[8,2,768,128]{3,2,1,0:T(8,128)(2,1)}), bf16[8,2,768,128]{3,2,1,0:T(8,128)(2,1)}, u32[]{:S(2)}, u32[]{:S(2)}) async-start(bf16[8,2,768,128]{3,2,1,0:T(8,128)(2,1)} %bitcast.35), calls=%async_computation.2 | async-start | bytes 6291456 | tf_op jit(solution)/shard_map/all_to_all | solution.py:236
  301.8 0.0 all-gather.9.cloned.1.call-start
  301.8 0.0 all-gather.7.cloned.1.call-done
  301.8 0.0 copy-done.4
  301.8 0.0 copy-start.3
  301.8 3.5 multiply_convert_fusion
  305.3 0.0 all-gather.5.cloned.1.call-done
  305.4 0.0 copy-done.3
  305.4 0.0 copy-start.1
  305.4 4.0 %fusion.1.first = bf16[128,384]{1,0:T(8,128)(2,1)S(1)} fusion(bf16[6144,128]{1,0:T(8,128)(2,1)S(1)} %bitcast.37, bf16[384,6144]{1,0:T(8,128)(2,1)} %all-gather.5.cloned.1.call-done, f32[128,384]{1,0:T(8,128)S(1)} %get-tuple-element.25), kind=kOutput, calls=%fused_computation.3 | convolution fusion | flops 604913664 | bytes 6586368 | tf_op jit(solution)/shard_map/dot_general | solution.py:243
  309.4 0.0 copy-done.1
  309.4 1.6 fusion
  311.0 0.9 copy.8
  311.9 0.5 shard_map.69
  312.5 0.0 copy-start.5
  312.5 0.7 shard_map.72
  313.2 0.0 all-gather.9.cloned.1.call-update
  313.2 2.2 collective-permute-start
  315.4 3.7 collective-permute-start.1
  319.1 2.5 collective-permute-start.2
  321.6 5.9 %collective-permute-done.refs_2_ = bf16[4,2,2,96,128]{4,3,2,1,0:T(8,128)(2,1)S(1)} collective-permute-done((bf16[4,2,2,96,128]{4,3,2,1,0:T(8,128)(2,1)S(1)}, bf16[4,2,2,96,128]{4,3,2,1,0:T(8,128)(2,1)S(1)}, u32[]{:S(2)}, u32[]{:S(2)}) %collective-permute-start) | collective-permute-done | bytes 393248 | tf_op jit(solution)/shard_map/ppermute | solution.py:205
  327.5 7.2 %collective-permute-done.1.refs_3_ = bf16[4,2,2,96,128]{4,3,2,1,0:T(8,128)(2,1)S(1)} collective-permute-done((bf16[4,2,2,96,128]{4,3,2,1,0:T(8,128)(2,1)S(1)}, bf16[4,2,2,96,128]{4,3,2,1,0:T(8,128)(2,1)S(1)}, u32[]{:S(2)}, u32[]{:S(2)}) %collective-permute-start.1) | collective-permute-done | bytes 393248 | tf_op jit(solution)/shard_map/ppermute | solution.py:205
  334.7 2.9 collective-permute-done.2.refs_4_
  337.6 0.2 shard_map.70
  337.8 2.5 collective-permute-start.3
  340.2 4.4 %collective-permute-start.4 = (bf16[2,2,96,128]{3,2,1,0:T(8,128)(2,1)S(1)}, bf16[2,2,96,128]{3,2,1,0:T(8,128)(2,1)S(1)}, u32[]{:S(2)}, u32[]{:S(2)}) collective-permute-start(bf16[2,2,96,128]{3,2,1,0:T(8,128)(2,1)S(1)} %get-tuple-element.21), channel_id=1, source_target_pairs={{0,16},{8,24},{16,0},{24,8},{1,17},{9,25},{17,1},{25,9},{2,18},{10... | collective-permute-start | bytes 294920 | tf_op jit(solution)/shard_map/ppermute | solution.py:205
  344.6 2.2 collective-permute-start.5
  346.8 0.0 all-to-all-done.2.refs_4_.pieces
  346.9 0.0 collective-permute-done.3.refs_1_
  346.9 4.2 %collective-permute-done.4.refs_2_ = bf16[2,2,96,128]{3,2,1,0:T(8,128)(2,1)S(1)} collective-permute-done((bf16[2,2,96,128]{3,2,1,0:T(8,128)(2,1)S(1)}, bf16[2,2,96,128]{3,2,1,0:T(8,128)(2,1)S(1)}, u32[]{:S(2)}, u32[]{:S(2)}) %collective-permute-start.4) | collective-permute-done | bytes 98336 | tf_op jit(solution)/shard_map/ppermute | solution.py:205
  351.1 1.6 collective-permute-done.5.refs_3_
  352.6 0.1 shard_map.71
  352.7 14.9 %all_to_all.21 = bf16[4,96,128]{2,1,0:T(8,128)(2,1)S(1)} all-to-all(bf16[4,96,128]{2,1,0:T(8,128)(2,1)S(1)} %bitcast.33), channel_id=1, replica_groups=mesh['x'=4,'core'=2,'sh'=2,'sl'=4,'y'=4,'zh'=2] {'sh','zh'}, dimensions={0} | all-to-all | bytes 196608 | tf_op jit(solution)/shard_map/all_to_all | solution.py:258
  367.6 0.0 copy-done.5
  367.7 0.6 fusion.7
  368.3 0.0 all-gather.9.cloned.1.call-done
  368.3 0.0 copy-start
  368.3 1.4 copy-done
  369.7 4.4 %shard_map.73 = f32[2,1,768,384]{3,2,1,0:T(8,128)} custom-call(bf16[8,2,768,128]{3,2,1,0:T(8,128)(2,1)} %all-to-all-done.2.refs_4_.pieces, bf16[8,128,768]{2,1,0:T(8,128)(2,1)S(1)} %bitcast.32), custom_call_target="tpu_custom_call" | custom-call | flops 1207959552 | bytes 7864320 | tf_op jit(solution)/shard_map/pallas_call | solution.py:184
  (2 shorter events, 0.0 us)
Async XLA Ops:
  7.2 294.6 %all-gather.7.cloned.1.call-start = ((), (), s32[]{:S(2)}) async-start(), calls=%async_computation.5 | async-start | bytes 5308416 | tf_op jit(solution)/shard_map/all_gather | solution.py:225
  7.9 297.5 %all-gather.5.cloned.1.call-start = ((), (), s32[]{:S(2)}) async-start(), calls=%async_computation.4 | async-start | bytes 5308416 | tf_op jit(solution)/shard_map/all_gather | solution.py:226
  60.3 37.1 %all-to-all-start.1 = ((bf16[4,4,4,2,96,128]{5,4,3,2,1,0:T(8,128)(2,1)}), bf16[4,4,4,2,96,128]{5,4,3,2,1,0:T(8,128)(2,1)S(1)}, u32[]{:S(2)}, u32[]{:S(2)}) async-start(bf16[4,4,4,2,96,128]{5,4,3,2,1,0:T(8,128)(2,1)} %broadcast_in_dim.5), calls=%async_computation.1 | async-start | bytes 6291456 | tf_op jit(solution)/shard_map/all_to_all | solution.py:30
  97.4 1.7 copy-start.2
  291.7 10.1 %copy-start.4 = (bf16[8,4,2,96,128]{4,3,2,1,0:T(8,128)(2,1)S(1)}, bf16[8,4,2,96,128]{4,3,2,1,0:T(8,128)(2,1)}, u32[]{:S(2)}) copy-start(bf16[8,4,2,96,128]{4,3,2,1,0:T(8,128)(2,1)} %get-tuple-element.14) | copy-start | bytes 4718596
  291.8 55.1 %all-to-all-start.2 = ((bf16[8,2,768,128]{3,2,1,0:T(8,128)(2,1)}), bf16[8,2,768,128]{3,2,1,0:T(8,128)(2,1)}, u32[]{:S(2)}, u32[]{:S(2)}) async-start(bf16[8,2,768,128]{3,2,1,0:T(8,128)(2,1)} %bitcast.35), calls=%async_computation.2 | async-start | bytes 6291456 | tf_op jit(solution)/shard_map/all_to_all | solution.py:236
  301.8 66.5 %all-gather.9.cloned.1.call-start = ((), (), s32[]{:S(2)}) async-start(), calls=%async_computation.6 | async-start | bytes 1769472 | tf_op jit(solution)/shard_map/all_gather | solution.py:254
  301.8 3.6 copy-start.3
  305.4 4.0 %copy-start.1 = (bf16[6144,384]{1,0:T(8,128)(2,1)S(1)}, bf16[6144,384]{1,0:T(8,128)(2,1)}, u32[]{:S(2)}) copy-start(bf16[6144,384]{1,0:T(8,128)(2,1)} %all-gather.7.cloned.1.call-done) | copy-start | bytes 14155780
  312.5 55.2 %copy-start.5 = (bf16[128,96]{0,1:T(8,128)(2,1)S(1)}, bf16[128,96]{0,1:T(8,128)(2,1)}, u32[]{:S(2)}) copy-start(bf16[128,96]{0,1:T(8,128)(2,1)} %param.5) | copy-start | bytes 73732
  313.2 14.3 %collective-permute-start = (bf16[4,2,2,96,128]{4,3,2,1,0:T(8,128)(2,1)S(1)}, bf16[4,2,2,96,128]{4,3,2,1,0:T(8,128)(2,1)S(1)}, u32[]{:S(2)}, u32[]{:S(2)}) collective-permute-start(bf16[4,2,2,96,128]{4,3,2,1,0:T(8,128)(2,1)S(1)} %get-tuple-element.16), channel_id=1, source_target_pairs={{0,2},{2,4},{4,6},{6,0},{1,3},{3,5},{5,7},{7,1},{8,10},{10,12},{12... | collective-permute-start | bytes 1179656 | tf_op jit(solution)/shard_map/ppermute | solution.py:205
  315.4 19.3 %collective-permute-start.1 = (bf16[4,2,2,96,128]{4,3,2,1,0:T(8,128)(2,1)S(1)}, bf16[4,2,2,96,128]{4,3,2,1,0:T(8,128)(2,1)S(1)}, u32[]{:S(2)}, u32[]{:S(2)}) collective-permute-start(bf16[4,2,2,96,128]{4,3,2,1,0:T(8,128)(2,1)S(1)} %get-tuple-element.17), channel_id=1, source_target_pairs={{0,4},{2,6},{4,0},{6,2},{1,5},{3,7},{5,1},{7,3},{8,12},{10,14},{12... | collective-permute-start | bytes 1179656 | tf_op jit(solution)/shard_map/ppermute | solution.py:205
  319.1 18.5 %collective-permute-start.2 = (bf16[4,2,2,96,128]{4,3,2,1,0:T(8,128)(2,1)S(1)}, bf16[4,2,2,96,128]{4,3,2,1,0:T(8,128)(2,1)S(1)}, u32[]{:S(2)}, u32[]{:S(2)}) collective-permute-start(bf16[4,2,2,96,128]{4,3,2,1,0:T(8,128)(2,1)S(1)} %get-tuple-element.18), channel_id=1, source_target_pairs={{0,6},{2,0},{4,2},{6,4},{1,7},{3,1},{5,3},{7,5},{8,14},{10,8},{12,... | collective-permute-start | bytes 1179656 | tf_op jit(solution)/shard_map/ppermute | solution.py:205
  337.8 9.1 %collective-permute-start.3 = (bf16[2,2,96,128]{3,2,1,0:T(8,128)(2,1)S(1)}, bf16[2,2,96,128]{3,2,1,0:T(8,128)(2,1)S(1)}, u32[]{:S(2)}, u32[]{:S(2)}) collective-permute-start(bf16[2,2,96,128]{3,2,1,0:T(8,128)(2,1)S(1)} %get-tuple-element.20), channel_id=1, source_target_pairs={{0,8},{8,16},{16,24},{24,0},{1,9},{9,17},{17,25},{25,1},{2,10},{10... | collective-permute-start | bytes 294920 | tf_op jit(solution)/shard_map/ppermute | solution.py:205
  340.2 10.8 %collective-permute-start.4 = (bf16[2,2,96,128]{3,2,1,0:T(8,128)(2,1)S(1)}, bf16[2,2,96,128]{3,2,1,0:T(8,128)(2,1)S(1)}, u32[]{:S(2)}, u32[]{:S(2)}) collective-permute-start(bf16[2,2,96,128]{3,2,1,0:T(8,128)(2,1)S(1)} %get-tuple-element.21), channel_id=1, source_target_pairs={{0,16},{8,24},{16,0},{24,8},{1,17},{9,25},{17,1},{25,9},{2,18},{10... | collective-permute-start | bytes 294920 | tf_op jit(solution)/shard_map/ppermute | solution.py:205
  344.6 8.0 %collective-permute-start.5 = (bf16[2,2,96,128]{3,2,1,0:T(8,128)(2,1)S(1)}, bf16[2,2,96,128]{3,2,1,0:T(8,128)(2,1)S(1)}, u32[]{:S(2)}, u32[]{:S(2)}) collective-permute-start(bf16[2,2,96,128]{3,2,1,0:T(8,128)(2,1)S(1)} %get-tuple-element.22), channel_id=1, source_target_pairs={{0,24},{8,0},{16,8},{24,16},{1,25},{9,1},{17,9},{25,17},{2,26},{10... | collective-permute-start | bytes 294920 | tf_op jit(solution)/shard_map/ppermute | solution.py:205
  368.3 1.4 copy-start
Sparse Core Ops, SparseCore 0:
  10.1 47.6 all-gather.6
  60.0 42.0 all-gather.4
  313.3 28.3 all-gather.8

commit v9 on v7

--- a/solution.py
+++ b/solution.py
@@ -14,6 +14,7 @@
 REP = ("x", "core")
 SHARD = ("sh", "sl", "y", "zh")
 SMALL = 24 * 1024 * 1024
+LARGE = 57 * 1024 * 1024
 
 
 def gelu_pair(values):
@@ -30,34 +31,26 @@
     return lax.all_to_all(copies, axes, split_axis=0, concat_axis=0, tiled=True)
 
 
-def arrange_kernel(owner, plain, *refs):
-    del owner
-    count = plain.shape[1]
-    chosen, (first, second, message) = refs[:count], refs[-3:]
+def arrange_kernel(owner, gathered, first, second, message):
+    _, n_sl, n_sh = gathered.shape[:3]
+    n_blocks = n_sl * n_sh
+    which, part = pl.program_id(0), pl.program_id(1)
     for j, flat in enumerate((first, second)):
 
-        @pl.when(pl.program_id(0) == j)
+        @pl.when(which == j)
         def _(flat=flat):
-            for b in range(count):
-                flat[b] = plain[:, b, 0, :, 0]
-
-    for k in range(count):
-        message[k, 0] = chosen[k][:, 0, 0, :, 0]
-
-
-def arrange(gathered, owner, after):
+            for k in range(n_sl):
+                flat[k] = gathered[:, k, part, :, 0]
+
+    for k in range(n_sl):
+        target = part * n_sl + k
+        b = sum(jnp.where(owner[which, i] == target, i, 0) for i in range(n_blocks))
+        message[k, 0] = gathered[:, lax.rem(b, n_sl), lax.div(b, n_sl), :, 0]
+
+
+def arrange(gathered, owner):
     n_y, n_sl, n_sh, n_zh, _, width, tokens = gathered.shape
     n_blocks = n_sl * n_sh
-    piece = (n_y, 1, 1, n_zh, 1, width, tokens)
-
-    def chosen_at(k):
-        def index(j, h, owner):
-            target = h * n_sl + k
-            b = sum(jnp.where(owner[j, i] == target, i, 0) for i in range(n_blocks))
-            return (0, lax.rem(b, n_sl), lax.div(b, n_sl), 0, j, 0, 0)
-
-        return index
-
     out = (n_y, n_zh, width, tokens)
     return pl.pallas_call(
         arrange_kernel,
@@ -66,11 +59,9 @@
             grid=(2, n_sh),
             in_specs=[
                 pl.BlockSpec(
-                    (n_y, n_sl, 1, n_zh, 1, width, tokens), lambda j, h, _: (0, 0, h, 0, j, 0, 0)
+                    (n_y, n_sl, n_sh, n_zh, 1, width, tokens), lambda j, h, _: (0, 0, 0, 0, j, 0, 0)
                 )
-            ]
-            + [pl.BlockSpec(piece, chosen_at(k)) for k in range(n_sl)]
-            + [pl.BlockSpec(memory_space=pl.ANY)] * len(after),
+            ],
             out_specs=[
                 pl.BlockSpec(
                     (n_sl,) + out, lambda j, h, _: (jnp.where(j == 0, h, n_sh - 1), 0, 0, 0, 0)
@@ -81,11 +72,11 @@
         ),
         out_shape=[jax.ShapeDtypeStruct((n_blocks,) + out, gathered.dtype)] * 2
         + [jax.ShapeDtypeStruct((n_blocks, 2) + out, gathered.dtype)],
-        compiler_params=pltpu.CompilerParams(vmem_limit_bytes=SMALL),
+        compiler_params=pltpu.CompilerParams(vmem_limit_bytes=LARGE),
         cost_estimate=pl.CostEstimate(
-            flops=0, bytes_accessed=8 * gathered.size, transcendentals=0
-        ),
-    )(owner, gathered, *([gathered] * n_sl), *after)
+            flops=0, bytes_accessed=6 * gathered.size, transcendentals=0
+        ),
+    )(owner, gathered)
 
 
 def cut_kernel(mine, *refs):
@@ -185,7 +176,7 @@
         ],
         out_specs=pl.BlockSpec((1, 1, rows, hidden_here), lambda j: (j, 0, 0, 0)),
         out_shape=jax.ShapeDtypeStruct((2, 1, rows, hidden_here), jnp.float32),
-        compiler_params=pltpu.CompilerParams(vmem_limit_bytes=SMALL),
+        compiler_params=pltpu.CompilerParams(vmem_limit_bytes=LARGE),
         cost_estimate=pl.CostEstimate(
             flops=4 * rows * groups * tokens * hidden_here,
             bytes_accessed=4 * rows * groups * tokens + 16 * rows * hidden_here,
@@ -196,10 +187,10 @@
 
 def trade(steps, axes):
     size = lax.axis_size(axes)
-    return [steps[0]] + [
-        lax.ppermute(steps[k], axes, [(i, (i + k) % size) for i in range(size)])
-        for k in range(1, size)
-    ]
+    came = list(steps)
+    for k in sorted(range(1, size), key=lambda k: -min(k, size - k)):
+        came[k] = lax.ppermute(steps[k], axes, [(i, (i + k) % size) for i in range(size)])
+    return came
 
 
 def place(axes):
@@ -226,9 +217,7 @@
     full = spread(column, "y", n_y)
     full = full.reshape(n_y, n_sl, n_sh, n_zh, 2, width, tokens)
 
-    inputs_flat, grads_flat, message = arrange(
-        full, block_owner, (up_full[:16, :128], down_full[:16, :128])
-    )
+    inputs_flat, grads_flat, message = arrange(full, block_owner)
     message = message.reshape(n_rep, 2, block, tokens)
     owned = lax.all_to_all(message, REP, split_axis=0, concat_axis=0, tiled=True)
 

time: 200 us -> 195 us (0.975)
  the two profiles are of different devices: /device:TPU:42 before, /device:TPU:1 now
where the time goes in v9:
time: 195 us; the launch traced here: 192 us
  blocking collectives  100 us (51%)
  starting transfers between devices  27.7 us (14%)
  waiting for transfers between devices  22.9 us (12%)
  between operations  13.9 us (7%)
  Pallas kernels  12 us (6%)
  matrix products  11.3 us (6%)
  other arithmetic  2.09 us (1%)
    all_to_all x2, blocking collectives, spread(): return lax.all_to_all(copies, axes, split_axis=0, concat_axis=0, tiled=True)  65.4 us
    ppermute x6, waiting for transfers between devices, trade(): lax.ppermute(steps[k], axes, [(i, (i + k) % size) for i in range(size)])  21.4 us
    all_gather x1, blocking collectives, body(): column = lax.all_gather(spaced, 'sl', axis=0, tiled=False)  20 us
    ppermute x6, starting transfers between devices, trade(): lax.ppermute(steps[k], axes, [(i, (i + k) % size) for i in range(size)])  17.6 us
    all_to_all x1, blocking collectives, body(): lax.all_to_all(parts, ('sh', 'zh'), split_axis=0, concat_axis=0, tiled=True)  15 us
    all_to_all x1, starting transfers between devices, body(): lax.all_to_all(message, REP, split_axis=0, concat_axis=0, tiled=True)  10 us
    pallas_call x1, Pallas kernels, arrange(): pl.pallas_call(arrange_kernel, grid_spec=pltpu.PrefetchScalarGridSpec(num...  6.61 us
    pallas_call x1, Pallas kernels, block_grads(): pl.pallas_call(grads_kernel, grid=(2,), in_specs=[pl.BlockSpec((groups, 1...  4.59 us
  transfers between devices with their start and end apart: 10, of which 5 were waited for; matrix products, arithmetic and copies ran while one was open for 8% of the time, Pallas kernels for 4%

profile of v9, /device:TPU:1, one launch (start us, length us, event | category | flops | bytes accessed | tf_op | source)
XLA Modules:
  0.0 192.0 jit_solution(9296316421853907222)
XLA Ops:
  7.2 0.0 all-gather.7.cloned.1.call-start
  7.2 0.7 all-gather.7.cloned.1.call-update
  7.9 0.0 all-gather.5.cloned.1.call-start
  7.9 0.7 all-gather.5.cloned.1.call-update
  8.6 0.8 pad_maximum_fusion.1
  9.4 28.3 %all_to_all.20 = bf16[4,2,96,128]{3,2,1,0:T(8,128)(2,1)S(1)} all-to-all(bf16[4,2,96,128]{3,2,1,0:T(8,128)(2,1)S(1)} %broadcast_in_dim.4), channel_id=1, replica_groups=mesh['x'=4,'core'=2,'sh'=2,'sl'=4,'y'=4,'zh'=2] {'sh','zh'}, dimensions={0} | all-to-all | bytes 393216 | tf_op jit(solution)/shard_map/all_to_all | solution.py:31
  37.8 20.0 %all-gather = bf16[16,2,96,128]{3,2,1,0:T(8,128)(2,1)S(1)} all-gather(bf16[4,2,96,128]{3,2,1,0:T(8,128)(2,1)S(1)} %all_to_all.20), channel_id=2, replica_groups=mesh['x'=4,'core'=2,'sh'=2,'sl'=4,'y'=4,'zh'=2] {'sl'}, dimensions={0}, use_global_device_ids=true | all-gather | bytes 983040 | tf_op jit(solution)/shard_map/all_gather | solution.py:216
  57.8 0.7 broadcast_in_dim.5
  58.6 37.0 %all_to_all.21 = bf16[4,4,4,2,96,128]{5,4,3,2,1,0:T(8,128)(2,1)} all-to-all(bf16[4,4,4,2,96,128]{5,4,3,2,1,0:T(8,128)(2,1)S(1)} %broadcast_in_dim.5), channel_id=1, replica_groups=mesh['x'=4,'core'=2,'sh'=2,'sl'=4,'y'=4,'zh'=2] {'y'}, dimensions={0} | all-to-all | bytes 6291456 | tf_op jit(solution)/shard_map/all_to_all | solution.py:31
  95.6 6.6 %shard_map.68 = (bf16[8,4,2,96,128]{4,3,2,1,0:T(8,128)(2,1)}, bf16[8,4,2,96,128]{4,3,2,1,0:T(8,128)(2,1)}, bf16[8,2,4,2,96,128]{5,4,3,2,1,0:T(8,128)(2,1)}) custom-call(s32[2,8]{1,0:T(2,128)} %owner.1, bf16[4,4,2,2,2,96,128]{6,5,4,3,2,1,0:T(8,128)(2,1)} %bitcast.33), custom_call_target="tpu_custom_call" | custom-call | bytes 9437184 | tf_op jit(solution)/shard_map/pallas_call | solution.py:55
  102.2 0.0 copy-start.1
  102.2 10.0 %all-to-all-start.2 = ((bf16[8,2,768,128]{3,2,1,0:T(8,128)(2,1)}), bf16[8,2,768,128]{3,2,1,0:T(8,128)(2,1)}, u32[]{:S(2)}, u32[]{:S(2)}) async-start(bf16[8,2,768,128]{3,2,1,0:T(8,128)(2,1)} %bitcast.34), calls=%async_computation.2 | async-start | bytes 6291456 | tf_op jit(solution)/shard_map/all_to_all | solution.py:222
  112.3 0.0 all-gather.9.cloned.1.call-start
  112.3 0.0 all-gather.7.cloned.1.call-done
  112.3 0.0 copy-done.1
  112.3 0.0 copy-start
  112.3 3.5 %multiply_convert_fusion = (bf16[128,384]{1,0:T(8,128)(2,1)S(1)}, f32[128,384]{1,0:T(8,128)S(1)}) fusion(bf16[6144,128]{1,0:T(8,128)(2,1)S(1)} %bitcast.38, bf16[6144,384]{1,0:T(8,128)(2,1)} %all-gather.7.cloned.1.call-done), kind=kOutput, calls=%fused_computation.12 | convolution fusion | flops 604422144 | bytes 6586368 | tf_op jit(solution)/shard_map/dot_general | solution.py:226
  115.8 0.0 all-gather.5.cloned.1.call-done
  115.9 0.0 copy-done
  115.9 3.9 %fusion.1 = bf16[128,384]{1,0:T(8,128)(2,1)S(1)} fusion(bf16[6144,128]{1,0:T(8,128)(2,1)S(1)} %bitcast.37, bf16[384,6144]{1,0:T(8,128)(2,1)} %all-gather.5.cloned.1.call-done, f32[128,384]{1,0:T(8,128)S(1)} %get-tuple-element.25), kind=kOutput, calls=%fused_computation.3 | convolution fusion | flops 604913664 | bytes 6586368 | tf_op jit(solution)/shard_map/dot_general | solution.py:229
  119.7 0.7 pad_maximum_fusion
  120.4 0.0 all-gather.9.cloned.1.call-update
  120.5 3.9 %fusion = bf16[6144,128]{0,1:T(8,128)(2,1)S(1)} fusion(bf16[128,384]{1,0:T(8,128)(2,1)S(1)} %fusion.1, bf16[6144,384]{1,0:T(8,128)(2,1)} %all-gather.7.cloned.1.call-done), kind=kOutput, calls=%fused_computation.1 | convolution fusion | flops 604766208 | bytes 6389760 | tf_op jit(solution)/shard_map/dot_general | solution.py:238
  124.4 0.9 copy.8
  125.3 0.5 shard_map.69
  125.8 0.0 copy-start.2
  125.8 2.2 %collective-permute-start = (bf16[4,2,2,96,128]{4,3,2,1,0:T(8,128)(2,1)S(1)}, bf16[4,2,2,96,128]{4,3,2,1,0:T(8,128)(2,1)S(1)}, u32[]{:S(2)}, u32[]{:S(2)}) collective-permute-start(bf16[4,2,2,96,128]{4,3,2,1,0:T(8,128)(2,1)S(1)} %get-tuple-element.16), channel_id=1, source_target_pairs={{0,2},{2,4},{4,6},{6,0},{1,3},{3,5},{5,7},{7,1},{8,10},{10,12},{12... | collective-permute-start | bytes 1179656 | tf_op jit(solution)/shard_map/ppermute | solution.py:192
  128.1 3.6 %collective-permute-start.1 = (bf16[4,2,2,96,128]{4,3,2,1,0:T(8,128)(2,1)S(1)}, bf16[4,2,2,96,128]{4,3,2,1,0:T(8,128)(2,1)S(1)}, u32[]{:S(2)}, u32[]{:S(2)}) collective-permute-start(bf16[4,2,2,96,128]{4,3,2,1,0:T(8,128)(2,1)S(1)} %get-tuple-element.17), channel_id=1, source_target_pairs={{0,4},{2,6},{4,0},{6,2},{1,5},{3,7},{5,1},{7,3},{8,12},{10,14},{12... | collective-permute-start | bytes 1179656 | tf_op jit(solution)/shard_map/ppermute | solution.py:192
  131.8 2.6 %collective-permute-start.2 = (bf16[4,2,2,96,128]{4,3,2,1,0:T(8,128)(2,1)S(1)}, bf16[4,2,2,96,128]{4,3,2,1,0:T(8,128)(2,1)S(1)}, u32[]{:S(2)}, u32[]{:S(2)}) collective-permute-start(bf16[4,2,2,96,128]{4,3,2,1,0:T(8,128)(2,1)S(1)} %get-tuple-element.18), channel_id=1, source_target_pairs={{0,6},{2,0},{4,2},{6,4},{1,7},{3,1},{5,3},{7,5},{8,14},{10,8},{12,... | collective-permute-start | bytes 1179656 | tf_op jit(solution)/shard_map/ppermute | solution.py:192
  134.3 5.8 %collective-permute-done.refs_2_ = bf16[4,2,2,96,128]{4,3,2,1,0:T(8,128)(2,1)S(1)} collective-permute-done((bf16[4,2,2,96,128]{4,3,2,1,0:T(8,128)(2,1)S(1)}, bf16[4,2,2,96,128]{4,3,2,1,0:T(8,128)(2,1)S(1)}, u32[]{:S(2)}, u32[]{:S(2)}) %collective-permute-start) | collective-permute-done | bytes 393248 | tf_op jit(solution)/shard_map/ppermute | solution.py:192
  140.2 7.2 %collective-permute-done.1.refs_3_ = bf16[4,2,2,96,128]{4,3,2,1,0:T(8,128)(2,1)S(1)} collective-permute-done((bf16[4,2,2,96,128]{4,3,2,1,0:T(8,128)(2,1)S(1)}, bf16[4,2,2,96,128]{4,3,2,1,0:T(8,128)(2,1)S(1)}, u32[]{:S(2)}, u32[]{:S(2)}) %collective-permute-start.1) | collective-permute-done | bytes 393248 | tf_op jit(solution)/shard_map/ppermute | solution.py:192
  147.3 2.9 %collective-permute-done.2.refs_4_ = bf16[4,2,2,96,128]{4,3,2,1,0:T(8,128)(2,1)S(1)} collective-permute-done((bf16[4,2,2,96,128]{4,3,2,1,0:T(8,128)(2,1)S(1)}, bf16[4,2,2,96,128]{4,3,2,1,0:T(8,128)(2,1)S(1)}, u32[]{:S(2)}, u32[]{:S(2)}) %collective-permute-start.2) | collective-permute-done | bytes 393248 | tf_op jit(solution)/shard_map/ppermute | solution.py:192
  150.2 0.2 shard_map.70
  150.4 2.5 %collective-permute-start.3 = (bf16[2,2,96,128]{3,2,1,0:T(8,128)(2,1)S(1)}, bf16[2,2,96,128]{3,2,1,0:T(8,128)(2,1)S(1)}, u32[]{:S(2)}, u32[]{:S(2)}) collective-permute-start(bf16[2,2,96,128]{3,2,1,0:T(8,128)(2,1)S(1)} %get-tuple-element.20), channel_id=1, source_target_pairs={{0,8},{8,16},{16,24},{24,0},{1,9},{9,17},{17,25},{25,1},{2,10},{10... | collective-permute-start | bytes 294920 | tf_op jit(solution)/shard_map/ppermute | solution.py:192
  152.9 4.4 %collective-permute-start.4 = (bf16[2,2,96,128]{3,2,1,0:T(8,128)(2,1)S(1)}, bf16[2,2,96,128]{3,2,1,0:T(8,128)(2,1)S(1)}, u32[]{:S(2)}, u32[]{:S(2)}) collective-permute-start(bf16[2,2,96,128]{3,2,1,0:T(8,128)(2,1)S(1)} %get-tuple-element.21), channel_id=1, source_target_pairs={{0,16},{8,24},{16,0},{24,8},{1,17},{9,25},{17,1},{25,9},{2,18},{10... | collective-permute-start | bytes 294920 | tf_op jit(solution)/shard_map/ppermute | solution.py:192
  157.3 2.3 %collective-permute-start.5 = (bf16[2,2,96,128]{3,2,1,0:T(8,128)(2,1)S(1)}, bf16[2,2,96,128]{3,2,1,0:T(8,128)(2,1)S(1)}, u32[]{:S(2)}, u32[]{:S(2)}) collective-permute-start(bf16[2,2,96,128]{3,2,1,0:T(8,128)(2,1)S(1)} %get-tuple-element.22), channel_id=1, source_target_pairs={{0,24},{8,0},{16,8},{24,16},{1,25},{9,1},{17,9},{25,17},{2,26},{10... | collective-permute-start | bytes 294920 | tf_op jit(solution)/shard_map/ppermute | solution.py:192
  159.6 0.0 all-to-all-done.2.refs_4_.pieces
  159.6 0.0 collective-permute-done.3.refs_1_
  159.6 4.1 %collective-permute-done.4.refs_2_ = bf16[2,2,96,128]{3,2,1,0:T(8,128)(2,1)S(1)} collective-permute-done((bf16[2,2,96,128]{3,2,1,0:T(8,128)(2,1)S(1)}, bf16[2,2,96,128]{3,2,1,0:T(8,128)(2,1)S(1)}, u32[]{:S(2)}, u32[]{:S(2)}) %collective-permute-start.4) | collective-permute-done | bytes 98336 | tf_op jit(solution)/shard_map/ppermute | solution.py:192
  163.7 1.4 collective-permute-done.5.refs_3_
  165.2 0.1 shard_map.71
  165.2 15.0 %all_to_all.22 = bf16[4,96,128]{2,1,0:T(8,128)(2,1)S(1)} all-to-all(bf16[4,96,128]{2,1,0:T(8,128)(2,1)S(1)} %bitcast.32), channel_id=1, replica_groups=mesh['x'=4,'core'=2,'sh'=2,'sl'=4,'y'=4,'zh'=2] {'sh','zh'}, dimensions={0} | all-to-all | bytes 196608 | tf_op jit(solution)/shard_map/all_to_all | solution.py:245
  180.3 0.0 copy-done.2
  180.3 0.6 fusion.7
  180.9 0.0 all-gather.9.cloned.1.call-done
  180.9 4.6 %shard_map.72 = f32[2,1,768,384]{3,2,1,0:T(8,128)} custom-call(bf16[8,2,768,128]{3,2,1,0:T(8,128)(2,1)} %all-to-all-done.2.refs_4_.pieces, bf16[8,128,768]{2,1,0:T(8,128)(2,1)} %bitcast.36), custom_call_target="tpu_custom_call" | custom-call | flops 1207959552 | bytes 7864320 | tf_op jit(solution)/shard_map/pallas_call | solution.py:170
  (2 shorter events, 0.0 us)
Async XLA Ops:
  7.2 105.1 %all-gather.7.cloned.1.call-start = ((), (), s32[]{:S(2)}) async-start(), calls=%async_computation.5 | async-start | bytes 5308416 | tf_op jit(solution)/shard_map/all_gather | solution.py:211
  7.9 108.0 %all-gather.5.cloned.1.call-start = ((), (), s32[]{:S(2)}) async-start(), calls=%async_computation.4 | async-start | bytes 5308416 | tf_op jit(solution)/shard_map/all_gather | solution.py:212
  102.2 10.0 %copy-start.1 = (bf16[8,4,2,96,128]{4,3,2,1,0:T(8,128)(2,1)S(1)}, bf16[8,4,2,96,128]{4,3,2,1,0:T(8,128)(2,1)}, u32[]{:S(2)}) copy-start(bf16[8,4,2,96,128]{4,3,2,1,0:T(8,128)(2,1)} %get-tuple-element.14) | copy-start | bytes 4718596
  102.2 57.3 %all-to-all-start.2 = ((bf16[8,2,768,128]{3,2,1,0:T(8,128)(2,1)}), bf16[8,2,768,128]{3,2,1,0:T(8,128)(2,1)}, u32[]{:S(2)}, u32[]{:S(2)}) async-start(bf16[8,2,768,128]{3,2,1,0:T(8,128)(2,1)} %bitcast.34), calls=%async_computation.2 | async-start | bytes 6291456 | tf_op jit(solution)/shard_map/all_to_all | solution.py:222
  112.3 68.6 %all-gather.9.cloned.1.call-start = ((), (), s32[]{:S(2)}) async-start(), calls=%async_computation.6 | async-start | bytes 1769472 | tf_op jit(solution)/shard_map/all_gather | solution.py:236
  112.3 3.6 %copy-start = (bf16[8,4,2,96,128]{4,3,2,1,0:T(8,128)(2,1)S(1)}, bf16[8,4,2,96,128]{4,3,2,1,0:T(8,128)(2,1)}, u32[]{:S(2)}) copy-start(bf16[8,4,2,96,128]{4,3,2,1,0:T(8,128)(2,1)} %get-tuple-element.13) | copy-start | bytes 4718596
  125.8 54.5 %copy-start.2 = (bf16[128,96]{0,1:T(8,128)(2,1)S(1)}, bf16[128,96]{0,1:T(8,128)(2,1)}, u32[]{:S(2)}) copy-start(bf16[128,96]{0,1:T(8,128)(2,1)} %param.5) | copy-start | bytes 73732
  125.8 14.3 %collective-permute-start = (bf16[4,2,2,96,128]{4,3,2,1,0:T(8,128)(2,1)S(1)}, bf16[4,2,2,96,128]{4,3,2,1,0:T(8,128)(2,1)S(1)}, u32[]{:S(2)}, u32[]{:S(2)}) collective-permute-start(bf16[4,2,2,96,128]{4,3,2,1,0:T(8,128)(2,1)S(1)} %get-tuple-element.16), channel_id=1, source_target_pairs={{0,2},{2,4},{4,6},{6,0},{1,3},{3,5},{5,7},{7,1},{8,10},{10,12},{12... | collective-permute-start | bytes 1179656 | tf_op jit(solution)/shard_map/ppermute | solution.py:192
  128.1 19.2 %collective-permute-start.1 = (bf16[4,2,2,96,128]{4,3,2,1,0:T(8,128)(2,1)S(1)}, bf16[4,2,2,96,128]{4,3,2,1,0:T(8,128)(2,1)S(1)}, u32[]{:S(2)}, u32[]{:S(2)}) collective-permute-start(bf16[4,2,2,96,128]{4,3,2,1,0:T(8,128)(2,1)S(1)} %get-tuple-element.17), channel_id=1, source_target_pairs={{0,4},{2,6},{4,0},{6,2},{1,5},{3,7},{5,1},{7,3},{8,12},{10,14},{12... | collective-permute-start | bytes 1179656 | tf_op jit(solution)/shard_map/ppermute | solution.py:192
  131.8 18.5 %collective-permute-start.2 = (bf16[4,2,2,96,128]{4,3,2,1,0:T(8,128)(2,1)S(1)}, bf16[4,2,2,96,128]{4,3,2,1,0:T(8,128)(2,1)S(1)}, u32[]{:S(2)}, u32[]{:S(2)}) collective-permute-start(bf16[4,2,2,96,128]{4,3,2,1,0:T(8,128)(2,1)S(1)} %get-tuple-element.18), channel_id=1, source_target_pairs={{0,6},{2,0},{4,2},{6,4},{1,7},{3,1},{5,3},{7,5},{8,14},{10,8},{12,... | collective-permute-start | bytes 1179656 | tf_op jit(solution)/shard_map/ppermute | solution.py:192
  150.4 9.2 %collective-permute-start.3 = (bf16[2,2,96,128]{3,2,1,0:T(8,128)(2,1)S(1)}, bf16[2,2,96,128]{3,2,1,0:T(8,128)(2,1)S(1)}, u32[]{:S(2)}, u32[]{:S(2)}) collective-permute-start(bf16[2,2,96,128]{3,2,1,0:T(8,128)(2,1)S(1)} %get-tuple-element.20), channel_id=1, source_target_pairs={{0,8},{8,16},{16,24},{24,0},{1,9},{9,17},{17,25},{25,1},{2,10},{10... | collective-permute-start | bytes 294920 | tf_op jit(solution)/shard_map/ppermute | solution.py:192
  152.9 10.8 %collective-permute-start.4 = (bf16[2,2,96,128]{3,2,1,0:T(8,128)(2,1)S(1)}, bf16[2,2,96,128]{3,2,1,0:T(8,128)(2,1)S(1)}, u32[]{:S(2)}, u32[]{:S(2)}) collective-permute-start(bf16[2,2,96,128]{3,2,1,0:T(8,128)(2,1)S(1)} %get-tuple-element.21), channel_id=1, source_target_pairs={{0,16},{8,24},{16,0},{24,8},{1,17},{9,25},{17,1},{25,9},{2,18},{10... | collective-permute-start | bytes 294920 | tf_op jit(solution)/shard_map/ppermute | solution.py:192
  157.3 7.9 %collective-permute-start.5 = (bf16[2,2,96,128]{3,2,1,0:T(8,128)(2,1)S(1)}, bf16[2,2,96,128]{3,2,1,0:T(8,128)(2,1)S(1)}, u32[]{:S(2)}, u32[]{:S(2)}) collective-permute-start(bf16[2,2,96,128]{3,2,1,0:T(8,128)(2,1)S(1)} %get-tuple-element.22), channel_id=1, source_target_pairs={{0,24},{8,0},{16,8},{24,16},{1,25},{9,1},{17,9},{25,17},{2,26},{10... | collective-permute-start | bytes 294920 | tf_op jit(solution)/shard_map/ppermute | solution.py:192
Sparse Core Ops, SparseCore 0:
  10.1 47.6 all-gather.6
  60.0 42.0 all-gather.4
  120.6 29.1 all-gather.8

commit v10 on v9

--- a/solution.py
+++ b/solution.py
@@ -14,7 +14,7 @@
 REP = ("x", "core")
 SHARD = ("sh", "sl", "y", "zh")
 SMALL = 24 * 1024 * 1024
-LARGE = 57 * 1024 * 1024
+LARGE = 56 * 1024 * 1024
 
 
 def gelu_pair(values):
@@ -133,6 +133,23 @@
     )(mine, *terms)
 
 
+def join_kernel(first, second, _, out):
+    columns = first.shape[1]
+    out[:, :columns] = first[...]
+    out[:, columns:] = second[...]
+
+
+def join(first, second, after):
+    rows, columns = first.shape
+    return pl.pallas_call(
+        join_kernel,
+        in_specs=[pl.BlockSpec(memory_space=pltpu.VMEM)] * 2 + [pl.BlockSpec(memory_space=pl.ANY)],
+        out_specs=pl.BlockSpec(memory_space=pltpu.VMEM),
+        out_shape=jax.ShapeDtypeStruct((rows, 2 * columns), first.dtype),
+        compiler_params=pltpu.CompilerParams(vmem_limit_bytes=SMALL),
+    )(first, second, after)
+
+
 def total_kernel(count, *refs):
     total = refs[0][...].astype(jnp.float32)
     for term in refs[1:count]:
@@ -233,12 +250,11 @@
     hidden = value.astype(jnp.bfloat16)
     dpre = (back_grad * deriv).astype(jnp.bfloat16)
 
-    both = lax.all_gather(jnp.concatenate([dpre, hidden], axis=1), REP, axis=0, tiled=True)
-
     partial_grad = lax.dot_general(
         up_full, dpre, (((1,), (1,)), ((), ())), preferred_element_type=jnp.float32
     ).astype(jnp.bfloat16)
     parts = cut(partial_grad.reshape(n_rep, n_y, n_zh, width, tokens), place("y"), n_sh)
+    both = lax.all_gather(join(dpre, hidden, parts[0]), REP, axis=0, tiled=True)
     parts = fold(trade(parts, "y"), place("sl"))
     parts = trade(parts, "sl")
     parts = total(parts, owned).reshape(n_sh * n_zh, width, tokens)

time: 195 us -> 196 us (level)
  blocking collectives: 100 us -> 63.4 us
  waiting for transfers between devices: 22.9 us -> 56.1 us
  starting transfers between devices: 27.7 us -> 31.8 us
  local copies, waits for them, and re-layouts: 1.69 us -> 5.02 us
  matrix products: 11.3 us -> 9.12 us
    all_to_all x2 -> x1, blocking collectives: 65.4 us -> 28.3 us  [spread(): return lax.all_to_all(copies, axes, split_axis=0, concat_axis=0, tiled=True)]
    all_to_all x0 -> x1, waiting for transfers between devices: none -> 33 us  [spread(): return lax.all_to_all(copies, axes, split_axis=0, concat_axis=0, tiled=True)]
    all_to_all x0 -> x1, starting transfers between devices: none -> 4.18 us  [spread(): return lax.all_to_all(copies, axes, split_axis=0, concat_axis=0, tiled=True)]
    dot_general x1, matrix products: 3.92 us -> 1.59 us  [body(): lax.dot_general(up_full, dpre, (((1,), (1,)), ((), ())), preferred_elemen...]
  transfers between devices with their start and end apart: 10 -> 11, of which waited for: 5 -> 6; matrix products, arithmetic and copies ran while one was open for 8% -> 7% of each run, Pallas kernels for 4% -> 4%
where the time goes in v10:
time: 196 us; the launch traced here: 193 us
  blocking collectives  63.4 us (32%)
  waiting for transfers between devices  56.1 us (29%)
  starting transfers between devices  31.8 us (16%)
  between operations  13.9 us (7%)
  Pallas kernels  12.7 us (6%)
  matrix products  9.12 us (5%)
  local copies, waits for them, and re-layouts  5.02 us (3%)
    all_to_all x1, waiting for transfers between devices, spread(): return lax.all_to_all(copies, axes, split_axis=0, concat_axis=0, tiled=True)  33 us
    all_to_all x1, blocking collectives, spread(): return lax.all_to_all(copies, axes, split_axis=0, concat_axis=0, tiled=True)  28.3 us
    ppermute x6, waiting for transfers between devices, trade(): lax.ppermute(steps[k], axes, [(i, (i + k) % size) for i in range(size)])  21.7 us
    all_gather x1, blocking collectives, body(): column = lax.all_gather(spaced, 'sl', axis=0, tiled=False)  20 us
    ppermute x6, starting transfers between devices, trade(): lax.ppermute(steps[k], axes, [(i, (i + k) % size) for i in range(size)])  17.5 us
    all_to_all x1, blocking collectives, body(): lax.all_to_all(parts, ('sh', 'zh'), split_axis=0, concat_axis=0, tiled=True)  15 us
    all_to_all x1, starting transfers between devices, body(): lax.all_to_all(message, REP, split_axis=0, concat_axis=0, tiled=True)  10.1 us
    pallas_call x1, Pallas kernels, arrange(): pl.pallas_call(arrange_kernel, grid_spec=pltpu.PrefetchScalarGridSpec(num...  6.59 us
  transfers between devices with their start and end apart: 11, of which 6 were waited for; matrix products, arithmetic and copies ran while one was open for 7% of the time, Pallas kernels for 4%

profile of v10, /device:TPU:1, one launch (start us, length us, event | category | flops | bytes accessed | tf_op | source)
XLA Modules:
  0.0 193.4 jit_solution(17583125475685385103)
XLA Ops:
  7.2 0.0 all-gather.7.cloned.1.call-start
  7.2 0.7 all-gather.7.cloned.1.call-update
  7.9 0.0 all-gather.5.cloned.1.call-start
  7.9 0.7 all-gather.5.cloned.1.call-update
  8.6 0.8 pad_maximum_fusion
  9.4 28.3 %all_to_all.20 = bf16[4,2,96,128]{3,2,1,0:T(8,128)(2,1)S(1)} all-to-all(bf16[4,2,96,128]{3,2,1,0:T(8,128)(2,1)S(1)} %broadcast_in_dim.4), channel_id=1, replica_groups=mesh['x'=4,'core'=2,'sh'=2,'sl'=4,'y'=4,'zh'=2] {'sh','zh'}, dimensions={0} | all-to-all | bytes 393216 | tf_op jit(solution)/shard_map/all_to_all | solution.py:31
  37.8 20.0 %all-gather = bf16[16,2,96,128]{3,2,1,0:T(8,128)(2,1)S(1)} all-gather(bf16[4,2,96,128]{3,2,1,0:T(8,128)(2,1)S(1)} %all_to_all.20), channel_id=2, replica_groups=mesh['x'=4,'core'=2,'sh'=2,'sl'=4,'y'=4,'zh'=2] {'sl'}, dimensions={0}, use_global_device_ids=true | all-gather | bytes 983040 | tf_op jit(solution)/shard_map/all_gather | solution.py:233
  57.8 2.4 %broadcast_in_dim.5 = bf16[4,4,4,2,96,128]{5,4,3,2,1,0:T(8,128)(2,1)} broadcast(bf16[4,4,2,96,128]{4,3,2,1,0:T(8,128)(2,1)S(1)} %bitcast.35), dimensions={1,2,3,4,5} | broadcast | bytes 3932160 | tf_op jit(solution)/shard_map/broadcast_in_dim | solution.py:30
  60.3 4.2 %all-to-all-start.1 = ((bf16[4,4,4,2,96,128]{5,4,3,2,1,0:T(8,128)(2,1)}), bf16[4,4,4,2,96,128]{5,4,3,2,1,0:T(8,128)(2,1)S(1)}, u32[]{:S(2)}, u32[]{:S(2)}) async-start(bf16[4,4,4,2,96,128]{5,4,3,2,1,0:T(8,128)(2,1)} %broadcast_in_dim.5), calls=%async_computation.1 | async-start | bytes 6291456 | tf_op jit(solution)/shard_map/all_to_all | solution.py:31
  64.4 33.0 %all-to-all-done.1 = bf16[4,4,4,2,96,128]{5,4,3,2,1,0:T(8,128)(2,1)S(1)} async-done(((bf16[4,4,4,2,96,128]{5,4,3,2,1,0:T(8,128)(2,1)}), bf16[4,4,4,2,96,128]{5,4,3,2,1,0:T(8,128)(2,1)S(1)}, u32[]{:S(2)}, u32[]{:S(2)}) %all-to-all-start.1) | async-done | bytes 3145760 | tf_op jit(solution)/shard_map/all_to_all | solution.py:31
  97.4 0.0 copy-start.1
  97.4 1.6 copy-done.1
  99.0 6.6 %shard_map.68 = (bf16[8,4,2,96,128]{4,3,2,1,0:T(8,128)(2,1)}, bf16[8,4,2,96,128]{4,3,2,1,0:T(8,128)(2,1)}, bf16[8,2,4,2,96,128]{5,4,3,2,1,0:T(8,128)(2,1)}) custom-call(s32[2,8]{1,0:T(2,128)} %owner.1, bf16[4,4,2,2,2,96,128]{6,5,4,3,2,1,0:T(8,128)(2,1)} %bitcast.33), custom_call_target="tpu_custom_call" | custom-call | bytes 9437184 | tf_op jit(solution)/shard_map/pallas_call | solution.py:55
  105.6 0.0 copy-start.3
  105.6 10.1 %all-to-all-start.2 = ((bf16[8,2,768,128]{3,2,1,0:T(8,128)(2,1)}), bf16[8,2,768,128]{3,2,1,0:T(8,128)(2,1)}, u32[]{:S(2)}, u32[]{:S(2)}) async-start(bf16[8,2,768,128]{3,2,1,0:T(8,128)(2,1)} %bitcast.34), calls=%async_computation.2 | async-start | bytes 6291456 | tf_op jit(solution)/shard_map/all_to_all | solution.py:239
  115.7 0.0 all-gather.9.cloned.1.call-start
  115.7 0.0 all-gather.7.cloned.1.call-done
  115.7 0.0 copy-done.3
  115.7 0.0 copy-start.2
  115.7 3.5 %multiply_convert_fusion = (bf16[128,384]{1,0:T(8,128)(2,1)S(1)}, f32[128,384]{1,0:T(8,128)S(1)}) fusion(bf16[6144,128]{1,0:T(8,128)(2,1)S(1)} %bitcast.38, bf16[6144,384]{1,0:T(8,128)(2,1)} %all-gather.7.cloned.1.call-done), kind=kOutput, calls=%fused_computation.11 | convolution fusion | flops 604422144 | bytes 6586368 | tf_op jit(solution)/shard_map/dot_general | solution.py:243
  119.2 0.0 all-gather.5.cloned.1.call-done
  119.3 0.0 copy-done.2
  119.3 0.0 copy-start
  119.3 4.0 %fusion.1.first = bf16[128,384]{1,0:T(8,128)(2,1)S(1)} fusion(bf16[6144,128]{1,0:T(8,128)(2,1)S(1)} %bitcast.37, bf16[384,6144]{1,0:T(8,128)(2,1)} %all-gather.5.cloned.1.call-done, f32[128,384]{1,0:T(8,128)S(1)} %get-tuple-element.25), kind=kOutput, calls=%fused_computation.3 | convolution fusion | flops 604913664 | bytes 6586368 | tf_op jit(solution)/shard_map/dot_general | solution.py:246
  123.3 0.0 copy-done
  123.3 1.6 fusion
  124.9 0.9 copy.8
  125.8 0.5 shard_map.69
  126.4 0.0 copy-start.4
  126.4 0.7 shard_map.72
  127.1 0.0 all-gather.9.cloned.1.call-update
  127.1 2.2 %collective-permute-start = (bf16[4,2,2,96,128]{4,3,2,1,0:T(8,128)(2,1)S(1)}, bf16[4,2,2,96,128]{4,3,2,1,0:T(8,128)(2,1)S(1)}, u32[]{:S(2)}, u32[]{:S(2)}) collective-permute-start(bf16[4,2,2,96,128]{4,3,2,1,0:T(8,128)(2,1)S(1)} %get-tuple-element.16), channel_id=1, source_target_pairs={{0,2},{2,4},{4,6},{6,0},{1,3},{3,5},{5,7},{7,1},{8,10},{10,12},{12... | collective-permute-start | bytes 1179656 | tf_op jit(solution)/shard_map/ppermute | solution.py:209
  129.3 3.7 %collective-permute-start.1 = (bf16[4,2,2,96,128]{4,3,2,1,0:T(8,128)(2,1)S(1)}, bf16[4,2,2,96,128]{4,3,2,1,0:T(8,128)(2,1)S(1)}, u32[]{:S(2)}, u32[]{:S(2)}) collective-permute-start(bf16[4,2,2,96,128]{4,3,2,1,0:T(8,128)(2,1)S(1)} %get-tuple-element.17), channel_id=1, source_target_pairs={{0,4},{2,6},{4,0},{6,2},{1,5},{3,7},{5,1},{7,3},{8,12},{10,14},{12... | collective-permute-start | bytes 1179656 | tf_op jit(solution)/shard_map/ppermute | solution.py:209
  133.0 2.5 %collective-permute-start.2 = (bf16[4,2,2,96,128]{4,3,2,1,0:T(8,128)(2,1)S(1)}, bf16[4,2,2,96,128]{4,3,2,1,0:T(8,128)(2,1)S(1)}, u32[]{:S(2)}, u32[]{:S(2)}) collective-permute-start(bf16[4,2,2,96,128]{4,3,2,1,0:T(8,128)(2,1)S(1)} %get-tuple-element.18), channel_id=1, source_target_pairs={{0,6},{2,0},{4,2},{6,4},{1,7},{3,1},{5,3},{7,5},{8,14},{10,8},{12,... | collective-permute-start | bytes 1179656 | tf_op jit(solution)/shard_map/ppermute | solution.py:209
  135.5 5.9 %collective-permute-done.refs_2_ = bf16[4,2,2,96,128]{4,3,2,1,0:T(8,128)(2,1)S(1)} collective-permute-done((bf16[4,2,2,96,128]{4,3,2,1,0:T(8,128)(2,1)S(1)}, bf16[4,2,2,96,128]{4,3,2,1,0:T(8,128)(2,1)S(1)}, u32[]{:S(2)}, u32[]{:S(2)}) %collective-permute-start) | collective-permute-done | bytes 393248 | tf_op jit(solution)/shard_map/ppermute | solution.py:209
  141.4 7.2 %collective-permute-done.1.refs_3_ = bf16[4,2,2,96,128]{4,3,2,1,0:T(8,128)(2,1)S(1)} collective-permute-done((bf16[4,2,2,96,128]{4,3,2,1,0:T(8,128)(2,1)S(1)}, bf16[4,2,2,96,128]{4,3,2,1,0:T(8,128)(2,1)S(1)}, u32[]{:S(2)}, u32[]{:S(2)}) %collective-permute-start.1) | collective-permute-done | bytes 393248 | tf_op jit(solution)/shard_map/ppermute | solution.py:209
  148.6 2.9 %collective-permute-done.2.refs_4_ = bf16[4,2,2,96,128]{4,3,2,1,0:T(8,128)(2,1)S(1)} collective-permute-done((bf16[4,2,2,96,128]{4,3,2,1,0:T(8,128)(2,1)S(1)}, bf16[4,2,2,96,128]{4,3,2,1,0:T(8,128)(2,1)S(1)}, u32[]{:S(2)}, u32[]{:S(2)}) %collective-permute-start.2) | collective-permute-done | bytes 393248 | tf_op jit(solution)/shard_map/ppermute | solution.py:209
  151.5 0.2 shard_map.70
  151.7 2.5 %collective-permute-start.3 = (bf16[2,2,96,128]{3,2,1,0:T(8,128)(2,1)S(1)}, bf16[2,2,96,128]{3,2,1,0:T(8,128)(2,1)S(1)}, u32[]{:S(2)}, u32[]{:S(2)}) collective-permute-start(bf16[2,2,96,128]{3,2,1,0:T(8,128)(2,1)S(1)} %get-tuple-element.20), channel_id=1, source_target_pairs={{0,8},{8,16},{16,24},{24,0},{1,9},{9,17},{17,25},{25,1},{2,10},{10... | collective-permute-start | bytes 294920 | tf_op jit(solution)/shard_map/ppermute | solution.py:209
  154.2 4.4 %collective-permute-start.4 = (bf16[2,2,96,128]{3,2,1,0:T(8,128)(2,1)S(1)}, bf16[2,2,96,128]{3,2,1,0:T(8,128)(2,1)S(1)}, u32[]{:S(2)}, u32[]{:S(2)}) collective-permute-start(bf16[2,2,96,128]{3,2,1,0:T(8,128)(2,1)S(1)} %get-tuple-element.21), channel_id=1, source_target_pairs={{0,16},{8,24},{16,0},{24,8},{1,17},{9,25},{17,1},{25,9},{2,18},{10... | collective-permute-start | bytes 294920 | tf_op jit(solution)/shard_map/ppermute | solution.py:209
  158.6 2.2 %collective-permute-start.5 = (bf16[2,2,96,128]{3,2,1,0:T(8,128)(2,1)S(1)}, bf16[2,2,96,128]{3,2,1,0:T(8,128)(2,1)S(1)}, u32[]{:S(2)}, u32[]{:S(2)}) collective-permute-start(bf16[2,2,96,128]{3,2,1,0:T(8,128)(2,1)S(1)} %get-tuple-element.22), channel_id=1, source_target_pairs={{0,24},{8,0},{16,8},{24,16},{1,25},{9,1},{17,9},{25,17},{2,26},{10... | collective-permute-start | bytes 294920 | tf_op jit(solution)/shard_map/ppermute | solution.py:209
  160.7 0.0 all-to-all-done.2.refs_4_.pieces
  160.7 0.0 collective-permute-done.3.refs_1_
  160.8 4.2 %collective-permute-done.4.refs_2_ = bf16[2,2,96,128]{3,2,1,0:T(8,128)(2,1)S(1)} collective-permute-done((bf16[2,2,96,128]{3,2,1,0:T(8,128)(2,1)S(1)}, bf16[2,2,96,128]{3,2,1,0:T(8,128)(2,1)S(1)}, u32[]{:S(2)}, u32[]{:S(2)}) %collective-permute-start.4) | collective-permute-done | bytes 98336 | tf_op jit(solution)/shard_map/ppermute | solution.py:209
  165.0 1.6 collective-permute-done.5.refs_3_
  166.6 0.1 shard_map.71
  166.6 15.0 %all_to_all.21 = bf16[4,96,128]{2,1,0:T(8,128)(2,1)S(1)} all-to-all(bf16[4,96,128]{2,1,0:T(8,128)(2,1)S(1)} %bitcast.32), channel_id=1, replica_groups=mesh['x'=4,'core'=2,'sh'=2,'sl'=4,'y'=4,'zh'=2] {'sh','zh'}, dimensions={0} | all-to-all | bytes 196608 | tf_op jit(solution)/shard_map/all_to_all | solution.py:261
  181.6 0.0 copy-done.4
  181.6 0.6 fusion.7
  182.2 0.0 all-gather.9.cloned.1.call-done
  182.3 4.6 %shard_map.73 = f32[2,1,768,384]{3,2,1,0:T(8,128)} custom-call(bf16[8,2,768,128]{3,2,1,0:T(8,128)(2,1)} %all-to-all-done.2.refs_4_.pieces, bf16[8,128,768]{2,1,0:T(8,128)(2,1)} %bitcast.36), custom_call_target="tpu_custom_call" | custom-call | flops 1207959552 | bytes 7864320 | tf_op jit(solution)/shard_map/pallas_call | solution.py:187
  (2 shorter events, 0.0 us)
Async XLA Ops:
  7.2 108.5 %all-gather.7.cloned.1.call-start = ((), (), s32[]{:S(2)}) async-start(), calls=%async_computation.5 | async-start | bytes 5308416 | tf_op jit(solution)/shard_map/all_gather | solution.py:228
  7.9 111.4 %all-gather.5.cloned.1.call-start = ((), (), s32[]{:S(2)}) async-start(), calls=%async_computation.4 | async-start | bytes 5308416 | tf_op jit(solution)/shard_map/all_gather | solution.py:229
  60.3 37.1 %all-to-all-start.1 = ((bf16[4,4,4,2,96,128]{5,4,3,2,1,0:T(8,128)(2,1)}), bf16[4,4,4,2,96,128]{5,4,3,2,1,0:T(8,128)(2,1)S(1)}, u32[]{:S(2)}, u32[]{:S(2)}) async-start(bf16[4,4,4,2,96,128]{5,4,3,2,1,0:T(8,128)(2,1)} %broadcast_in_dim.5), calls=%async_computation.1 | async-start | bytes 6291456 | tf_op jit(solution)/shard_map/all_to_all | solution.py:31
  97.4 1.6 copy-start.1
  105.6 10.1 %copy-start.3 = (bf16[8,4,2,96,128]{4,3,2,1,0:T(8,128)(2,1)S(1)}, bf16[8,4,2,96,128]{4,3,2,1,0:T(8,128)(2,1)}, u32[]{:S(2)}) copy-start(bf16[8,4,2,96,128]{4,3,2,1,0:T(8,128)(2,1)} %get-tuple-element.14) | copy-start | bytes 4718596
  105.6 55.1 %all-to-all-start.2 = ((bf16[8,2,768,128]{3,2,1,0:T(8,128)(2,1)}), bf16[8,2,768,128]{3,2,1,0:T(8,128)(2,1)}, u32[]{:S(2)}, u32[]{:S(2)}) async-start(bf16[8,2,768,128]{3,2,1,0:T(8,128)(2,1)} %bitcast.34), calls=%async_computation.2 | async-start | bytes 6291456 | tf_op jit(solution)/shard_map/all_to_all | solution.py:239
  115.7 66.6 %all-gather.9.cloned.1.call-start = ((), (), s32[]{:S(2)}) async-start(), calls=%async_computation.6 | async-start | bytes 1769472 | tf_op jit(solution)/shard_map/all_gather | solution.py:257
  115.7 3.6 %copy-start.2 = (bf16[8,4,2,96,128]{4,3,2,1,0:T(8,128)(2,1)S(1)}, bf16[8,4,2,96,128]{4,3,2,1,0:T(8,128)(2,1)}, u32[]{:S(2)}) copy-start(bf16[8,4,2,96,128]{4,3,2,1,0:T(8,128)(2,1)} %get-tuple-element.13) | copy-start | bytes 4718596
  119.3 4.0 %copy-start = (bf16[6144,384]{1,0:T(8,128)(2,1)S(1)}, bf16[6144,384]{1,0:T(8,128)(2,1)}, u32[]{:S(2)}) copy-start(bf16[6144,384]{1,0:T(8,128)(2,1)} %all-gather.7.cloned.1.call-done) | copy-start | bytes 14155780
  126.4 55.3 %copy-start.4 = (bf16[128,96]{0,1:T(8,128)(2,1)S(1)}, bf16[128,96]{0,1:T(8,128)(2,1)}, u32[]{:S(2)}) copy-start(bf16[128,96]{0,1:T(8,128)(2,1)} %param.5) | copy-start | bytes 73732
  127.1 14.3 %collective-permute-start = (bf16[4,2,2,96,128]{4,3,2,1,0:T(8,128)(2,1)S(1)}, bf16[4,2,2,96,128]{4,3,2,1,0:T(8,128)(2,1)S(1)}, u32[]{:S(2)}, u32[]{:S(2)}) collective-permute-start(bf16[4,2,2,96,128]{4,3,2,1,0:T(8,128)(2,1)S(1)} %get-tuple-element.16), channel_id=1, source_target_pairs={{0,2},{2,4},{4,6},{6,0},{1,3},{3,5},{5,7},{7,1},{8,10},{10,12},{12... | collective-permute-start | bytes 1179656 | tf_op jit(solution)/shard_map/ppermute | solution.py:209
  129.3 19.3 %collective-permute-start.1 = (bf16[4,2,2,96,128]{4,3,2,1,0:T(8,128)(2,1)S(1)}, bf16[4,2,2,96,128]{4,3,2,1,0:T(8,128)(2,1)S(1)}, u32[]{:S(2)}, u32[]{:S(2)}) collective-permute-start(bf16[4,2,2,96,128]{4,3,2,1,0:T(8,128)(2,1)S(1)} %get-tuple-element.17), channel_id=1, source_target_pairs={{0,4},{2,6},{4,0},{6,2},{1,5},{3,7},{5,1},{7,3},{8,12},{10,14},{12... | collective-permute-start | bytes 1179656 | tf_op jit(solution)/shard_map/ppermute | solution.py:209
  133.0 18.5 %collective-permute-start.2 = (bf16[4,2,2,96,128]{4,3,2,1,0:T(8,128)(2,1)S(1)}, bf16[4,2,2,96,128]{4,3,2,1,0:T(8,128)(2,1)S(1)}, u32[]{:S(2)}, u32[]{:S(2)}) collective-permute-start(bf16[4,2,2,96,128]{4,3,2,1,0:T(8,128)(2,1)S(1)} %get-tuple-element.18), channel_id=1, source_target_pairs={{0,6},{2,0},{4,2},{6,4},{1,7},{3,1},{5,3},{7,5},{8,14},{10,8},{12,... | collective-permute-start | bytes 1179656 | tf_op jit(solution)/shard_map/ppermute | solution.py:209
  151.7 9.1 %collective-permute-start.3 = (bf16[2,2,96,128]{3,2,1,0:T(8,128)(2,1)S(1)}, bf16[2,2,96,128]{3,2,1,0:T(8,128)(2,1)S(1)}, u32[]{:S(2)}, u32[]{:S(2)}) collective-permute-start(bf16[2,2,96,128]{3,2,1,0:T(8,128)(2,1)S(1)} %get-tuple-element.20), channel_id=1, source_target_pairs={{0,8},{8,16},{16,24},{24,0},{1,9},{9,17},{17,25},{25,1},{2,10},{10... | collective-permute-start | bytes 294920 | tf_op jit(solution)/shard_map/ppermute | solution.py:209
  154.2 10.8 %collective-permute-start.4 = (bf16[2,2,96,128]{3,2,1,0:T(8,128)(2,1)S(1)}, bf16[2,2,96,128]{3,2,1,0:T(8,128)(2,1)S(1)}, u32[]{:S(2)}, u32[]{:S(2)}) collective-permute-start(bf16[2,2,96,128]{3,2,1,0:T(8,128)(2,1)S(1)} %get-tuple-element.21), channel_id=1, source_target_pairs={{0,16},{8,24},{16,0},{24,8},{1,17},{9,25},{17,1},{25,9},{2,18},{10... | collective-permute-start | bytes 294920 | tf_op jit(solution)/shard_map/ppermute | solution.py:209
  158.6 8.0 %collective-permute-start.5 = (bf16[2,2,96,128]{3,2,1,0:T(8,128)(2,1)S(1)}, bf16[2,2,96,128]{3,2,1,0:T(8,128)(2,1)S(1)}, u32[]{:S(2)}, u32[]{:S(2)}) collective-permute-start(bf16[2,2,96,128]{3,2,1,0:T(8,128)(2,1)S(1)} %get-tuple-element.22), channel_id=1, source_target_pairs={{0,24},{8,0},{16,8},{24,16},{1,25},{9,1},{17,9},{25,17},{2,26},{10... | collective-permute-start | bytes 294920 | tf_op jit(solution)/shard_map/ppermute | solution.py:209
Sparse Core Ops, SparseCore 0:
  10.1 47.6 all-gather.6
  60.0 42.0 all-gather.4
  127.2 28.3 all-gather.8
